TPU v7x, 512 devices: a whole 4x4x16 slice. The times are simulated.
512 devices in a mesh: dp: 16 (over y_lo, x, core), mp: 32 (over y_hi, z).
Axes of the slice: x: 4, y: 4 (y_hi: 2, y_lo: 2; y = y_hi * 2 + y_lo), z: 16, core: 2. Of those that a mesh axis runs over, the one named last changes fastest.
Arguments:
- hidden: bfloat16 [8192, 16384], P('dp', 'mp'), may hold values from -6 to 6
- out_grad: bfloat16 [8192, 4096], P('dp', 'mp'), may hold values from -0.125 to 0.125
- token_counts: int32 [16], P('dp'), may hold values from 1 to 512, 5120 in all
- factor_state: float32 [8192, 16384], P('dp', 'mp'), as said below
- stale_root: bfloat16 [8192, 16384], P('dp', 'mp'), as said below
- newton_steps: int32 [16, 32], P('dp', 'mp'), may hold values from 0 to 3, as said below
Outputs:
- update: bfloat16 [4096, 16384], P('dp', 'mp')
- new_factor: float32 [8192, 16384], P('dp', 'mp')
- new_root: bfloat16 [8192, 16384], P('dp', 'mp')
Inputs may be any that keep to these rules, and one draw needn't show every extreme that they name: `token_counts`: the shards' counts sum to 5120; some shard is full. `factor_state`: every 512 x 512 block is symmetric with a strictly dominant positive diagonal. `stale_root`: every 512 x 512 block is symmetric with a strictly dominant positive diagonal. `newton_steps`: 0 keeps the stale root; a factor that is refreshed takes 2 or 3 iterations; some factor takes 3.
All inputs are finite; a program needn't handle non-finite values.
Results may differ from a plain program's by a relative error of at most 0.03.
Values may be sent and summed in bfloat16 or wider, within the bound.
No kernel may reach another device: no remote copies, remote signals or barrier semaphores. Data moves between devices by JAX's collectives and lax.ppermute only.
A program may use at most 64 MiB of HBM per device.

v0:
```python
import jax
import jax.numpy as jnp
from jax import lax
from jax.sharding import PartitionSpec as P

NEWTON = 3


BETA = 0.9
NORM_EPS = 1e-06


def from_partner(value, axis, stride):
    mask = 2**stride
    pairs = [(source, source ^ mask) for source in range(lax.axis_size(axis))]
    return lax.ppermute(value, axis, pairs)


def passed_along(array, axis, by):
    devices = lax.axis_size(axis)
    pairs = [(i, i + by) for i in range(devices) if 0 <= i + by < devices]
    return lax.ppermute(array, axis, pairs)


def newton_turn(matrix):
    identity = jnp.eye(matrix.shape[0], dtype=jnp.float32)
    return ((5.0 * identity - matrix.astype(jnp.float32)) * 0.25).astype(jnp.bfloat16)


def coupled_root(start, root_scale, steps):
    turned = newton_turn(start)
    current = (root_scale * turned.astype(jnp.float32)).astype(jnp.bfloat16)
    state = (current, start, turned)
    for level in range(1, NEWTON):

        def advance(carried):
            current, matrix, turned = carried
            square = jnp.dot(turned, turned, preferred_element_type=jnp.float32).astype(
                jnp.bfloat16
            )
            fourth = jnp.dot(square, square, preferred_element_type=jnp.float32).astype(
                jnp.bfloat16
            )
            matrix = jnp.dot(fourth, matrix, preferred_element_type=jnp.float32).astype(
                jnp.bfloat16
            )
            turned = newton_turn(matrix)
            current = jnp.dot(current, turned, preferred_element_type=jnp.float32).astype(
                jnp.bfloat16
            )
            return (current, matrix, turned)

        def keep(carried):
            return carried

        state = lax.cond(level < steps, advance, keep, state)
    return state[0]


def finish_root(scaled, root_scale, steps, stale):
    iterate = coupled_root(scaled, root_scale.astype(jnp.float32), steps)
    return jnp.where(steps > 0, iterate, stale)


def per_device(hidden, out_grad, token_counts, factor_state, stale_root, newton_steps):
    token_rows = hidden.shape[0]
    positions = lax.broadcasted_iota(jnp.int32, (token_rows, 1), 0)
    kept = jnp.where(positions < token_counts[0], hidden, jnp.zeros_like(hidden))
    full_grad = lax.all_gather(out_grad, "mp", axis=1, tiled=True)
    own_rows = lax.psum_scatter(
        lax.dot_general(
            full_grad, kept, (((0,), (0,)), ((), ())), preferred_element_type=jnp.float32
        ).astype(jnp.bfloat16),
        "dp",
        scatter_dimension=0,
        tiled=True,
    )
    other_rows = from_partner(own_rows, "dp", 0)
    pair_side = lax.axis_index("dp") % 2
    is_left = pair_side == 0
    upper = jnp.where(is_left, own_rows, other_rows)
    lower = jnp.where(is_left, other_rows, own_rows)
    grad_block = jnp.concatenate([upper, lower], axis=0)
    operand = jnp.where(is_left, grad_block, grad_block.T)
    statistic = lax.dot_general(
        operand, operand, (((1,), (1,)), ((), ())), preferred_element_type=jnp.float32
    )
    new_factor = BETA * factor_state + (1.0 - BETA) * statistic
    norm_value = jnp.sqrt(jnp.sum(new_factor * new_factor) + NORM_EPS)
    scaled = (new_factor / norm_value).astype(jnp.bfloat16)
    root_scale = (norm_value ** (-0.25)).astype(jnp.bfloat16).reshape(1)
    steps = newton_steps[0, 0]
    steps_sent = steps.astype(jnp.bfloat16).reshape(1)
    got_matrix, got_stale, got_scale, got_steps = passed_along(
        (scaled, stale_root, root_scale, steps_sent), "dp", -1
    )

    def compute_both(unused):
        left_fresh = finish_root(scaled, root_scale[0], steps, stale_root)
        right_fresh = finish_root(
            got_matrix, got_scale[0], got_steps[0].astype(jnp.int32), got_stale
        )
        return (left_fresh, right_fresh)

    def skip_both(unused):
        return (jnp.zeros_like(stale_root), jnp.zeros_like(stale_root))

    left_fresh, right_fresh = lax.cond(is_left, compute_both, skip_both, 0)
    back_left, back_right = passed_along((left_fresh, right_fresh), "dp", 1)
    left_root = jnp.where(is_left, left_fresh, back_left)
    right_root = jnp.where(is_left, right_fresh, back_right)
    new_root = jnp.where(is_left, left_root, right_root)
    product = jnp.dot(grad_block, right_root, preferred_element_type=jnp.float32).astype(
        jnp.bfloat16
    )
    half_rows = own_rows.shape[0]
    left_rows = lax.dynamic_slice_in_dim(left_root, pair_side * half_rows, half_rows, 0)
    raw_update = jnp.dot(left_rows, product, preferred_element_type=jnp.float32)
    update_square = jnp.sum(raw_update * raw_update).reshape(1)
    partner_square = from_partner(update_square, "dp", 0)
    grad_square = jnp.sum(jnp.square(grad_block.astype(jnp.float32)))
    ratio = jnp.sqrt(grad_square) / jnp.sqrt(update_square[0] + partner_square[0] + NORM_EPS)
    update = (raw_update * ratio).astype(jnp.bfloat16)
    return (update, new_factor, new_root)


def solution(mesh):
    in_specs = (P("dp", "mp"), P("dp", "mp"), P("dp"), P("dp", "mp"), P("dp", "mp"), P("dp", "mp"))
    out_specs = (P("dp", "mp"), P("dp", "mp"), P("dp", "mp"))
    return jax.shard_map(
        per_device, mesh=mesh, in_specs=in_specs, out_specs=out_specs, check_vma=False
    )
```

profile of v0, /device:TPU:89, one launch (start us, length us, event | category | flops | bytes accessed | tf_op | source)
XLA Modules:
  0.0 345.5 jit_solution(5313643022404360714)
XLA Ops:
  7.2 0.0 all-gather.2.cloned.1.call-start
  7.2 0.7 all-gather.2.cloned.1.call-update
  7.9 0.0 reduce-scatter.2.cloned.1.call-start
  8.6 161.5 %all-gather.2.cloned.1.call-done = bf16[512,4096]{1,0:T(8,128)(2,1)} async-done(((bf16[512,128]{1,0:T(8,128)(2,1)}), bf16[512,4096]{1,0:T(8,128)(2,1)}) %all-gather.2.cloned.1.call-update) | async-done | bytes 4194320 | tf_op jit(solution)/shard_map/all_gather | solution.py:69
  170.1 6.8 %fusion.30 = bf16[4096,512]{0,1:T(8,128)(2,1)} fusion(bf16[512,4096]{1,0:T(8,128)(2,1)} %all-gather.2.cloned.1.call-done, bf16[512,512]{1,0:T(8,128)(2,1)} %param.16, pred[512]{0:T(512)(128)(4,1)S(1)} %iota_compare_fusion.7), kind=kOutput, calls=%fused_computation.60 | convolution fusion | flops 2149842944 | bytes 8913408 | tf_op jit(solution)/shard_map/dot_general | solution.py:71
  176.8 0.0 copy-start
  176.8 0.0 reduce-scatter.2.cloned.1.call-update
  176.8 75.2 %reduce-scatter.2.cloned.1.call-done = bf16[256,512]{0,1:T(8,128)(2,1)} async-done(((bf16[4096,512]{0,1:T(8,128)(2,1)}), bf16[256,512]{0,1:T(8,128)(2,1)}) %reduce-scatter.2.cloned.1.call-update) | async-done | bytes 262160 | tf_op jit(solution)/shard_map/reduce_scatter | solution.py:70
  252.1 5.6 %collective-permute-start = (bf16[256,512]{0,1:T(8,128)(2,1)}, bf16[256,512]{0,1:T(8,128)(2,1)S(1)}, u32[]{:S(2)}, u32[]{:S(2)}) collective-permute-start(bf16[256,512]{0,1:T(8,128)(2,1)} %reduce-scatter.2.cloned.1.call-done), channel_id=1, source_target_pairs={{0,32},{32,0},{64,96},{96,64},{128,160},{160,128},{192,224},{224,1... | collective-permute-start | bytes 786440 | tf_op jit(solution)/shard_map/ppermute | solution.py:16
  257.7 0.0 copy-done
  257.7 1.0 copy.14
  258.8 1.9 collective-permute-start.4
  260.7 0.0 collective-permute-done
  260.7 1.0 broadcast_select_fusion.6
  261.7 1.0 copy.13
  262.7 2.8 multiply_reduce_fusion.1
  265.5 0.0 copy-start.2
  266.2 0.1 divide_convert_fusion
  266.4 3.0 collective-permute-start.3
  270.0 3.4 collective-permute-start.1
  273.4 5.9 %collective-permute-start.2 = (bf16[1]{0:T(256)(128)(2,1)}, bf16[1]{0:T(256)(128)(2,1)}, u32[]{:S(2)}, u32[]{:S(2)}) collective-permute-start(bf16[1]{0:T(256)(128)(2,1)} %bitcast.11), channel_id=1, source_target_pairs={{32,0},{64,32},{96,64},{128,96},{160,128},{192,160},{224,192},{256... | collective-permute-start | bytes 14 | tf_op jit(solution)/shard_map/ppermute | solution.py:22
  279.3 0.0 collective-permute-done.1
  279.4 0.0 collective-permute-done.4
  279.4 0.7 collective-permute-done.2
  280.0 0.0 collective-permute-done.3
  280.0 0.0 copy-done.2
  280.0 1.7 conditional.5
  280.0 0.8 broadcast.40
  280.9 0.8 broadcast.40.clone
  281.7 22.5 %collective-permute-start.5 = (bf16[512,512]{0,1:T(8,128)(2,1)}, bf16[512,512]{0,1:T(8,128)(2,1)S(1)}, u32[]{:S(2)}, u32[]{:S(2)}) collective-permute-start(bf16[512,512]{0,1:T(8,128)(2,1)} %get-tuple-element.107), channel_id=1, source_target_pairs={{0,32},{32,64},{64,96},{96,128},{128,160},{160,192},{192,224},{224... | collective-permute-start | bytes 1572872 | tf_op jit(solution)/shard_map/ppermute | solution.py:22
  304.2 1.9 collective-permute-start.6
  306.2 0.9 multiply_reduce_fusion
  307.7 7.3 %collective-permute-done.5 = bf16[512,512]{0,1:T(8,128)(2,1)S(1)} collective-permute-done((bf16[512,512]{0,1:T(8,128)(2,1)}, bf16[512,512]{0,1:T(8,128)(2,1)S(1)}, u32[]{:S(2)}, u32[]{:S(2)}) %collective-permute-start.5) | collective-permute-done | bytes 524320 | tf_op jit(solution)/shard_map/ppermute | solution.py:22
  315.0 1.9 collective-permute-done.6
  317.0 0.1 broadcast_select_fusion.2
  317.1 1.3 multiply_reduce_fusion.2
  318.4 17.1 %collective-permute-start.7 = (f32[1]{0:T(128)}, f32[1]{0:T(128)}, u32[]{:S(2)}, u32[]{:S(2)}) collective-permute-start(f32[1]{0:T(128)} %bitcast.12), channel_id=1, source_target_pairs={{0,32},{32,0},{64,96},{96,64},{128,160},{160,128},{192,224},{224,1... | collective-permute-start | bytes 20 | tf_op jit(solution)/shard_map/ppermute | solution.py:16
  335.5 1.0 copy.16
  336.5 0.1 collective-permute-done.7
  337.9 0.7 multiply_convert_fusion.4
  (2 shorter events, 0.0 us)
Async XLA Ops:
  7.2 162.9 %all-gather.2.cloned.1.call-start = ((), (), s32[]{:S(2)}) async-start(), calls=%async_computation.1 | async-start | bytes 4325376 | tf_op jit(solution)/shard_map/all_gather | solution.py:69
  7.9 244.2 %reduce-scatter.2.cloned.1.call-start = ((), (), s32[]{:S(2)}) async-start(), calls=%async_computation.2 | async-start | bytes 4456448 | tf_op jit(solution)/shard_map/reduce_scatter | solution.py:70
  176.8 80.9 %copy-start = (bf16[512,512]{1,0:T(8,128)(2,1)S(1)}, bf16[512,512]{1,0:T(8,128)(2,1)}, u32[]{:S(2)}) copy-start(bf16[512,512]{1,0:T(8,128)(2,1)} %param.20) | copy-start | bytes 1572868
  252.1 8.6 %collective-permute-start = (bf16[256,512]{0,1:T(8,128)(2,1)}, bf16[256,512]{0,1:T(8,128)(2,1)S(1)}, u32[]{:S(2)}, u32[]{:S(2)}) collective-permute-start(bf16[256,512]{0,1:T(8,128)(2,1)} %reduce-scatter.2.cloned.1.call-done), channel_id=1, source_target_pairs={{0,32},{32,0},{64,96},{96,64},{128,160},{160,128},{192,224},{224,1... | collective-permute-start | bytes 786440 | tf_op jit(solution)/shard_map/ppermute | solution.py:16
  258.8 20.6 %collective-permute-start.4 = (bf16[512,512]{0,1:T(8,128)(2,1)}, bf16[512,512]{0,1:T(8,128)(2,1)S(1)}, u32[]{:S(2)}, u32[]{:S(2)}) collective-permute-start(bf16[512,512]{0,1:T(8,128)(2,1)} %copy.14), channel_id=1, source_target_pairs={{32,0},{64,32},{96,64},{128,96},{160,128},{192,160},{224,192},{256... | collective-permute-start | bytes 1572872 | tf_op jit(solution)/shard_map/ppermute | solution.py:22
  265.5 14.5 %copy-start.2 = (f32[512,512]{1,0:T(8,128)}, f32[512,512]{1,0:T(8,128)S(1)}, u32[]{:S(2)}) copy-start(f32[512,512]{1,0:T(8,128)S(1)} %get-tuple-element.171) | copy-start | bytes 3145732
  266.4 13.7 %collective-permute-start.3 = (bf16[512,512]{1,0:T(8,128)(2,1)S(1)}, bf16[512,512]{1,0:T(8,128)(2,1)}, u32[]{:S(2)}, u32[]{:S(2)}) collective-permute-start(bf16[512,512]{1,0:T(8,128)(2,1)S(1)} %divide_convert_fusion), channel_id=1, source_target_pairs={{32,0},{64,32},{96,64},{128,96},{160,128},{192,160},{224,192},{256... | collective-permute-start | bytes 1572872 | tf_op jit(solution)/shard_map/ppermute | solution.py:22
  270.0 9.3 %collective-permute-start.1 = (bf16[1]{0:T(256)(128)(2,1)}, bf16[1]{0:T(256)(128)(2,1)}, u32[]{:S(2)}, u32[]{:S(2)}) collective-permute-start(bf16[1]{0:T(256)(128)(2,1)} %bitcast.10), channel_id=1, source_target_pairs={{32,0},{64,32},{96,64},{128,96},{160,128},{192,160},{224,192},{256... | collective-permute-start | bytes 14 | tf_op jit(solution)/shard_map/ppermute | solution.py:22
  273.4 6.6 %collective-permute-start.2 = (bf16[1]{0:T(256)(128)(2,1)}, bf16[1]{0:T(256)(128)(2,1)}, u32[]{:S(2)}, u32[]{:S(2)}) collective-permute-start(bf16[1]{0:T(256)(128)(2,1)} %bitcast.11), channel_id=1, source_target_pairs={{32,0},{64,32},{96,64},{128,96},{160,128},{192,160},{224,192},{256... | collective-permute-start | bytes 14 | tf_op jit(solution)/shard_map/ppermute | solution.py:22
  281.7 33.3 %collective-permute-start.5 = (bf16[512,512]{0,1:T(8,128)(2,1)}, bf16[512,512]{0,1:T(8,128)(2,1)S(1)}, u32[]{:S(2)}, u32[]{:S(2)}) collective-permute-start(bf16[512,512]{0,1:T(8,128)(2,1)} %get-tuple-element.107), channel_id=1, source_target_pairs={{0,32},{32,64},{64,96},{96,128},{128,160},{160,192},{192,224},{224... | collective-permute-start | bytes 1572872 | tf_op jit(solution)/shard_map/ppermute | solution.py:22
  304.2 12.7 %collective-permute-start.6 = (bf16[512,512]{0,1:T(8,128)(2,1)}, bf16[512,512]{0,1:T(8,128)(2,1)S(1)}, u32[]{:S(2)}, u32[]{:S(2)}) collective-permute-start(bf16[512,512]{0,1:T(8,128)(2,1)} %get-tuple-element.108), channel_id=1, source_target_pairs={{0,32},{32,64},{64,96},{96,128},{128,160},{160,192},{192,224},{224... | collective-permute-start | bytes 1572872 | tf_op jit(solution)/shard_map/ppermute | solution.py:22
  318.4 18.2 %collective-permute-start.7 = (f32[1]{0:T(128)}, f32[1]{0:T(128)}, u32[]{:S(2)}, u32[]{:S(2)}) collective-permute-start(f32[1]{0:T(128)} %bitcast.12), channel_id=1, source_target_pairs={{0,32},{32,0},{64,96},{96,64},{128,160},{160,128},{192,224},{224,1... | collective-permute-start | bytes 20 | tf_op jit(solution)/shard_map/ppermute | solution.py:16
Sparse Core Ops, SparseCore 0:
  10.9 159.1 all-gather.1
  177.0 75.0 reduce-scatter.1
where the time goes:
time: 346 us; the launch traced here: 345 us
  waiting for transfers between devices  247 us (71%)
  starting transfers between devices  61.5 us (18%)
  between operations  18.2 us (5%)
  matrix products  10.9 us (3%)
  local copies, waits for them, and re-layouts  4.69 us (1%)
    all_gather x1, waiting for transfers between devices, per_device(): full_grad = lax.all_gather(out_grad, 'mp', axis=1, tiled=True)  161 us
    reduce_scatter x1, waiting for transfers between devices, per_device(): lax.psum_scatter(lax.dot_general(full_grad, kept, (((0,), (0,)), ((), ())...  75.2 us
    ppermute x6, starting transfers between devices, passed_along(): return lax.ppermute(array, axis, pairs)  38.6 us
    ppermute x2, starting transfers between devices, from_partner(): return lax.ppermute(value, axis, pairs)  22.7 us
    ppermute x6, waiting for transfers between devices, passed_along(): return lax.ppermute(array, axis, pairs)  9.89 us
  transfers between devices with their start and end apart: 10, of which 6 were waited for; matrix products, arithmetic and copies ran while one was open for 2% of the time, Pallas kernels for 0%

commit v1 on v0

v1 whole, which is shorter than its diff:
```python
import functools

import jax
import jax.numpy as jnp
from jax import lax
from jax.experimental import pallas as pl
from jax.experimental.pallas import tpu as pltpu
from jax.sharding import Mesh
from jax.sharding import PartitionSpec as P

BETA = 0.9
NORM_EPS = 1e-06
BLOCK = 512
HALF = BLOCK // 2
CLASSES = 4
VMEM = pl.BlockSpec(memory_space=pltpu.VMEM)
SMEM = pl.BlockSpec(memory_space=pltpu.SMEM)
LIMIT = pltpu.CompilerParams(vmem_limit_bytes=48 * 2**20)
AXES = ("y_lo", "x", "core", "y_hi", "z")
BF16 = jnp.bfloat16
F32 = jnp.float32


def dot(a, b, contract=((1,), (0,))):
    return lax.dot_general(a, b, (contract, ((), ())), preferred_element_type=F32)


def partial_kernel(classes, *refs):
    features, hidden, out = refs[:classes], refs[classes:-1], refs[-1]
    rows = features[0].shape[0] // CLASSES
    tokens = hidden[0].shape[0]
    for column in range(2):
        for at in range(classes):
            total = dot(features[at][:, :tokens], hidden[2 * column][...])
            total += dot(features[at][:, tokens:], hidden[2 * column + 1][...])
            total = total.astype(BF16)
            for block in range(CLASSES):
                out[column * CLASSES + block, at * rows : (at + 1) * rows, :] = total[
                    block * rows : (block + 1) * rows
                ]


def partials(features, hidden):
    classes = len(features)
    rows = features[0].shape[0] // CLASSES
    width = hidden[0].shape[1]
    return pl.pallas_call(
        functools.partial(partial_kernel, classes),
        out_shape=jax.ShapeDtypeStruct((2 * CLASSES, classes * rows, width), BF16),
        in_specs=[VMEM] * (classes + 4),
        out_specs=VMEM,
        compiler_params=LIMIT,
    )(*features, *hidden)


def newton_kernel(info, own, other, state, stale, new_factor, new_root, payload, grad_square, grad, matrix, turned, square):
    side, first, steps = info[0], info[1], info[2]
    rows = HALF // CLASSES
    for at, shift in enumerate((0, 1, 3, 2)):
        start = lax.rem(first + shift, CLASSES) * (2 * rows)
        mine = pl.multiple_of(start + side * rows, rows)
        theirs = pl.multiple_of(start + (1 - side) * rows, rows)
        grad[pl.ds(mine, rows), :] = own[at * rows : (at + 1) * rows, :]
        grad[pl.ds(theirs, rows), :] = other[at * rows : (at + 1) * rows, :]

    @pl.when(side == 0)
    def _():
        new_factor[...] = BETA * state[...] + (1.0 - BETA) * dot(grad[...], grad[...], ((1,), (1,)))

    @pl.when(side != 0)
    def _():
        new_factor[...] = BETA * state[...] + (1.0 - BETA) * dot(grad[...], grad[...], ((0,), (0,)))

    grad_square[...] = jnp.sum(jnp.square(grad[...].astype(F32)), keepdims=True)
    new_root[...] = stale[...]

    def turn(value):
        row = lax.broadcasted_iota(jnp.int32, value.shape, 0)
        column = lax.broadcasted_iota(jnp.int32, value.shape, 1)
        identity = jnp.where(row == column, 5.0, 0.0)
        return ((identity - value.astype(F32)) * 0.25).astype(BF16)

    @pl.when(steps > 0)
    def _():
        factor = new_factor[...]
        norm = jnp.sqrt(jnp.sum(factor * factor, keepdims=True) + NORM_EPS)
        matrix[...] = (factor * (1.0 / norm)).astype(BF16)
        root_scale = lax.rsqrt(jnp.sqrt(norm)).astype(BF16).astype(F32)
        turned[...] = turn(matrix[...])
        new_root[...] = (root_scale * turned[...].astype(F32)).astype(BF16)

        def advance(level, carry):
            square[...] = dot(turned[...], turned[...]).astype(BF16)
            square[...] = dot(square[...], square[...]).astype(BF16)
            matrix[...] = dot(square[...], matrix[...]).astype(BF16)
            turned[...] = turn(matrix[...])
            new_root[...] = dot(new_root[...], turned[...]).astype(BF16)
            return carry

        lax.fori_loop(1, steps, advance, 0)

    @pl.when(side == 0)
    def _():
        payload[...] = new_root[...]

    @pl.when(side != 0)
    def _():
        payload[...] = dot(grad[...], new_root[...]).astype(BF16)


def roots(info, own, other, state, stale):
    full = jax.ShapeDtypeStruct((BLOCK, BLOCK), BF16)
    return pl.pallas_call(
        newton_kernel,
        out_shape=(
            jax.ShapeDtypeStruct((BLOCK, BLOCK), F32),
            full,
            full,
            jax.ShapeDtypeStruct((1, 1), F32),
        ),
        in_specs=[SMEM] + [VMEM] * 4,
        out_specs=[VMEM] * 4,
        scratch_shapes=[pltpu.VMEM((BLOCK, BLOCK), BF16)] * 4,
        compiler_params=LIMIT,
    )(info, own, other, state, stale)


def update_kernel(info, own, other, grad_square, out):
    side = info[0]

    def finish(left, product, start):
        raw = dot(left[...], product[...])
        total = jnp.sum(raw * raw, keepdims=True)
        ratio = jnp.sqrt(grad_square[...]) / jnp.sqrt(total + NORM_EPS)
        out[...] = (raw[start : start + HALF] * ratio).astype(BF16)

    @pl.when(side == 0)
    def _():
        finish(own, other, 0)

    @pl.when(side != 0)
    def _():
        finish(other, own, HALF)


def grafted(info, own, other, grad_square):
    return pl.pallas_call(
        update_kernel,
        out_shape=jax.ShapeDtypeStruct((HALF, BLOCK), BF16),
        in_specs=[SMEM] + [VMEM] * 3,
        out_specs=VMEM,
        compiler_params=LIMIT,
    )(info, own, other, grad_square)


def other_of(value, axis):
    return lax.ppermute(value, axis, [(0, 1), (1, 0)])


def along_z(value, by):
    size = lax.axis_size("z")
    return lax.ppermute(value, "z", [(i, (i - by) % size) for i in range(size)])


def two_away(value):
    size = lax.axis_size("z")
    pairs = [(i, (i - 2) % size) for i in range(size)]
    pairs += [(size + i, size + (i + 2) % size) for i in range(size)]
    return lax.ppermute(value, ("core", "z"), pairs)


def to_home(value):
    pairs = [(2 * lo + hi, 2 * hi + (hi ^ lo)) for lo in range(2) for hi in range(2)]
    return lax.ppermute(value, ("y_lo", "y_hi"), pairs)


def reduced(parts):
    got = lax.all_to_all(parts, ("y_lo", "x"), 0, 0, tiled=True)
    return jnp.sum(got.astype(F32), axis=0).astype(BF16)


def per_device(hidden, out_grad, token_counts, factor_state, stale_root, newton_steps):
    core = lax.axis_index("core")
    first = lax.rem(lax.axis_index("z"), CLASSES)
    far = other_of(hidden, "y_hi")
    near = other_of(hidden, "core")
    positions = lax.broadcasted_iota(jnp.int32, (out_grad.shape[0], 1), 0)
    kept = jnp.where(positions < token_counts[0], out_grad, jnp.zeros_like(out_grad)).T
    rows = kept.shape[0] // 2
    mine = lax.dynamic_slice_in_dim(kept, core * rows, rows, 0)
    sent = lax.dynamic_slice_in_dim(kept, (1 - core) * rows, rows, 0)
    block = jnp.concatenate([mine, other_of(sent, "core")], axis=1)
    size = lax.axis_size("z")
    strided = [[at + CLASSES * i for i in range(size // CLASSES)] for at in range(CLASSES)]
    own_class = lax.all_gather(block, "z", axis=0, tiled=True, axis_index_groups=strided)
    above = along_z(own_class, 1)
    below = along_z(own_class, -1)
    across = two_away(own_class)
    columns = (hidden, near, far, other_of(far, "core"))
    pieces = [
        reduced(partials([own_class], columns)),
        reduced(partials([above, below], columns)),
        reduced(partials([across], columns)),
    ]
    own = to_home(jnp.concatenate(pieces, axis=0))
    other = other_of(own, "core")
    info = jnp.stack([core, first, newton_steps[0, 0]]).astype(jnp.int32)
    new_factor, new_root, payload, grad_square = roots(info, own, other, factor_state, stale_root)
    update = grafted(info, payload, other_of(payload, "core"), grad_square)
    return (update, new_factor, new_root)


def solution(mesh):
    fine = Mesh(mesh.devices.reshape(2, 4, 2, 2, 16), AXES)
    spec = P(AXES[:3], AXES[3:])
    in_specs = (spec, spec, P(AXES[:3]), spec, spec, spec)
    return jax.shard_map(per_device, mesh=fine, in_specs=in_specs, out_specs=(spec, spec, spec), check_vma=False)
```

time: 346 us -> 136 us (0.39)
  the two profiles are of different devices: /device:TPU:89 before, /device:TPU:17 now
where the time goes in v1:
time: 136 us; the launch traced here: 135 us
  starting transfers between devices  54.7 us (40%)
  blocking collectives  31.4 us (23%)
  waiting for transfers between devices  28.6 us (21%)
  Pallas kernels  15.9 us (12%)
  between operations  2.13 us (2%)
  other arithmetic  1.47 us (1%)
    all_gather x1, blocking collectives, per_device(): lax.all_gather(block, 'z', axis=0, tiled=True, axis_index_groups=strided)  31.4 us
    ppermute x6, starting transfers between devices, other_of(): return lax.ppermute(value, axis, [(0, 1), (1, 0)])  30.8 us
    all_to_all x3, starting transfers between devices, reduced(): got = lax.all_to_all(parts, ('y_lo', 'x'), 0, 0, tiled=True)  14.1 us
    all_to_all x3, waiting for transfers between devices, reduced(): got = lax.all_to_all(parts, ('y_lo', 'x'), 0, 0, tiled=True)  9.18 us
    pallas_call x1, Pallas kernels, roots(): pl.pallas_call(newton_kernel, out_shape=(jax.ShapeDtypeStruct((BLOCK, BLO...  6.76 us
    pallas_call x3, Pallas kernels, partials(): pl.pallas_call(functools.partial(partial_kernel, classes), out_shape=jax....  6.42 us
    ppermute x6, waiting for transfers between devices, other_of(): return lax.ppermute(value, axis, [(0, 1), (1, 0)])  5.74 us
    ppermute x2, waiting for transfers between devices, along_z(): return lax.ppermute(value, 'z', [(i, (i - by) % size) for i in range(size)])  5.45 us
  transfers between devices with their start and end apart: 13, of which 8 were waited for; matrix products, arithmetic and copies ran while one was open for 2% of the time, Pallas kernels for 5%

profile of v1, /device:TPU:17, one launch (start us, length us, event | category | flops | bytes accessed | tf_op | source)
XLA Modules:
  0.0 135.2 jit_solution(17150680138080045804)
XLA Ops:
  0.6 1.9 %collective-permute-start.2 = (bf16[512,512]{1,0:T(8,128)(2,1)}, bf16[512,512]{1,0:T(8,128)(2,1)S(1)}, u32[]{:S(2)}, u32[]{:S(2)}) collective-permute-start(bf16[512,512]{1,0:T(8,128)(2,1)} %refs_1_.3), channel_id=1, source_target_pairs={{0,16},{16,0},{1,17},{17,1},{2,18},{18,2},{3,19},{19,3},{4,20},{20... | collective-permute-start | bytes 1572872 | tf_op jit(solution)/shard_map/ppermute | solution.py:157
  2.6 8.3 %collective-permute-start.1 = (bf16[512,512]{1,0:T(8,128)(2,1)}, bf16[512,512]{1,0:T(8,128)(2,1)S(1)}, u32[]{:S(2)}, u32[]{:S(2)}) collective-permute-start(bf16[512,512]{1,0:T(8,128)(2,1)} %refs_1_.3), channel_id=1, source_target_pairs={{0,32},{32,0},{1,33},{33,1},{2,34},{34,2},{3,35},{35,3},{4,36},{36... | collective-permute-start | bytes 1572872 | tf_op jit(solution)/shard_map/ppermute | solution.py:157
  10.9 1.0 copy.9
  12.6 2.2 %collective-permute-done.2.refs_3_.refs_4_ = bf16[512,512]{1,0:T(8,128)(2,1)S(1)} collective-permute-done((bf16[512,512]{1,0:T(8,128)(2,1)}, bf16[512,512]{1,0:T(8,128)(2,1)S(1)}, u32[]{:S(2)}, u32[]{:S(2)}) %collective-permute-start.2) | collective-permute-done | bytes 524320 | tf_op jit(solution)/shard_map/ppermute | solution.py:157
  14.8 5.7 %collective-permute-start.3 = (bf16[512,512]{1,0:T(8,128)(2,1)S(1)}, bf16[512,512]{1,0:T(8,128)(2,1)S(1)}, u32[]{:S(2)}, u32[]{:S(2)}) collective-permute-start(bf16[512,512]{1,0:T(8,128)(2,1)S(1)} %collective-permute-done.2.refs_3_.refs_4_), channel_id=1, source_target_pairs={{0,32},{32,0},{1,33},{33,1},{2,34},{34,2},{3,35},{35,3},{4,36},{36... | collective-permute-start | bytes 1572872 | tf_op jit(solution)/shard_map/ppermute | solution.py:157
  20.5 0.0 copy-start
  20.5 2.1 %collective-permute-start = (bf16[64,512]{1,0:T(8,128)(2,1)S(1)}, bf16[64,512]{1,0:T(8,128)(2,1)S(1)}, u32[]{:S(2)}, u32[]{:S(2)}) collective-permute-start(bf16[64,512]{1,0:T(8,128)(2,1)S(1)} %get-tuple-element.12), channel_id=1, source_target_pairs={{0,32},{32,0},{1,33},{33,1},{2,34},{34,2},{3,35},{35,3},{4,36},{36... | collective-permute-start | bytes 196616 | tf_op jit(solution)/shard_map/ppermute | solution.py:157
  22.6 1.2 collective-permute-done
  23.8 31.4 %all_gather.3.refs_0_ = bf16[256,1024]{1,0:T(8,128)(2,1)S(1)} all-gather(bf16[64,1024]{1,0:T(8,128)(2,1)S(1)} %pad_maximum_fusion.1), channel_id=1, replica_groups={{0,4,8,12},{1,5,9,13},{2,6,10,14},{3,7,11,15},{16,20,24,28},{17,21,25,2..., dimensions={0}, use_global_device_ids=true | all-gather | bytes 655360 | tf_op jit(solution)/shard_map/all_gather | solution.py:195
  55.2 2.2 %collective-permute-start.6 = (bf16[256,1024]{1,0:T(8,128)(2,1)S(1)}, bf16[256,1024]{1,0:T(8,128)(2,1)S(1)}, u32[]{:S(2)}, u32[]{:S(2)}) collective-permute-start(bf16[256,1024]{1,0:T(8,128)(2,1)S(1)} %all_gather.3.refs_0_), channel_id=1, source_target_pairs={{0,14},{1,15},{2,0},{3,1},{4,2},{5,3},{6,4},{7,5},{8,6},{9,7},{10,... | collective-permute-start | bytes 1572872 | tf_op jit(solution)/shard_map/ppermute | solution.py:169
  57.4 0.0 collective-permute-done.1.refs_2_.refs_3_
  57.4 0.0 collective-permute-done.3.refs_4_.refs_5_
  57.4 0.0 copy-done
  57.4 1.5 %shard_map.85 = bf16[8,64,512]{2,1,0:T(8,128)(2,1)} custom-call(bf16[256,1024]{1,0:T(8,128)(2,1)S(1)} %all_gather.3.refs_0_, bf16[512,512]{1,0:T(8,128)(2,1)S(1)} %copy-done, bf16[512,512]{1,0:T(8,128)(2,1)S(1)} %collective-permute-done.1.refs_2_.refs_3_, bf16[512,512]{1,0:T(8,128)(2,1)S(1)} %collective-permute-done.2.refs_3_.refs_4_, ...), custom_call_target="tpu_custom_call" | custom-call | tf_op jit(solution)/shard_map/pallas_call | solution.py:47
  58.9 4.7 %all-to-all-start = ((bf16[8,64,512]{2,1,0:T(8,128)(2,1)}), bf16[8,64,512]{2,1,0:T(8,128)(2,1)}, u32[]{:S(2)}, u32[]{:S(2)}) async-start(bf16[8,64,512]{2,1,0:T(8,128)(2,1)} %shard_map.85), calls=%async_computation | async-start | bytes 1048576 | tf_op jit(solution)/shard_map/all_to_all | solution.py:178
  63.7 3.1 %collective-permute-start.4 = (bf16[256,1024]{1,0:T(8,128)(2,1)S(1)}, bf16[256,1024]{1,0:T(8,128)(2,1)}, u32[]{:S(2)}, u32[]{:S(2)}) collective-permute-start(bf16[256,1024]{1,0:T(8,128)(2,1)S(1)} %all_gather.3.refs_0_), channel_id=1, source_target_pairs={{0,15},{1,0},{2,1},{3,2},{4,3},{5,4},{6,5},{7,6},{8,7},{9,8},{10,9... | collective-permute-start | bytes 1572872 | tf_op jit(solution)/shard_map/ppermute | solution.py:162
  66.8 2.2 %collective-permute-start.5 = (bf16[256,1024]{1,0:T(8,128)(2,1)S(1)}, bf16[256,1024]{1,0:T(8,128)(2,1)}, u32[]{:S(2)}, u32[]{:S(2)}) collective-permute-start(bf16[256,1024]{1,0:T(8,128)(2,1)S(1)} %all_gather.3.refs_0_), channel_id=1, source_target_pairs={{0,1},{1,2},{2,3},{3,4},{4,5},{5,6},{6,7},{7,8},{8,9},{9,10},{10,1... | collective-permute-start | bytes 1572872 | tf_op jit(solution)/shard_map/ppermute | solution.py:162
  69.0 3.2 %collective-permute-done.6.refs_0_ = bf16[256,1024]{1,0:T(8,128)(2,1)S(1)} collective-permute-done((bf16[256,1024]{1,0:T(8,128)(2,1)S(1)}, bf16[256,1024]{1,0:T(8,128)(2,1)S(1)}, u32[]{:S(2)}, u32[]{:S(2)}) %collective-permute-start.6) | collective-permute-done | bytes 524320 | tf_op jit(solution)/shard_map/ppermute | solution.py:169
  72.2 1.5 %shard_map.87 = bf16[8,64,512]{2,1,0:T(8,128)(2,1)} custom-call(bf16[256,1024]{1,0:T(8,128)(2,1)S(1)} %collective-permute-done.6.refs_0_, bf16[512,512]{1,0:T(8,128)(2,1)S(1)} %copy-done, bf16[512,512]{1,0:T(8,128)(2,1)S(1)} %collective-permute-done.1.refs_2_.refs_3_, bf16[512,512]{1,0:T(8,128)(2,1)S(1)} %collective-permute-done.2.refs_3_.refs_4_, ...), custom_call_target="tpu_custom_call" | custom-call | tf_op jit(solution)/shard_map/pallas_call | solution.py:47
  73.7 0.0 all-to-all-done
  73.7 4.7 %all-to-all-start.2 = ((bf16[8,64,512]{2,1,0:T(8,128)(2,1)}), bf16[8,64,512]{2,1,0:T(8,128)(2,1)S(1)}, u32[]{:S(2)}, u32[]{:S(2)}) async-start(bf16[8,64,512]{2,1,0:T(8,128)(2,1)} %shard_map.87), calls=%async_computation.2 | async-start | bytes 1048576 | tf_op jit(solution)/shard_map/all_to_all | solution.py:178
  78.4 5.5 %collective-permute-done.4.refs_0_ = bf16[256,1024]{1,0:T(8,128)(2,1)} collective-permute-done((bf16[256,1024]{1,0:T(8,128)(2,1)S(1)}, bf16[256,1024]{1,0:T(8,128)(2,1)}, u32[]{:S(2)}, u32[]{:S(2)}) %collective-permute-start.4) | collective-permute-done | bytes 524320 | tf_op jit(solution)/shard_map/ppermute | solution.py:162
  83.9 0.0 collective-permute-done.5.refs_1_
  83.9 3.4 %shard_map.86 = bf16[8,128,512]{2,1,0:T(8,128)(2,1)} custom-call(bf16[256,1024]{1,0:T(8,128)(2,1)} %collective-permute-done.4.refs_0_, bf16[256,1024]{1,0:T(8,128)(2,1)} %collective-permute-done.5.refs_1_, bf16[512,512]{1,0:T(8,128)(2,1)S(1)} %copy-done, bf16[512,512]{1,0:T(8,128)(2,1)S(1)} %collective-permute-done.1.refs_2_.refs_3_, ...), custom_call_target="tpu_custom_call" | custom-call | tf_op jit(solution)/shard_map/pallas_call | solution.py:47
  87.3 0.0 all-to-all-done.2
  87.3 4.6 %all-to-all-start.1 = ((bf16[8,128,512]{2,1,0:T(8,128)(2,1)}), bf16[8,128,512]{2,1,0:T(8,128)(2,1)S(1)}, u32[]{:S(2)}, u32[]{:S(2)}) async-start(bf16[8,128,512]{2,1,0:T(8,128)(2,1)} %shard_map.86), calls=%async_computation.1 | async-start | bytes 2097152 | tf_op jit(solution)/shard_map/all_to_all | solution.py:178
  91.9 1.1 reduce_sum.36
  93.0 0.0 copy-start.1
  93.0 0.1 reduce_sum.38
  93.1 9.2 %all-to-all-done.1 = bf16[8,128,512]{2,1,0:T(8,128)(2,1)S(1)} async-done(((bf16[8,128,512]{2,1,0:T(8,128)(2,1)}), bf16[8,128,512]{2,1,0:T(8,128)(2,1)S(1)}, u32[]{:S(2)}, u32[]{:S(2)}) %all-to-all-start.1) | async-done | bytes 1048608 | tf_op jit(solution)/shard_map/all_to_all | solution.py:178
  102.3 0.1 reduce_sum.37
  102.4 0.0 copy-start.2
  102.5 2.4 %collective-permute-start.7 = (bf16[256,512]{1,0:T(8,128)(2,1)S(1)}, bf16[256,512]{1,0:T(8,128)(2,1)S(1)}, u32[]{:S(2)}, u32[]{:S(2)}) collective-permute-start(bf16[256,512]{1,0:T(8,128)(2,1)S(1)} %pad_maximum_fusion), channel_id=1, source_target_pairs={{0,0},{16,272},{256,16},{272,256},{1,1},{17,273},{257,17},{273,257... | collective-permute-start | bytes 786440 | tf_op jit(solution)/shard_map/ppermute | solution.py:174
  104.9 5.0 %collective-permute-done.7.own = bf16[256,512]{1,0:T(8,128)(2,1)S(1)} collective-permute-done((bf16[256,512]{1,0:T(8,128)(2,1)S(1)}, bf16[256,512]{1,0:T(8,128)(2,1)S(1)}, u32[]{:S(2)}, u32[]{:S(2)}) %collective-permute-start.7) | collective-permute-done | bytes 262176 | tf_op jit(solution)/shard_map/ppermute | solution.py:174
  109.8 11.0 %collective-permute-start.8 = (bf16[256,512]{1,0:T(8,128)(2,1)S(1)}, bf16[256,512]{1,0:T(8,128)(2,1)S(1)}, u32[]{:S(2)}, u32[]{:S(2)}) collective-permute-start(bf16[256,512]{1,0:T(8,128)(2,1)S(1)} %collective-permute-done.7.own), channel_id=1, source_target_pairs={{0,32},{32,0},{1,33},{33,1},{2,34},{34,2},{3,35},{35,3},{4,36},{36... | collective-permute-start | bytes 786440 | tf_op jit(solution)/shard_map/ppermute | solution.py:157
  121.5 0.1 pad_add_fusion.info
  121.6 0.4 collective-permute-done.8.other
  122.0 0.0 copy-done.1
  122.0 0.0 copy-done.2
  122.0 6.8 %shard_map.88 = (f32[512,512]{1,0:T(8,128)}, bf16[512,512]{1,0:T(8,128)(2,1)}, bf16[512,512]{1,0:T(8,128)(2,1)S(1)}, f32[1,1]{1,0:T(1,128)}) custom-call(s32[3]{0:T(128)S(1)} %pad_add_fusion.info, bf16[256,512]{1,0:T(8,128)(2,1)S(1)} %collective-permute-done.7.own, bf16[256,512]{1,0:T(8,128)(2,1)S(1)} %collective-permute-done.8.other, ...), custom_call_target="tpu_custom_call" | custom-call | tf_op jit(solution)/shard_map/pallas_call | solution.py:113
  128.7 1.9 %collective-permute-start.9 = (bf16[512,512]{1,0:T(8,128)(2,1)S(1)}, bf16[512,512]{1,0:T(8,128)(2,1)S(1)}, u32[]{:S(2)}, u32[]{:S(2)}) collective-permute-start(bf16[512,512]{1,0:T(8,128)(2,1)S(1)} %get-tuple-element.7.own), channel_id=1, source_target_pairs={{0,32},{32,0},{1,33},{33,1},{2,34},{34,2},{3,35},{35,3},{4,36},{36... | collective-permute-start | bytes 1572872 | tf_op jit(solution)/shard_map/ppermute | solution.py:157
  130.7 1.9 %collective-permute-done.9.other = bf16[512,512]{1,0:T(8,128)(2,1)S(1)} collective-permute-done((bf16[512,512]{1,0:T(8,128)(2,1)S(1)}, bf16[512,512]{1,0:T(8,128)(2,1)S(1)}, u32[]{:S(2)}, u32[]{:S(2)}) %collective-permute-start.9) | collective-permute-done | bytes 524320 | tf_op jit(solution)/shard_map/ppermute | solution.py:157
  132.5 2.7 %shard_map.89 = bf16[256,512]{1,0:T(8,128)(2,1)} custom-call(s32[3]{0:T(128)S(1)} %pad_add_fusion.info, bf16[512,512]{1,0:T(8,128)(2,1)S(1)} %get-tuple-element.7.own, bf16[512,512]{1,0:T(8,128)(2,1)S(1)} %collective-permute-done.9.other, f32[1,1]{1,0:T(1,128)} %get-tuple-element.8.grad_square), custom_call_target="tpu_custom_call" | custom-call | tf_op jit(solution)/shard_map/pallas_call | solution.py:147
  (5 shorter events, 0.1 us)
Async XLA Ops:
  0.6 14.2 %collective-permute-start.2 = (bf16[512,512]{1,0:T(8,128)(2,1)}, bf16[512,512]{1,0:T(8,128)(2,1)S(1)}, u32[]{:S(2)}, u32[]{:S(2)}) collective-permute-start(bf16[512,512]{1,0:T(8,128)(2,1)} %refs_1_.3), channel_id=1, source_target_pairs={{0,16},{16,0},{1,17},{17,1},{2,18},{18,2},{3,19},{19,3},{4,20},{20... | collective-permute-start | bytes 1572872 | tf_op jit(solution)/shard_map/ppermute | solution.py:157
  2.6 54.8 %collective-permute-start.1 = (bf16[512,512]{1,0:T(8,128)(2,1)}, bf16[512,512]{1,0:T(8,128)(2,1)S(1)}, u32[]{:S(2)}, u32[]{:S(2)}) collective-permute-start(bf16[512,512]{1,0:T(8,128)(2,1)} %refs_1_.3), channel_id=1, source_target_pairs={{0,32},{32,0},{1,33},{33,1},{2,34},{34,2},{3,35},{35,3},{4,36},{36... | collective-permute-start | bytes 1572872 | tf_op jit(solution)/shard_map/ppermute | solution.py:157
  14.8 42.6 %collective-permute-start.3 = (bf16[512,512]{1,0:T(8,128)(2,1)S(1)}, bf16[512,512]{1,0:T(8,128)(2,1)S(1)}, u32[]{:S(2)}, u32[]{:S(2)}) collective-permute-start(bf16[512,512]{1,0:T(8,128)(2,1)S(1)} %collective-permute-done.2.refs_3_.refs_4_), channel_id=1, source_target_pairs={{0,32},{32,0},{1,33},{33,1},{2,34},{34,2},{3,35},{35,3},{4,36},{36... | collective-permute-start | bytes 1572872 | tf_op jit(solution)/shard_map/ppermute | solution.py:157
  20.5 36.9 %copy-start = (bf16[512,512]{1,0:T(8,128)(2,1)S(1)}, bf16[512,512]{1,0:T(8,128)(2,1)}, u32[]{:S(2)}) copy-start(bf16[512,512]{1,0:T(8,128)(2,1)} %refs_1_.3) | copy-start | bytes 1572868
  20.5 3.3 %collective-permute-start = (bf16[64,512]{1,0:T(8,128)(2,1)S(1)}, bf16[64,512]{1,0:T(8,128)(2,1)S(1)}, u32[]{:S(2)}, u32[]{:S(2)}) collective-permute-start(bf16[64,512]{1,0:T(8,128)(2,1)S(1)} %get-tuple-element.12), channel_id=1, source_target_pairs={{0,32},{32,0},{1,33},{33,1},{2,34},{34,2},{3,35},{35,3},{4,36},{36... | collective-permute-start | bytes 196616 | tf_op jit(solution)/shard_map/ppermute | solution.py:157
  55.2 17.0 %collective-permute-start.6 = (bf16[256,1024]{1,0:T(8,128)(2,1)S(1)}, bf16[256,1024]{1,0:T(8,128)(2,1)S(1)}, u32[]{:S(2)}, u32[]{:S(2)}) collective-permute-start(bf16[256,1024]{1,0:T(8,128)(2,1)S(1)} %all_gather.3.refs_0_), channel_id=1, source_target_pairs={{0,14},{1,15},{2,0},{3,1},{4,2},{5,3},{6,4},{7,5},{8,6},{9,7},{10,... | collective-permute-start | bytes 1572872 | tf_op jit(solution)/shard_map/ppermute | solution.py:169
  58.9 14.7 %all-to-all-start = ((bf16[8,64,512]{2,1,0:T(8,128)(2,1)}), bf16[8,64,512]{2,1,0:T(8,128)(2,1)}, u32[]{:S(2)}, u32[]{:S(2)}) async-start(bf16[8,64,512]{2,1,0:T(8,128)(2,1)} %shard_map.85), calls=%async_computation | async-start | bytes 1048576 | tf_op jit(solution)/shard_map/all_to_all | solution.py:178
  63.7 20.2 %collective-permute-start.4 = (bf16[256,1024]{1,0:T(8,128)(2,1)S(1)}, bf16[256,1024]{1,0:T(8,128)(2,1)}, u32[]{:S(2)}, u32[]{:S(2)}) collective-permute-start(bf16[256,1024]{1,0:T(8,128)(2,1)S(1)} %all_gather.3.refs_0_), channel_id=1, source_target_pairs={{0,15},{1,0},{2,1},{3,2},{4,3},{5,4},{6,5},{7,6},{8,7},{9,8},{10,9... | collective-permute-start | bytes 1572872 | tf_op jit(solution)/shard_map/ppermute | solution.py:162
  66.8 17.1 %collective-permute-start.5 = (bf16[256,1024]{1,0:T(8,128)(2,1)S(1)}, bf16[256,1024]{1,0:T(8,128)(2,1)}, u32[]{:S(2)}, u32[]{:S(2)}) collective-permute-start(bf16[256,1024]{1,0:T(8,128)(2,1)S(1)} %all_gather.3.refs_0_), channel_id=1, source_target_pairs={{0,1},{1,2},{2,3},{3,4},{4,5},{5,6},{6,7},{7,8},{8,9},{9,10},{10,1... | collective-permute-start | bytes 1572872 | tf_op jit(solution)/shard_map/ppermute | solution.py:162
  73.7 13.6 %all-to-all-start.2 = ((bf16[8,64,512]{2,1,0:T(8,128)(2,1)}), bf16[8,64,512]{2,1,0:T(8,128)(2,1)S(1)}, u32[]{:S(2)}, u32[]{:S(2)}) async-start(bf16[8,64,512]{2,1,0:T(8,128)(2,1)} %shard_map.87), calls=%async_computation.2 | async-start | bytes 1048576 | tf_op jit(solution)/shard_map/all_to_all | solution.py:178
  87.3 15.0 %all-to-all-start.1 = ((bf16[8,128,512]{2,1,0:T(8,128)(2,1)}), bf16[8,128,512]{2,1,0:T(8,128)(2,1)S(1)}, u32[]{:S(2)}, u32[]{:S(2)}) async-start(bf16[8,128,512]{2,1,0:T(8,128)(2,1)} %shard_map.86), calls=%async_computation.1 | async-start | bytes 2097152 | tf_op jit(solution)/shard_map/all_to_all | solution.py:178
  93.0 29.0 %copy-start.1 = (f32[512,512]{1,0:T(8,128)S(1)}, f32[512,512]{1,0:T(8,128)}, u32[]{:S(2)}) copy-start(f32[512,512]{1,0:T(8,128)} %state.1) | copy-start | bytes 3145732
  102.4 19.5 %copy-start.2 = (bf16[512,512]{1,0:T(8,128)(2,1)S(1)}, bf16[512,512]{1,0:T(8,128)(2,1)}, u32[]{:S(2)}) copy-start(bf16[512,512]{1,0:T(8,128)(2,1)} %stale.1) | copy-start | bytes 1572868
  102.5 7.4 %collective-permute-start.7 = (bf16[256,512]{1,0:T(8,128)(2,1)S(1)}, bf16[256,512]{1,0:T(8,128)(2,1)S(1)}, u32[]{:S(2)}, u32[]{:S(2)}) collective-permute-start(bf16[256,512]{1,0:T(8,128)(2,1)S(1)} %pad_maximum_fusion), channel_id=1, source_target_pairs={{0,0},{16,272},{256,16},{272,256},{1,1},{17,273},{257,17},{273,257... | collective-permute-start | bytes 786440 | tf_op jit(solution)/shard_map/ppermute | solution.py:174
  109.8 12.1 %collective-permute-start.8 = (bf16[256,512]{1,0:T(8,128)(2,1)S(1)}, bf16[256,512]{1,0:T(8,128)(2,1)S(1)}, u32[]{:S(2)}, u32[]{:S(2)}) collective-permute-start(bf16[256,512]{1,0:T(8,128)(2,1)S(1)} %collective-permute-done.7.own), channel_id=1, source_target_pairs={{0,32},{32,0},{1,33},{33,1},{2,34},{34,2},{3,35},{35,3},{4,36},{36... | collective-permute-start | bytes 786440 | tf_op jit(solution)/shard_map/ppermute | solution.py:157
  128.7 3.8 %collective-permute-start.9 = (bf16[512,512]{1,0:T(8,128)(2,1)S(1)}, bf16[512,512]{1,0:T(8,128)(2,1)S(1)}, u32[]{:S(2)}, u32[]{:S(2)}) collective-permute-start(bf16[512,512]{1,0:T(8,128)(2,1)S(1)} %get-tuple-element.7.own), channel_id=1, source_target_pairs={{0,32},{32,0},{1,33},{33,1},{2,34},{34,2},{3,35},{35,3},{4,36},{36... | collective-permute-start | bytes 1572872 | tf_op jit(solution)/shard_map/ppermute | solution.py:157

commit v2 on v1

--- a/solution.py
+++ b/solution.py
@@ -53,15 +53,19 @@
     )(*features, *hidden)
 
 
-def newton_kernel(info, own, other, state, stale, new_factor, new_root, payload, grad_square, grad, matrix, turned, square):
+def newton_kernel(info, own, last, other, other_last, state, stale, new_factor, new_root, payload, grad_square, grad, matrix, turned, square):
     side, first, steps = info[0], info[1], info[2]
     rows = HALF // CLASSES
     for at, shift in enumerate((0, 1, 3, 2)):
         start = lax.rem(first + shift, CLASSES) * (2 * rows)
         mine = pl.multiple_of(start + side * rows, rows)
         theirs = pl.multiple_of(start + (1 - side) * rows, rows)
-        grad[pl.ds(mine, rows), :] = own[at * rows : (at + 1) * rows, :]
-        grad[pl.ds(theirs, rows), :] = other[at * rows : (at + 1) * rows, :]
+        if at < CLASSES - 1:
+            grad[pl.ds(mine, rows), :] = own[at * rows : (at + 1) * rows, :]
+            grad[pl.ds(theirs, rows), :] = other[at * rows : (at + 1) * rows, :]
+        else:
+            grad[pl.ds(mine, rows), :] = last[...]
+            grad[pl.ds(theirs, rows), :] = other_last[...]
 
     @pl.when(side == 0)
     def _():
@@ -108,7 +112,7 @@
         payload[...] = dot(grad[...], new_root[...]).astype(BF16)
 
 
-def roots(info, own, other, state, stale):
+def roots(info, own, last, other, other_last, state, stale):
     full = jax.ShapeDtypeStruct((BLOCK, BLOCK), BF16)
     return pl.pallas_call(
         newton_kernel,
@@ -118,11 +122,11 @@
             full,
             jax.ShapeDtypeStruct((1, 1), F32),
         ),
-        in_specs=[SMEM] + [VMEM] * 4,
+        in_specs=[SMEM] + [VMEM] * 6,
         out_specs=[VMEM] * 4,
         scratch_shapes=[pltpu.VMEM((BLOCK, BLOCK), BF16)] * 4,
         compiler_params=LIMIT,
-    )(info, own, other, state, stale)
+    )(info, own, last, other, other_last, state, stale)
 
 
 def update_kernel(info, own, other, grad_square, out):
@@ -157,6 +161,10 @@
     return lax.ppermute(value, axis, [(0, 1), (1, 0)])
 
 
+def across_chip(value):
+    return lax.ppermute(value, ("core", "y_hi"), [(i, 3 - i) for i in range(4)])
+
+
 def along_z(value, by):
     size = lax.axis_size("z")
     return lax.ppermute(value, "z", [(i, (i - by) % size) for i in range(size)])
@@ -182,30 +190,32 @@
 def per_device(hidden, out_grad, token_counts, factor_state, stale_root, newton_steps):
     core = lax.axis_index("core")
     first = lax.rem(lax.axis_index("z"), CLASSES)
-    far = other_of(hidden, "y_hi")
-    near = other_of(hidden, "core")
     positions = lax.broadcasted_iota(jnp.int32, (out_grad.shape[0], 1), 0)
     kept = jnp.where(positions < token_counts[0], out_grad, jnp.zeros_like(out_grad)).T
     rows = kept.shape[0] // 2
     mine = lax.dynamic_slice_in_dim(kept, core * rows, rows, 0)
     sent = lax.dynamic_slice_in_dim(kept, (1 - core) * rows, rows, 0)
+    sent, hidden = lax.optimization_barrier((sent, hidden))
     block = jnp.concatenate([mine, other_of(sent, "core")], axis=1)
+    far = other_of(hidden, "y_hi")
+    near = other_of(hidden, "core")
+    columns = (hidden, near, far, across_chip(hidden))
     size = lax.axis_size("z")
     strided = [[at + CLASSES * i for i in range(size // CLASSES)] for at in range(CLASSES)]
     own_class = lax.all_gather(block, "z", axis=0, tiled=True, axis_index_groups=strided)
     above = along_z(own_class, 1)
     below = along_z(own_class, -1)
     across = two_away(own_class)
-    columns = (hidden, near, far, other_of(far, "core"))
-    pieces = [
-        reduced(partials([own_class], columns)),
-        reduced(partials([above, below], columns)),
-        reduced(partials([across], columns)),
-    ]
-    own = to_home(jnp.concatenate(pieces, axis=0))
-    other = other_of(own, "core")
+    own = reduced(partials([own_class], columns))
+    above, below, across, own = lax.optimization_barrier((above, below, across, own))
+    rest = reduced(partials([above, below, across], columns))
+    home = to_home(jnp.concatenate([own, rest], axis=0))
+    away = other_of(home, "core")
+    own, last, other, other_last = home[:192], home[192:], away[:192], away[192:]
     info = jnp.stack([core, first, newton_steps[0, 0]]).astype(jnp.int32)
-    new_factor, new_root, payload, grad_square = roots(info, own, other, factor_state, stale_root)
+    new_factor, new_root, payload, grad_square = roots(
+        info, own, last, other, other_last, factor_state, stale_root
+    )
     update = grafted(info, payload, other_of(payload, "core"), grad_square)
     return (update, new_factor, new_root)
 

time: 136 us -> 130 us (0.956)
  the two profiles are of different devices: /device:TPU:17 before, /device:TPU:9 now
where the time goes in v2:
time: 130 us
  blocking collectives  63.7 us (49%)
  starting transfers between devices  34.4 us (26%)
  waiting for transfers between devices  13.6 us (10%)
  Pallas kernels  13.2 us (10%)
  between operations  2.21 us (2%)
  other arithmetic  1.5 us (1%)
    all_to_all x2, blocking collectives, reduced(): got = lax.all_to_all(parts, ('y_lo', 'x'), 0, 0, tiled=True)  32.3 us
    all_gather x1, blocking collectives, per_device(): lax.all_gather(block, 'z', axis=0, tiled=True, axis_index_groups=strided)  31.4 us
    ppermute x5, starting transfers between devices, other_of(): return lax.ppermute(value, axis, [(0, 1), (1, 0)])  17.3 us
    pallas_call x1, Pallas kernels, roots(): pl.pallas_call(newton_kernel, out_shape=(jax.ShapeDtypeStruct((BLOCK, BLO...  6.77 us
    ppermute x2, starting transfers between devices, along_z(): return lax.ppermute(value, 'z', [(i, (i - by) % size) for i in range(size)])  6.5 us
    ppermute x2, waiting for transfers between devices, along_z(): return lax.ppermute(value, 'z', [(i, (i - by) % size) for i in range(size)])  5.68 us
    ppermute x1, waiting for transfers between devices, to_home(): return lax.ppermute(value, ('y_lo', 'y_hi'), pairs)  4.8 us
    ppermute x1, starting transfers between devices, across_chip(): return lax.ppermute(value, ('core', 'y_hi'), [(i, 3 - i) for i in range(4)])  4.49 us
  transfers between devices with their start and end apart: 10, of which 6 were waited for; matrix products, arithmetic and copies ran while one was open for 1% of the time, Pallas kernels for 1%

profile of v2, /device:TPU:9, one launch (start us, length us, event | category | flops | bytes accessed | tf_op | source)
XLA Modules:
  0.0 129.7 jit_solution(686196363613487674)
XLA Ops:
  0.6 0.0 copy-start
  1.4 1.0 copy.9
  2.4 4.5 %collective-permute-start.6 = (bf16[512,512]{1,0:T(8,128)(2,1)}, bf16[512,512]{1,0:T(8,128)(2,1)S(1)}, u32[]{:S(2)}, u32[]{:S(2)}) collective-permute-start(bf16[512,512]{1,0:T(8,128)(2,1)} %refs_3_), channel_id=1, source_target_pairs={{0,48},{16,32},{32,16},{48,0},{1,49},{17,33},{33,17},{49,1},{2,50}... | collective-permute-start | bytes 1572872 | tf_op jit(solution)/shard_map/ppermute | solution.py:165
  6.9 2.9 %collective-permute-start.5 = (bf16[512,512]{1,0:T(8,128)(2,1)}, bf16[512,512]{1,0:T(8,128)(2,1)S(1)}, u32[]{:S(2)}, u32[]{:S(2)}) collective-permute-start(bf16[512,512]{1,0:T(8,128)(2,1)} %refs_3_), channel_id=1, source_target_pairs={{0,16},{16,0},{1,17},{17,1},{2,18},{18,2},{3,19},{19,3},{4,20},{20... | collective-permute-start | bytes 1572872 | tf_op jit(solution)/shard_map/ppermute | solution.py:161
  9.8 2.0 %collective-permute-start.4 = (bf16[512,512]{1,0:T(8,128)(2,1)}, bf16[512,512]{1,0:T(8,128)(2,1)S(1)}, u32[]{:S(2)}, u32[]{:S(2)}) collective-permute-start(bf16[512,512]{1,0:T(8,128)(2,1)} %refs_3_), channel_id=1, source_target_pairs={{0,32},{32,0},{1,33},{33,1},{2,34},{34,2},{3,35},{35,3},{4,36},{36... | collective-permute-start | bytes 1572872 | tf_op jit(solution)/shard_map/ppermute | solution.py:161
  11.8 2.3 %collective-permute-start = (bf16[64,512]{1,0:T(8,128)(2,1)S(1)}, bf16[64,512]{1,0:T(8,128)(2,1)S(1)}, u32[]{:S(2)}, u32[]{:S(2)}) collective-permute-start(bf16[64,512]{1,0:T(8,128)(2,1)S(1)} %get-tuple-element.13), channel_id=1, source_target_pairs={{0,32},{32,0},{1,33},{33,1},{2,34},{34,2},{3,35},{35,3},{4,36},{36... | collective-permute-start | bytes 196616 | tf_op jit(solution)/shard_map/ppermute | solution.py:161
  14.1 0.9 collective-permute-done
  15.0 31.4 %all_gather.3.refs_0_ = bf16[256,1024]{1,0:T(8,128)(2,1)S(1)} all-gather(bf16[64,1024]{1,0:T(8,128)(2,1)S(1)} %pad_maximum_fusion.1), channel_id=1, replica_groups={{0,4,8,12},{1,5,9,13},{2,6,10,14},{3,7,11,15},{16,20,24,28},{17,21,25,2..., dimensions={0}, use_global_device_ids=true | all-gather | bytes 655360 | tf_op jit(solution)/shard_map/all_gather | solution.py:205
  46.5 2.1 %collective-permute-start.3 = (bf16[256,1024]{1,0:T(8,128)(2,1)S(1)}, bf16[256,1024]{1,0:T(8,128)(2,1)S(1)}, u32[]{:S(2)}, u32[]{:S(2)}) collective-permute-start(bf16[256,1024]{1,0:T(8,128)(2,1)S(1)} %all_gather.3.refs_0_), channel_id=1, source_target_pairs={{0,14},{1,15},{2,0},{3,1},{4,2},{5,3},{6,4},{7,5},{8,6},{9,7},{10,... | collective-permute-start | bytes 1572872 | tf_op jit(solution)/shard_map/ppermute | solution.py:177
  48.5 2.6 %collective-permute-start.2 = (bf16[256,1024]{1,0:T(8,128)(2,1)S(1)}, bf16[256,1024]{1,0:T(8,128)(2,1)}, u32[]{:S(2)}, u32[]{:S(2)}) collective-permute-start(bf16[256,1024]{1,0:T(8,128)(2,1)S(1)} %all_gather.3.refs_0_), channel_id=1, source_target_pairs={{0,1},{1,2},{2,3},{3,4},{4,5},{5,6},{6,7},{7,8},{8,9},{9,10},{10,1... | collective-permute-start | bytes 1572872 | tf_op jit(solution)/shard_map/ppermute | solution.py:170
  51.2 0.0 collective-permute-done.6.refs_4_.refs_6_
  51.2 3.9 %collective-permute-start.1 = (bf16[256,1024]{1,0:T(8,128)(2,1)S(1)}, bf16[256,1024]{1,0:T(8,128)(2,1)}, u32[]{:S(2)}, u32[]{:S(2)}) collective-permute-start(bf16[256,1024]{1,0:T(8,128)(2,1)S(1)} %all_gather.3.refs_0_), channel_id=1, source_target_pairs={{0,15},{1,0},{2,1},{3,2},{4,3},{5,4},{6,5},{7,6},{8,7},{9,8},{10,9... | collective-permute-start | bytes 1572872 | tf_op jit(solution)/shard_map/ppermute | solution.py:170
  55.1 0.0 collective-permute-done.5.refs_3_.refs_5_
  55.1 0.0 collective-permute-done.4.refs_2_.refs_4_
  55.1 0.0 copy-done
  55.1 0.7 shard_map.85
  55.8 11.5 %all_to_all.10 = bf16[8,64,512]{2,1,0:T(8,128)(2,1)} all-to-all(bf16[8,64,512]{2,1,0:T(8,128)(2,1)S(1)} %shard_map.85), channel_id=1, replica_groups=mesh['y_lo'=2,'x'=4,'core'=2,'y_hi'=2,'z'=16] {'y_lo','x'}, dimensions={0} | all-to-all | bytes 1048576 | tf_op jit(solution)/shard_map/all_to_all | solution.py:186
  67.3 1.1 reduce_sum.24
  68.4 0.0 collective-permute-done.3.refs_2_
  68.4 4.1 %collective-permute-done.2.refs_1_ = bf16[256,1024]{1,0:T(8,128)(2,1)} collective-permute-done((bf16[256,1024]{1,0:T(8,128)(2,1)S(1)}, bf16[256,1024]{1,0:T(8,128)(2,1)}, u32[]{:S(2)}, u32[]{:S(2)}) %collective-permute-start.2) | collective-permute-done | bytes 524320 | tf_op jit(solution)/shard_map/ppermute | solution.py:170
  72.5 1.6 %collective-permute-done.1.refs_0_ = bf16[256,1024]{1,0:T(8,128)(2,1)} collective-permute-done((bf16[256,1024]{1,0:T(8,128)(2,1)S(1)}, bf16[256,1024]{1,0:T(8,128)(2,1)}, u32[]{:S(2)}, u32[]{:S(2)}) %collective-permute-start.1) | collective-permute-done | bytes 524320 | tf_op jit(solution)/shard_map/ppermute | solution.py:170
  74.1 3.0 %shard_map.86 = bf16[8,192,512]{2,1,0:T(8,128)(2,1)S(1)} custom-call(bf16[256,1024]{1,0:T(8,128)(2,1)} %collective-permute-done.1.refs_0_, bf16[256,1024]{1,0:T(8,128)(2,1)} %collective-permute-done.2.refs_1_, bf16[256,1024]{1,0:T(8,128)(2,1)S(1)} %collective-permute-done.3.refs_2_, bf16[512,512]{1,0:T(8,128)(2,1)S(1)} %copy-done, ...), custom_call_target="tpu_custom_call" | custom-call | tf_op jit(solution)/shard_map/pallas_call | solution.py:47
  77.1 20.8 %all_to_all.11 = bf16[8,192,512]{2,1,0:T(8,128)(2,1)S(1)} all-to-all(bf16[8,192,512]{2,1,0:T(8,128)(2,1)S(1)} %shard_map.86), channel_id=1, replica_groups=mesh['y_lo'=2,'x'=4,'core'=2,'y_hi'=2,'z'=16] {'y_lo','x'}, dimensions={0} | all-to-all | bytes 3145728 | tf_op jit(solution)/shard_map/all_to_all | solution.py:186
  97.9 0.0 copy-start.1
  97.9 0.0 copy-start.2
  97.9 0.3 reduce_sum.25
  98.1 4.1 %collective-permute-start.7 = (bf16[256,512]{1,0:T(8,128)(2,1)S(1)}, bf16[256,512]{1,0:T(8,128)(2,1)S(1)}, u32[]{:S(2)}, u32[]{:S(2)}) collective-permute-start(bf16[256,512]{1,0:T(8,128)(2,1)S(1)} %pad_maximum_fusion), channel_id=1, source_target_pairs={{0,0},{16,272},{256,16},{272,256},{1,1},{17,273},{257,17},{273,257... | collective-permute-start | bytes 786440 | tf_op jit(solution)/shard_map/ppermute | solution.py:182
  102.2 4.8 %collective-permute-done.7 = bf16[256,512]{1,0:T(8,128)(2,1)S(1)} collective-permute-done((bf16[256,512]{1,0:T(8,128)(2,1)S(1)}, bf16[256,512]{1,0:T(8,128)(2,1)S(1)}, u32[]{:S(2)}, u32[]{:S(2)}) %collective-permute-start.7) | collective-permute-done | bytes 262176 | tf_op jit(solution)/shard_map/ppermute | solution.py:182
  107.0 8.2 %collective-permute-start.8 = (bf16[256,512]{1,0:T(8,128)(2,1)S(1)}, bf16[256,512]{1,0:T(8,128)(2,1)S(1)}, u32[]{:S(2)}, u32[]{:S(2)}) collective-permute-start(bf16[256,512]{1,0:T(8,128)(2,1)S(1)} %collective-permute-done.7), channel_id=1, source_target_pairs={{0,32},{32,0},{1,33},{33,1},{2,34},{34,2},{3,35},{35,3},{4,36},{36... | collective-permute-start | bytes 786440 | tf_op jit(solution)/shard_map/ppermute | solution.py:161
  115.9 0.1 pad_add_fusion.info
  116.0 0.4 collective-permute-done.8
  116.4 0.0 copy-done.1
  116.4 0.0 copy-done.2
  116.4 6.8 %shard_map.87 = (f32[512,512]{1,0:T(8,128)}, bf16[512,512]{1,0:T(8,128)(2,1)}, bf16[512,512]{1,0:T(8,128)(2,1)S(1)}, f32[1,1]{1,0:T(1,128)}) custom-call(s32[3]{0:T(128)S(1)} %pad_add_fusion.info, bf16[192,512]{1,0:T(8,128)(2,1)S(1)} %slice.16.own, bf16[64,512]{1,0:T(8,128)(2,1)S(1)} %slice.17.last, bf16[192,512]{1,0:T(8,128)(2,1)S(1)} %slice.18.other, ...), custom_call_target="tpu_custom_call" | custom-call | tf_op jit(solution)/shard_map/pallas_call | solution.py:117
  123.2 1.9 %collective-permute-start.9 = (bf16[512,512]{1,0:T(8,128)(2,1)S(1)}, bf16[512,512]{1,0:T(8,128)(2,1)S(1)}, u32[]{:S(2)}, u32[]{:S(2)}) collective-permute-start(bf16[512,512]{1,0:T(8,128)(2,1)S(1)} %get-tuple-element.19.own), channel_id=1, source_target_pairs={{0,32},{32,0},{1,33},{33,1},{2,34},{34,2},{3,35},{35,3},{4,36},{36... | collective-permute-start | bytes 1572872 | tf_op jit(solution)/shard_map/ppermute | solution.py:161
  125.1 1.9 %collective-permute-done.9.other = bf16[512,512]{1,0:T(8,128)(2,1)S(1)} collective-permute-done((bf16[512,512]{1,0:T(8,128)(2,1)S(1)}, bf16[512,512]{1,0:T(8,128)(2,1)S(1)}, u32[]{:S(2)}, u32[]{:S(2)}) %collective-permute-start.9) | collective-permute-done | bytes 524320 | tf_op jit(solution)/shard_map/ppermute | solution.py:161
  127.0 2.7 %shard_map.88 = bf16[256,512]{1,0:T(8,128)(2,1)} custom-call(s32[3]{0:T(128)S(1)} %pad_add_fusion.info, bf16[512,512]{1,0:T(8,128)(2,1)S(1)} %get-tuple-element.19.own, bf16[512,512]{1,0:T(8,128)(2,1)S(1)} %collective-permute-done.9.other, f32[1,1]{1,0:T(1,128)} %get-tuple-element.20.grad_square), custom_call_target="tpu_custom_call" | custom-call | tf_op jit(solution)/shard_map/pallas_call | solution.py:151
  (9 shorter events, 0.1 us)
Async XLA Ops:
  0.6 54.5 %copy-start = (bf16[512,512]{1,0:T(8,128)(2,1)S(1)}, bf16[512,512]{1,0:T(8,128)(2,1)}, u32[]{:S(2)}) copy-start(bf16[512,512]{1,0:T(8,128)(2,1)} %refs_3_) | copy-start | bytes 1572868
  2.4 48.8 %collective-permute-start.6 = (bf16[512,512]{1,0:T(8,128)(2,1)}, bf16[512,512]{1,0:T(8,128)(2,1)S(1)}, u32[]{:S(2)}, u32[]{:S(2)}) collective-permute-start(bf16[512,512]{1,0:T(8,128)(2,1)} %refs_3_), channel_id=1, source_target_pairs={{0,48},{16,32},{32,16},{48,0},{1,49},{17,33},{33,17},{49,1},{2,50}... | collective-permute-start | bytes 1572872 | tf_op jit(solution)/shard_map/ppermute | solution.py:165
  6.9 48.1 %collective-permute-start.5 = (bf16[512,512]{1,0:T(8,128)(2,1)}, bf16[512,512]{1,0:T(8,128)(2,1)S(1)}, u32[]{:S(2)}, u32[]{:S(2)}) collective-permute-start(bf16[512,512]{1,0:T(8,128)(2,1)} %refs_3_), channel_id=1, source_target_pairs={{0,16},{16,0},{1,17},{17,1},{2,18},{18,2},{3,19},{19,3},{4,20},{20... | collective-permute-start | bytes 1572872 | tf_op jit(solution)/shard_map/ppermute | solution.py:161
  9.8 45.3 %collective-permute-start.4 = (bf16[512,512]{1,0:T(8,128)(2,1)}, bf16[512,512]{1,0:T(8,128)(2,1)S(1)}, u32[]{:S(2)}, u32[]{:S(2)}) collective-permute-start(bf16[512,512]{1,0:T(8,128)(2,1)} %refs_3_), channel_id=1, source_target_pairs={{0,32},{32,0},{1,33},{33,1},{2,34},{34,2},{3,35},{35,3},{4,36},{36... | collective-permute-start | bytes 1572872 | tf_op jit(solution)/shard_map/ppermute | solution.py:161
  11.8 3.2 %collective-permute-start = (bf16[64,512]{1,0:T(8,128)(2,1)S(1)}, bf16[64,512]{1,0:T(8,128)(2,1)S(1)}, u32[]{:S(2)}, u32[]{:S(2)}) collective-permute-start(bf16[64,512]{1,0:T(8,128)(2,1)S(1)} %get-tuple-element.13), channel_id=1, source_target_pairs={{0,32},{32,0},{1,33},{33,1},{2,34},{34,2},{3,35},{35,3},{4,36},{36... | collective-permute-start | bytes 196616 | tf_op jit(solution)/shard_map/ppermute | solution.py:161
  46.5 21.9 %collective-permute-start.3 = (bf16[256,1024]{1,0:T(8,128)(2,1)S(1)}, bf16[256,1024]{1,0:T(8,128)(2,1)S(1)}, u32[]{:S(2)}, u32[]{:S(2)}) collective-permute-start(bf16[256,1024]{1,0:T(8,128)(2,1)S(1)} %all_gather.3.refs_0_), channel_id=1, source_target_pairs={{0,14},{1,15},{2,0},{3,1},{4,2},{5,3},{6,4},{7,5},{8,6},{9,7},{10,... | collective-permute-start | bytes 1572872 | tf_op jit(solution)/shard_map/ppermute | solution.py:177
  48.5 23.9 %collective-permute-start.2 = (bf16[256,1024]{1,0:T(8,128)(2,1)S(1)}, bf16[256,1024]{1,0:T(8,128)(2,1)}, u32[]{:S(2)}, u32[]{:S(2)}) collective-permute-start(bf16[256,1024]{1,0:T(8,128)(2,1)S(1)} %all_gather.3.refs_0_), channel_id=1, source_target_pairs={{0,1},{1,2},{2,3},{3,4},{4,5},{5,6},{6,7},{7,8},{8,9},{9,10},{10,1... | collective-permute-start | bytes 1572872 | tf_op jit(solution)/shard_map/ppermute | solution.py:170
  51.2 22.9 %collective-permute-start.1 = (bf16[256,1024]{1,0:T(8,128)(2,1)S(1)}, bf16[256,1024]{1,0:T(8,128)(2,1)}, u32[]{:S(2)}, u32[]{:S(2)}) collective-permute-start(bf16[256,1024]{1,0:T(8,128)(2,1)S(1)} %all_gather.3.refs_0_), channel_id=1, source_target_pairs={{0,15},{1,0},{2,1},{3,2},{4,3},{5,4},{6,5},{7,6},{8,7},{9,8},{10,9... | collective-permute-start | bytes 1572872 | tf_op jit(solution)/shard_map/ppermute | solution.py:170
  97.9 18.5 %copy-start.1 = (f32[512,512]{1,0:T(8,128)S(1)}, f32[512,512]{1,0:T(8,128)}, u32[]{:S(2)}) copy-start(f32[512,512]{1,0:T(8,128)} %state.1) | copy-start | bytes 3145732
  97.9 18.6 %copy-start.2 = (bf16[512,512]{1,0:T(8,128)(2,1)S(1)}, bf16[512,512]{1,0:T(8,128)(2,1)}, u32[]{:S(2)}) copy-start(bf16[512,512]{1,0:T(8,128)(2,1)} %stale.1) | copy-start | bytes 1572868
  98.1 8.9 %collective-permute-start.7 = (bf16[256,512]{1,0:T(8,128)(2,1)S(1)}, bf16[256,512]{1,0:T(8,128)(2,1)S(1)}, u32[]{:S(2)}, u32[]{:S(2)}) collective-permute-start(bf16[256,512]{1,0:T(8,128)(2,1)S(1)} %pad_maximum_fusion), channel_id=1, source_target_pairs={{0,0},{16,272},{256,16},{272,256},{1,1},{17,273},{257,17},{273,257... | collective-permute-start | bytes 786440 | tf_op jit(solution)/shard_map/ppermute | solution.py:182
  107.0 9.4 %collective-permute-start.8 = (bf16[256,512]{1,0:T(8,128)(2,1)S(1)}, bf16[256,512]{1,0:T(8,128)(2,1)S(1)}, u32[]{:S(2)}, u32[]{:S(2)}) collective-permute-start(bf16[256,512]{1,0:T(8,128)(2,1)S(1)} %collective-permute-done.7), channel_id=1, source_target_pairs={{0,32},{32,0},{1,33},{33,1},{2,34},{34,2},{3,35},{35,3},{4,36},{36... | collective-permute-start | bytes 786440 | tf_op jit(solution)/shard_map/ppermute | solution.py:161
  123.2 3.8 %collective-permute-start.9 = (bf16[512,512]{1,0:T(8,128)(2,1)S(1)}, bf16[512,512]{1,0:T(8,128)(2,1)S(1)}, u32[]{:S(2)}, u32[]{:S(2)}) collective-permute-start(bf16[512,512]{1,0:T(8,128)(2,1)S(1)} %get-tuple-element.19.own), channel_id=1, source_target_pairs={{0,32},{32,0},{1,33},{33,1},{2,34},{34,2},{3,35},{35,3},{4,36},{36... | collective-permute-start | bytes 1572872 | tf_op jit(solution)/shard_map/ppermute | solution.py:161

commit v3 on v2

--- a/solution.py
+++ b/solution.py
@@ -25,32 +25,34 @@
     return lax.dot_general(a, b, (contract, ((), ())), preferred_element_type=F32)
 
 
-def partial_kernel(classes, *refs):
+def total_of(value):
+    return jnp.sum(jnp.sum(value, axis=0, keepdims=True), axis=1, keepdims=True)
+
+
+def partial_kernel(classes, flip, *refs):
     features, hidden, out = refs[:classes], refs[classes:-1], refs[-1]
     rows = features[0].shape[0] // CLASSES
-    tokens = hidden[0].shape[0]
     for column in range(2):
+        first = jnp.where(flip[0] == 0, column, 1 - column) * CLASSES
         for at in range(classes):
-            total = dot(features[at][:, :tokens], hidden[2 * column][...])
-            total += dot(features[at][:, tokens:], hidden[2 * column + 1][...])
-            total = total.astype(BF16)
+            total = dot(features[at][...], hidden[column][...]).astype(BF16)
             for block in range(CLASSES):
-                out[column * CLASSES + block, at * rows : (at + 1) * rows, :] = total[
+                out[first + block, at * rows : (at + 1) * rows, :] = total[
                     block * rows : (block + 1) * rows
                 ]
 
 
-def partials(features, hidden):
+def partials(flip, features, hidden):
     classes = len(features)
     rows = features[0].shape[0] // CLASSES
     width = hidden[0].shape[1]
     return pl.pallas_call(
         functools.partial(partial_kernel, classes),
         out_shape=jax.ShapeDtypeStruct((2 * CLASSES, classes * rows, width), BF16),
-        in_specs=[VMEM] * (classes + 4),
+        in_specs=[SMEM] + [VMEM] * (classes + 2),
         out_specs=VMEM,
         compiler_params=LIMIT,
-    )(*features, *hidden)
+    )(flip, *features, *hidden)
 
 
 def newton_kernel(info, own, last, other, other_last, state, stale, new_factor, new_root, payload, grad_square, grad, matrix, turned, square):
@@ -75,7 +77,7 @@
     def _():
         new_factor[...] = BETA * state[...] + (1.0 - BETA) * dot(grad[...], grad[...], ((0,), (0,)))
 
-    grad_square[...] = jnp.sum(jnp.square(grad[...].astype(F32)), keepdims=True)
+    grad_square[...] = total_of(jnp.square(grad[...].astype(F32)))
     new_root[...] = stale[...]
 
     def turn(value):
@@ -87,7 +89,7 @@
     @pl.when(steps > 0)
     def _():
         factor = new_factor[...]
-        norm = jnp.sqrt(jnp.sum(factor * factor, keepdims=True) + NORM_EPS)
+        norm = jnp.sqrt(total_of(factor * factor) + NORM_EPS)
         matrix[...] = (factor * (1.0 / norm)).astype(BF16)
         root_scale = lax.rsqrt(jnp.sqrt(norm)).astype(BF16).astype(F32)
         turned[...] = turn(matrix[...])
@@ -134,7 +136,7 @@
 
     def finish(left, product, start):
         raw = dot(left[...], product[...])
-        total = jnp.sum(raw * raw, keepdims=True)
+        total = total_of(raw * raw)
         ratio = jnp.sqrt(grad_square[...]) / jnp.sqrt(total + NORM_EPS)
         out[...] = (raw[start : start + HALF] * ratio).astype(BF16)
 
@@ -161,10 +163,6 @@
     return lax.ppermute(value, axis, [(0, 1), (1, 0)])
 
 
-def across_chip(value):
-    return lax.ppermute(value, ("core", "y_hi"), [(i, 3 - i) for i in range(4)])
-
-
 def along_z(value, by):
     size = lax.axis_size("z")
     return lax.ppermute(value, "z", [(i, (i - by) % size) for i in range(size)])
@@ -178,7 +176,7 @@
 
 
 def to_home(value):
-    pairs = [(2 * lo + hi, 2 * hi + (hi ^ lo)) for lo in range(2) for hi in range(2)]
+    pairs = [(2 * lo + hi, 2 * hi + lo) for lo in range(2) for hi in range(2)]
     return lax.ppermute(value, ("y_lo", "y_hi"), pairs)
 
 
@@ -190,25 +188,24 @@
 def per_device(hidden, out_grad, token_counts, factor_state, stale_root, newton_steps):
     core = lax.axis_index("core")
     first = lax.rem(lax.axis_index("z"), CLASSES)
+    column = jnp.concatenate([hidden, other_of(hidden, "core")], axis=0)
+    columns = (column, other_of(column, "y_hi"))
     positions = lax.broadcasted_iota(jnp.int32, (out_grad.shape[0], 1), 0)
     kept = jnp.where(positions < token_counts[0], out_grad, jnp.zeros_like(out_grad)).T
     rows = kept.shape[0] // 2
     mine = lax.dynamic_slice_in_dim(kept, core * rows, rows, 0)
     sent = lax.dynamic_slice_in_dim(kept, (1 - core) * rows, rows, 0)
-    sent, hidden = lax.optimization_barrier((sent, hidden))
     block = jnp.concatenate([mine, other_of(sent, "core")], axis=1)
-    far = other_of(hidden, "y_hi")
-    near = other_of(hidden, "core")
-    columns = (hidden, near, far, across_chip(hidden))
     size = lax.axis_size("z")
     strided = [[at + CLASSES * i for i in range(size // CLASSES)] for at in range(CLASSES)]
     own_class = lax.all_gather(block, "z", axis=0, tiled=True, axis_index_groups=strided)
     above = along_z(own_class, 1)
     below = along_z(own_class, -1)
     across = two_away(own_class)
-    own = reduced(partials([own_class], columns))
+    flip = lax.axis_index("y_hi").astype(jnp.int32).reshape(1)
+    own = reduced(partials(flip, [own_class], columns))
     above, below, across, own = lax.optimization_barrier((above, below, across, own))
-    rest = reduced(partials([above, below, across], columns))
+    rest = reduced(partials(flip, [above, below, across], columns))
     home = to_home(jnp.concatenate([own, rest], axis=0))
     away = other_of(home, "core")
     own, last, other, other_last = home[:192], home[192:], away[:192], away[192:]

time: 130 us -> 126 us (0.969)
  the two profiles are of different devices: /device:TPU:9 before, /device:TPU:11 now
where the time goes in v3:
time: 126 us; the launch traced here: 125 us
  blocking collectives  61.9 us (49%)
  starting transfers between devices  31.5 us (25%)
  waiting for transfers between devices  14.4 us (11%)
  Pallas kernels  12.6 us (10%)
  between operations  2.14 us (2%)
  other arithmetic  1.5 us (1%)
  local copies, waits for them, and re-layouts  1.3 us (1%)
    all_gather x1, blocking collectives, per_device(): lax.all_gather(block, 'z', axis=0, tiled=True, axis_index_groups=strided)  31.4 us
    all_to_all x2, blocking collectives, reduced(): got = lax.all_to_all(parts, ('y_lo', 'x'), 0, 0, tiled=True)  30.5 us
    ppermute x5, starting transfers between devices, other_of(): return lax.ppermute(value, axis, [(0, 1), (1, 0)])  20 us
    ppermute x2, starting transfers between devices, along_z(): return lax.ppermute(value, 'z', [(i, (i - by) % size) for i in range(size)])  6.5 us
    ppermute x2, waiting for transfers between devices, along_z(): return lax.ppermute(value, 'z', [(i, (i - by) % size) for i in range(size)])  6.33 us
    pallas_call x1, Pallas kernels, roots(): pl.pallas_call(newton_kernel, out_shape=(jax.ShapeDtypeStruct((BLOCK, BLO...  6.28 us
    ppermute x1, waiting for transfers between devices, to_home(): return lax.ppermute(value, ('y_lo', 'y_hi'), pairs)  4.3 us
    ppermute x5, waiting for transfers between devices, other_of(): return lax.ppermute(value, axis, [(0, 1), (1, 0)])  3.79 us
  transfers between devices with their start and end apart: 9, of which 7 were waited for; matrix products, arithmetic and copies ran while one was open for 2% of the time, Pallas kernels for 1%

profile of v3, /device:TPU:11, one launch (start us, length us, event | category | flops | bytes accessed | tf_op | source)
XLA Modules:
  0.0 125.3 jit_solution(16078818894315169673)
XLA Ops:
  0.6 0.0 copy-start.2
  0.6 2.7 %collective-permute-start.4 = (bf16[512,512]{1,0:T(8,128)(2,1)}, bf16[512,512]{1,0:T(8,128)(2,1)S(1)}, u32[]{:S(2)}, u32[]{:S(2)}) collective-permute-start(bf16[512,512]{1,0:T(8,128)(2,1)} %param.6), channel_id=1, source_target_pairs={{0,32},{32,0},{1,33},{33,1},{2,34},{34,2},{3,35},{35,3},{4,36},{36... | collective-permute-start | bytes 1572872 | tf_op jit(solution)/shard_map/ppermute | solution.py:163
  3.4 1.1 constant_dynamic-update-slice_fusion.1
  4.4 0.6 collective-permute-done.4
  5.1 3.9 %collective-permute-start.5 = (bf16[1024,512]{1,0:T(8,128)(2,1)S(1)}, bf16[1024,512]{1,0:T(8,128)(2,1)S(1)}, u32[]{:S(2)}, u32[]{:S(2)}) collective-permute-start(bf16[1024,512]{1,0:T(8,128)(2,1)S(1)} %constant_dynamic-update-slice_fusion.refs_1_.refs_3_), channel_id=1, source_target_pairs={{0,16},{16,0},{1,17},{17,1},{2,18},{18,2},{3,19},{19,3},{4,20},{20... | collective-permute-start | bytes 3145736 | tf_op jit(solution)/shard_map/ppermute | solution.py:163
  9.7 0.0 copy-done.2
  9.7 0.1 copy.9
  9.9 2.6 %collective-permute-start = (bf16[64,512]{1,0:T(8,128)(2,1)S(1)}, bf16[64,512]{1,0:T(8,128)(2,1)S(1)}, u32[]{:S(2)}, u32[]{:S(2)}) collective-permute-start(bf16[64,512]{1,0:T(8,128)(2,1)S(1)} %get-tuple-element.20), channel_id=1, source_target_pairs={{0,32},{32,0},{1,33},{33,1},{2,34},{34,2},{3,35},{35,3},{4,36},{36... | collective-permute-start | bytes 196616 | tf_op jit(solution)/shard_map/ppermute | solution.py:163
  12.5 0.9 collective-permute-done
  13.4 31.4 %all_gather.3.refs_0_ = bf16[256,1024]{1,0:T(8,128)(2,1)S(1)} all-gather(bf16[64,1024]{1,0:T(8,128)(2,1)S(1)} %pad_maximum_fusion.1), channel_id=1, replica_groups={{0,4,8,12},{1,5,9,13},{2,6,10,14},{3,7,11,15},{16,20,24,28},{17,21,25,2..., dimensions={0}, use_global_device_ids=true | all-gather | bytes 655360 | tf_op jit(solution)/shard_map/all_gather | solution.py:201
  44.8 2.1 %collective-permute-start.3 = (bf16[256,1024]{1,0:T(8,128)(2,1)S(1)}, bf16[256,1024]{1,0:T(8,128)(2,1)S(1)}, u32[]{:S(2)}, u32[]{:S(2)}) collective-permute-start(bf16[256,1024]{1,0:T(8,128)(2,1)S(1)} %all_gather.3.refs_0_), channel_id=1, source_target_pairs={{0,14},{1,15},{2,0},{3,1},{4,2},{5,3},{6,4},{7,5},{8,6},{9,7},{10,... | collective-permute-start | bytes 1572872 | tf_op jit(solution)/shard_map/ppermute | solution.py:175
  46.9 2.6 %collective-permute-start.2 = (bf16[256,1024]{1,0:T(8,128)(2,1)S(1)}, bf16[256,1024]{1,0:T(8,128)(2,1)}, u32[]{:S(2)}, u32[]{:S(2)}) collective-permute-start(bf16[256,1024]{1,0:T(8,128)(2,1)S(1)} %all_gather.3.refs_0_), channel_id=1, source_target_pairs={{0,1},{1,2},{2,3},{3,4},{4,5},{5,6},{6,7},{7,8},{8,9},{9,10},{10,1... | collective-permute-start | bytes 1572872 | tf_op jit(solution)/shard_map/ppermute | solution.py:168
  49.5 3.9 %collective-permute-start.1 = (bf16[256,1024]{1,0:T(8,128)(2,1)S(1)}, bf16[256,1024]{1,0:T(8,128)(2,1)}, u32[]{:S(2)}, u32[]{:S(2)}) collective-permute-start(bf16[256,1024]{1,0:T(8,128)(2,1)S(1)} %all_gather.3.refs_0_), channel_id=1, source_target_pairs={{0,15},{1,0},{2,1},{3,2},{4,3},{5,4},{6,5},{7,6},{8,7},{9,8},{10,9... | collective-permute-start | bytes 1572872 | tf_op jit(solution)/shard_map/ppermute | solution.py:168
  53.4 0.0 collective-permute-done.5.refs_2_.refs_4_
  53.4 0.7 shard_map.85
  54.1 10.8 %all_to_all.10 = bf16[8,64,512]{2,1,0:T(8,128)(2,1)} all-to-all(bf16[8,64,512]{2,1,0:T(8,128)(2,1)S(1)} %shard_map.85), channel_id=1, replica_groups=mesh['y_lo'=2,'x'=4,'core'=2,'y_hi'=2,'z'=16] {'y_lo','x'}, dimensions={0} | all-to-all | bytes 1048576 | tf_op jit(solution)/shard_map/all_to_all | solution.py:184
  64.9 1.1 reduce_sum.24
  66.1 0.0 collective-permute-done.3.refs_2_
  66.1 4.7 %collective-permute-done.2.refs_1_ = bf16[256,1024]{1,0:T(8,128)(2,1)} collective-permute-done((bf16[256,1024]{1,0:T(8,128)(2,1)S(1)}, bf16[256,1024]{1,0:T(8,128)(2,1)}, u32[]{:S(2)}, u32[]{:S(2)}) %collective-permute-start.2) | collective-permute-done | bytes 524320 | tf_op jit(solution)/shard_map/ppermute | solution.py:168
  70.8 1.6 %collective-permute-done.1.refs_0_ = bf16[256,1024]{1,0:T(8,128)(2,1)} collective-permute-done((bf16[256,1024]{1,0:T(8,128)(2,1)S(1)}, bf16[256,1024]{1,0:T(8,128)(2,1)}, u32[]{:S(2)}, u32[]{:S(2)}) %collective-permute-start.1) | collective-permute-done | bytes 524320 | tf_op jit(solution)/shard_map/ppermute | solution.py:168
  72.4 3.0 %shard_map.86 = bf16[8,192,512]{2,1,0:T(8,128)(2,1)S(1)} custom-call(s32[1]{0:T(128)} %bitcast.6.flip, bf16[256,1024]{1,0:T(8,128)(2,1)} %collective-permute-done.1.refs_0_, bf16[256,1024]{1,0:T(8,128)(2,1)} %collective-permute-done.2.refs_1_, bf16[256,1024]{1,0:T(8,128)(2,1)S(1)} %collective-permute-done.3.refs_2_, ...), custom_call_target="tpu_custom_call" | custom-call | tf_op jit(solution)/shard_map/pallas_call | solution.py:49
  75.4 19.6 %all_to_all.11 = bf16[8,192,512]{2,1,0:T(8,128)(2,1)S(1)} all-to-all(bf16[8,192,512]{2,1,0:T(8,128)(2,1)S(1)} %shard_map.86), channel_id=1, replica_groups=mesh['y_lo'=2,'x'=4,'core'=2,'y_hi'=2,'z'=16] {'y_lo','x'}, dimensions={0} | all-to-all | bytes 3145728 | tf_op jit(solution)/shard_map/all_to_all | solution.py:184
  95.0 0.0 copy-start
  95.0 0.0 copy-start.1
  95.0 0.3 reduce_sum.25
  95.3 2.9 %collective-permute-start.6 = (bf16[256,512]{1,0:T(8,128)(2,1)S(1)}, bf16[256,512]{1,0:T(8,128)(2,1)S(1)}, u32[]{:S(2)}, u32[]{:S(2)}) collective-permute-start(bf16[256,512]{1,0:T(8,128)(2,1)S(1)} %pad_maximum_fusion), channel_id=1, source_target_pairs={{0,0},{16,256},{256,16},{272,272},{1,1},{17,257},{257,17},{273,273... | collective-permute-start | bytes 786440 | tf_op jit(solution)/shard_map/ppermute | solution.py:180
  98.3 4.3 %collective-permute-done.6 = bf16[256,512]{1,0:T(8,128)(2,1)S(1)} collective-permute-done((bf16[256,512]{1,0:T(8,128)(2,1)S(1)}, bf16[256,512]{1,0:T(8,128)(2,1)S(1)}, u32[]{:S(2)}, u32[]{:S(2)}) %collective-permute-start.6) | collective-permute-done | bytes 262176 | tf_op jit(solution)/shard_map/ppermute | solution.py:180
  102.6 8.9 %collective-permute-start.7 = (bf16[256,512]{1,0:T(8,128)(2,1)S(1)}, bf16[256,512]{1,0:T(8,128)(2,1)S(1)}, u32[]{:S(2)}, u32[]{:S(2)}) collective-permute-start(bf16[256,512]{1,0:T(8,128)(2,1)S(1)} %collective-permute-done.6), channel_id=1, source_target_pairs={{0,32},{32,0},{1,33},{33,1},{2,34},{34,2},{3,35},{35,3},{4,36},{36... | collective-permute-start | bytes 786440 | tf_op jit(solution)/shard_map/ppermute | solution.py:163
  112.1 0.1 pad_add_fusion.info
  112.2 0.4 collective-permute-done.7
  112.6 0.0 copy-done
  112.6 0.0 copy-done.1
  112.6 6.3 %shard_map.87 = (f32[512,512]{1,0:T(8,128)}, bf16[512,512]{1,0:T(8,128)(2,1)}, bf16[512,512]{1,0:T(8,128)(2,1)S(1)}, f32[1,1]{1,0:T(1,128)}) custom-call(s32[3]{0:T(128)S(1)} %pad_add_fusion.info, bf16[192,512]{1,0:T(8,128)(2,1)S(1)} %slice.16.own, bf16[64,512]{1,0:T(8,128)(2,1)S(1)} %slice.17.last, bf16[192,512]{1,0:T(8,128)(2,1)S(1)} %slice.18.other, ...), custom_call_target="tpu_custom_call" | custom-call | tf_op jit(solution)/shard_map/pallas_call | solution.py:119
  118.9 1.9 %collective-permute-start.8 = (bf16[512,512]{1,0:T(8,128)(2,1)S(1)}, bf16[512,512]{1,0:T(8,128)(2,1)S(1)}, u32[]{:S(2)}, u32[]{:S(2)}) collective-permute-start(bf16[512,512]{1,0:T(8,128)(2,1)S(1)} %get-tuple-element.15.own), channel_id=1, source_target_pairs={{0,32},{32,0},{1,33},{33,1},{2,34},{34,2},{3,35},{35,3},{4,36},{36... | collective-permute-start | bytes 1572872 | tf_op jit(solution)/shard_map/ppermute | solution.py:163
  120.8 1.9 %collective-permute-done.8.other = bf16[512,512]{1,0:T(8,128)(2,1)S(1)} collective-permute-done((bf16[512,512]{1,0:T(8,128)(2,1)S(1)}, bf16[512,512]{1,0:T(8,128)(2,1)S(1)}, u32[]{:S(2)}, u32[]{:S(2)}) %collective-permute-start.8) | collective-permute-done | bytes 524320 | tf_op jit(solution)/shard_map/ppermute | solution.py:163
  122.7 2.6 %shard_map.88 = bf16[256,512]{1,0:T(8,128)(2,1)} custom-call(s32[3]{0:T(128)S(1)} %pad_add_fusion.info, bf16[512,512]{1,0:T(8,128)(2,1)S(1)} %get-tuple-element.15.own, bf16[512,512]{1,0:T(8,128)(2,1)S(1)} %collective-permute-done.8.other, f32[1,1]{1,0:T(1,128)} %get-tuple-element.16.grad_square), custom_call_target="tpu_custom_call" | custom-call | tf_op jit(solution)/shard_map/pallas_call | solution.py:153
  (10 shorter events, 0.1 us)
Async XLA Ops:
  0.6 9.1 %copy-start.2 = (bf16[512,128]{1,0:T(8,128)(2,1)S(1)}, bf16[512,128]{1,0:T(8,128)(2,1)}, u32[]{:S(2)}) copy-start(bf16[512,128]{1,0:T(8,128)(2,1)} %param.7) | copy-start | bytes 393220
  0.6 4.4 %collective-permute-start.4 = (bf16[512,512]{1,0:T(8,128)(2,1)}, bf16[512,512]{1,0:T(8,128)(2,1)S(1)}, u32[]{:S(2)}, u32[]{:S(2)}) collective-permute-start(bf16[512,512]{1,0:T(8,128)(2,1)} %param.6), channel_id=1, source_target_pairs={{0,32},{32,0},{1,33},{33,1},{2,34},{34,2},{3,35},{35,3},{4,36},{36... | collective-permute-start | bytes 1572872 | tf_op jit(solution)/shard_map/ppermute | solution.py:163
  5.1 48.3 %collective-permute-start.5 = (bf16[1024,512]{1,0:T(8,128)(2,1)S(1)}, bf16[1024,512]{1,0:T(8,128)(2,1)S(1)}, u32[]{:S(2)}, u32[]{:S(2)}) collective-permute-start(bf16[1024,512]{1,0:T(8,128)(2,1)S(1)} %constant_dynamic-update-slice_fusion.refs_1_.refs_3_), channel_id=1, source_target_pairs={{0,16},{16,0},{1,17},{17,1},{2,18},{18,2},{3,19},{19,3},{4,20},{20... | collective-permute-start | bytes 3145736 | tf_op jit(solution)/shard_map/ppermute | solution.py:163
  9.9 3.5 %collective-permute-start = (bf16[64,512]{1,0:T(8,128)(2,1)S(1)}, bf16[64,512]{1,0:T(8,128)(2,1)S(1)}, u32[]{:S(2)}, u32[]{:S(2)}) collective-permute-start(bf16[64,512]{1,0:T(8,128)(2,1)S(1)} %get-tuple-element.20), channel_id=1, source_target_pairs={{0,32},{32,0},{1,33},{33,1},{2,34},{34,2},{3,35},{35,3},{4,36},{36... | collective-permute-start | bytes 196616 | tf_op jit(solution)/shard_map/ppermute | solution.py:163
  44.8 21.3 %collective-permute-start.3 = (bf16[256,1024]{1,0:T(8,128)(2,1)S(1)}, bf16[256,1024]{1,0:T(8,128)(2,1)S(1)}, u32[]{:S(2)}, u32[]{:S(2)}) collective-permute-start(bf16[256,1024]{1,0:T(8,128)(2,1)S(1)} %all_gather.3.refs_0_), channel_id=1, source_target_pairs={{0,14},{1,15},{2,0},{3,1},{4,2},{5,3},{6,4},{7,5},{8,6},{9,7},{10,... | collective-permute-start | bytes 1572872 | tf_op jit(solution)/shard_map/ppermute | solution.py:175
  46.9 23.9 %collective-permute-start.2 = (bf16[256,1024]{1,0:T(8,128)(2,1)S(1)}, bf16[256,1024]{1,0:T(8,128)(2,1)}, u32[]{:S(2)}, u32[]{:S(2)}) collective-permute-start(bf16[256,1024]{1,0:T(8,128)(2,1)S(1)} %all_gather.3.refs_0_), channel_id=1, source_target_pairs={{0,1},{1,2},{2,3},{3,4},{4,5},{5,6},{6,7},{7,8},{8,9},{9,10},{10,1... | collective-permute-start | bytes 1572872 | tf_op jit(solution)/shard_map/ppermute | solution.py:168
  49.5 22.9 %collective-permute-start.1 = (bf16[256,1024]{1,0:T(8,128)(2,1)S(1)}, bf16[256,1024]{1,0:T(8,128)(2,1)}, u32[]{:S(2)}, u32[]{:S(2)}) collective-permute-start(bf16[256,1024]{1,0:T(8,128)(2,1)S(1)} %all_gather.3.refs_0_), channel_id=1, source_target_pairs={{0,15},{1,0},{2,1},{3,2},{4,3},{5,4},{6,5},{7,6},{8,7},{9,8},{10,9... | collective-permute-start | bytes 1572872 | tf_op jit(solution)/shard_map/ppermute | solution.py:168
  95.0 17.6 %copy-start = (f32[512,512]{1,0:T(8,128)S(1)}, f32[512,512]{1,0:T(8,128)}, u32[]{:S(2)}) copy-start(f32[512,512]{1,0:T(8,128)} %state.1) | copy-start | bytes 3145732
  95.0 17.6 %copy-start.1 = (bf16[512,512]{1,0:T(8,128)(2,1)S(1)}, bf16[512,512]{1,0:T(8,128)(2,1)}, u32[]{:S(2)}) copy-start(bf16[512,512]{1,0:T(8,128)(2,1)} %stale.1) | copy-start | bytes 1572868
  95.3 7.2 %collective-permute-start.6 = (bf16[256,512]{1,0:T(8,128)(2,1)S(1)}, bf16[256,512]{1,0:T(8,128)(2,1)S(1)}, u32[]{:S(2)}, u32[]{:S(2)}) collective-permute-start(bf16[256,512]{1,0:T(8,128)(2,1)S(1)} %pad_maximum_fusion), channel_id=1, source_target_pairs={{0,0},{16,256},{256,16},{272,272},{1,1},{17,257},{257,17},{273,273... | collective-permute-start | bytes 786440 | tf_op jit(solution)/shard_map/ppermute | solution.py:180
  102.6 10.0 %collective-permute-start.7 = (bf16[256,512]{1,0:T(8,128)(2,1)S(1)}, bf16[256,512]{1,0:T(8,128)(2,1)S(1)}, u32[]{:S(2)}, u32[]{:S(2)}) collective-permute-start(bf16[256,512]{1,0:T(8,128)(2,1)S(1)} %collective-permute-done.6), channel_id=1, source_target_pairs={{0,32},{32,0},{1,33},{33,1},{2,34},{34,2},{3,35},{35,3},{4,36},{36... | collective-permute-start | bytes 786440 | tf_op jit(solution)/shard_map/ppermute | solution.py:163
  118.9 3.8 %collective-permute-start.8 = (bf16[512,512]{1,0:T(8,128)(2,1)S(1)}, bf16[512,512]{1,0:T(8,128)(2,1)S(1)}, u32[]{:S(2)}, u32[]{:S(2)}) collective-permute-start(bf16[512,512]{1,0:T(8,128)(2,1)S(1)} %get-tuple-element.15.own), channel_id=1, source_target_pairs={{0,32},{32,0},{1,33},{33,1},{2,34},{34,2},{3,35},{35,3},{4,36},{36... | collective-permute-start | bytes 1572872 | tf_op jit(solution)/shard_map/ppermute | solution.py:163

commit v4 on v3

--- a/solution.py
+++ b/solution.py
@@ -15,7 +15,7 @@
 CLASSES = 4
 VMEM = pl.BlockSpec(memory_space=pltpu.VMEM)
 SMEM = pl.BlockSpec(memory_space=pltpu.SMEM)
-LIMIT = pltpu.CompilerParams(vmem_limit_bytes=48 * 2**20)
+LIMIT = pltpu.CompilerParams(vmem_limit_bytes=16 * 2**20)
 AXES = ("y_lo", "x", "core", "y_hi", "z")
 BF16 = jnp.bfloat16
 F32 = jnp.float32
@@ -29,11 +29,12 @@
     return jnp.sum(jnp.sum(value, axis=0, keepdims=True), axis=1, keepdims=True)
 
 
-def partial_kernel(classes, flip, *refs):
+def partial_kernel(classes, *refs):
     features, hidden, out = refs[:classes], refs[classes:-1], refs[-1]
     rows = features[0].shape[0] // CLASSES
+    own = lax.axis_index("y_hi")
     for column in range(2):
-        first = jnp.where(flip[0] == 0, column, 1 - column) * CLASSES
+        first = (own + column - 2 * own * column) * CLASSES
         for at in range(classes):
             total = dot(features[at][...], hidden[column][...]).astype(BF16)
             for block in range(CLASSES):
@@ -42,32 +43,28 @@
                 ]
 
 
-def partials(flip, features, hidden):
+def partials(features, hidden):
     classes = len(features)
     rows = features[0].shape[0] // CLASSES
     width = hidden[0].shape[1]
     return pl.pallas_call(
         functools.partial(partial_kernel, classes),
         out_shape=jax.ShapeDtypeStruct((2 * CLASSES, classes * rows, width), BF16),
-        in_specs=[SMEM] + [VMEM] * (classes + 2),
+        in_specs=[VMEM] * (classes + 2),
         out_specs=VMEM,
         compiler_params=LIMIT,
-    )(flip, *features, *hidden)
-
-
-def newton_kernel(info, own, last, other, other_last, state, stale, new_factor, new_root, payload, grad_square, grad, matrix, turned, square):
-    side, first, steps = info[0], info[1], info[2]
+    )(*features, *hidden)
+
+
+def newton_kernel(count, own, other, state, stale, new_factor, new_root, payload, grad_square, grad, matrix, turned, square):
+    side, first, steps = lax.axis_index("core"), lax.rem(lax.axis_index("z"), CLASSES), count[0, 0]
     rows = HALF // CLASSES
     for at, shift in enumerate((0, 1, 3, 2)):
         start = lax.rem(first + shift, CLASSES) * (2 * rows)
         mine = pl.multiple_of(start + side * rows, rows)
         theirs = pl.multiple_of(start + (1 - side) * rows, rows)
-        if at < CLASSES - 1:
-            grad[pl.ds(mine, rows), :] = own[at * rows : (at + 1) * rows, :]
-            grad[pl.ds(theirs, rows), :] = other[at * rows : (at + 1) * rows, :]
-        else:
-            grad[pl.ds(mine, rows), :] = last[...]
-            grad[pl.ds(theirs, rows), :] = other_last[...]
+        grad[pl.ds(mine, rows), :] = own[at * rows : (at + 1) * rows, :]
+        grad[pl.ds(theirs, rows), :] = other[at * rows : (at + 1) * rows, :]
 
     @pl.when(side == 0)
     def _():
@@ -77,7 +74,7 @@
     def _():
         new_factor[...] = BETA * state[...] + (1.0 - BETA) * dot(grad[...], grad[...], ((0,), (0,)))
 
-    grad_square[...] = total_of(jnp.square(grad[...].astype(F32)))
+    grad_square[...] = jnp.broadcast_to(total_of(jnp.square(grad[...].astype(F32))), grad_square.shape)
     new_root[...] = stale[...]
 
     def turn(value):
@@ -114,7 +111,7 @@
         payload[...] = dot(grad[...], new_root[...]).astype(BF16)
 
 
-def roots(info, own, last, other, other_last, state, stale):
+def roots(count, own, other, state, stale):
     full = jax.ShapeDtypeStruct((BLOCK, BLOCK), BF16)
     return pl.pallas_call(
         newton_kernel,
@@ -122,22 +119,22 @@
             jax.ShapeDtypeStruct((BLOCK, BLOCK), F32),
             full,
             full,
-            jax.ShapeDtypeStruct((1, 1), F32),
+            jax.ShapeDtypeStruct((8, 128), F32),
         ),
-        in_specs=[SMEM] + [VMEM] * 6,
+        in_specs=[SMEM] + [VMEM] * 4,
         out_specs=[VMEM] * 4,
         scratch_shapes=[pltpu.VMEM((BLOCK, BLOCK), BF16)] * 4,
         compiler_params=LIMIT,
-    )(info, own, last, other, other_last, state, stale)
-
-
-def update_kernel(info, own, other, grad_square, out):
-    side = info[0]
+    )(count, own, other, state, stale)
+
+
+def update_kernel(own, other, grad_square, out):
+    side = lax.axis_index("core")
 
     def finish(left, product, start):
         raw = dot(left[...], product[...])
         total = total_of(raw * raw)
-        ratio = jnp.sqrt(grad_square[...]) / jnp.sqrt(total + NORM_EPS)
+        ratio = jnp.sqrt(grad_square[:1, :1]) / jnp.sqrt(total + NORM_EPS)
         out[...] = (raw[start : start + HALF] * ratio).astype(BF16)
 
     @pl.when(side == 0)
@@ -149,14 +146,14 @@
         finish(other, own, HALF)
 
 
-def grafted(info, own, other, grad_square):
+def grafted(own, other, grad_square):
     return pl.pallas_call(
         update_kernel,
         out_shape=jax.ShapeDtypeStruct((HALF, BLOCK), BF16),
-        in_specs=[SMEM] + [VMEM] * 3,
+        in_specs=[VMEM] * 3,
         out_specs=VMEM,
         compiler_params=LIMIT,
-    )(info, own, other, grad_square)
+    )(own, other, grad_square)
 
 
 def other_of(value, axis):
@@ -187,7 +184,6 @@
 
 def per_device(hidden, out_grad, token_counts, factor_state, stale_root, newton_steps):
     core = lax.axis_index("core")
-    first = lax.rem(lax.axis_index("z"), CLASSES)
     column = jnp.concatenate([hidden, other_of(hidden, "core")], axis=0)
     columns = (column, other_of(column, "y_hi"))
     positions = lax.broadcasted_iota(jnp.int32, (out_grad.shape[0], 1), 0)
@@ -202,18 +198,13 @@
     above = along_z(own_class, 1)
     below = along_z(own_class, -1)
     across = two_away(own_class)
-    flip = lax.axis_index("y_hi").astype(jnp.int32).reshape(1)
-    own = reduced(partials(flip, [own_class], columns))
+    own = reduced(partials([own_class], columns))
     above, below, across, own = lax.optimization_barrier((above, below, across, own))
-    rest = reduced(partials(flip, [above, below, across], columns))
-    home = to_home(jnp.concatenate([own, rest], axis=0))
-    away = other_of(home, "core")
-    own, last, other, other_last = home[:192], home[192:], away[:192], away[192:]
-    info = jnp.stack([core, first, newton_steps[0, 0]]).astype(jnp.int32)
-    new_factor, new_root, payload, grad_square = roots(
-        info, own, last, other, other_last, factor_state, stale_root
-    )
-    update = grafted(info, payload, other_of(payload, "core"), grad_square)
+    rest = reduced(partials([above, below, across], columns))
+    own = to_home(jnp.concatenate([own, rest], axis=0))
+    other = other_of(own, "core")
+    new_factor, new_root, payload, grad_square = roots(newton_steps, own, other, factor_state, stale_root)
+    update = grafted(payload, other_of(payload, "core"), grad_square)
     return (update, new_factor, new_root)
 
 

time: 126 us -> 125 us (level)
  the two profiles are of different devices: /device:TPU:11 before, /device:TPU:105 now
where the time goes in v4:
time: 125 us
  blocking collectives  64.8 us (52%)
  starting transfers between devices  27.9 us (22%)
  waiting for transfers between devices  16.4 us (13%)
  Pallas kernels  10.7 us (9%)
  between operations  2.12 us (2%)
  other arithmetic  1.42 us (1%)
  local copies, waits for them, and re-layouts  1.26 us (1%)
    all_to_all x2, blocking collectives, reduced(): got = lax.all_to_all(parts, ('y_lo', 'x'), 0, 0, tiled=True)  37.1 us
    all_gather x1, blocking collectives, per_device(): lax.all_gather(block, 'z', axis=0, tiled=True, axis_index_groups=strided)  27.7 us
    ppermute x5, starting transfers between devices, other_of(): return lax.ppermute(value, axis, [(0, 1), (1, 0)])  14.7 us
    ppermute x2, starting transfers between devices, along_z(): return lax.ppermute(value, 'z', [(i, (i - by) % size) for i in range(size)])  7.08 us
    ppermute x1, waiting for transfers between devices, two_away(): return lax.ppermute(value, ('core', 'z'), pairs)  6.42 us
    ppermute x1, waiting for transfers between devices, to_home(): return lax.ppermute(value, ('y_lo', 'y_hi'), pairs)  6.05 us
    pallas_call x1, Pallas kernels, roots(): pl.pallas_call(newton_kernel, out_shape=(jax.ShapeDtypeStruct((BLOCK, BLO...  5.74 us
    ppermute x5, waiting for transfers between devices, other_of(): return lax.ppermute(value, axis, [(0, 1), (1, 0)])  3.9 us
  transfers between devices with their start and end apart: 9, of which 6 were waited for; matrix products, arithmetic and copies ran while one was open for 2% of the time, Pallas kernels for 1%

profile of v4, /device:TPU:105, one launch (start us, length us, event | category | flops | bytes accessed | tf_op | source)
XLA Modules:
  0.0 124.6 jit_solution(14736884584074704766)
XLA Ops:
  0.6 0.0 copy-start.2
  0.6 2.7 %collective-permute-start.4 = (bf16[512,512]{1,0:T(8,128)(2,1)}, bf16[512,512]{1,0:T(8,128)(2,1)S(1)}, u32[]{:S(2)}, u32[]{:S(2)}) collective-permute-start(bf16[512,512]{1,0:T(8,128)(2,1)} %param.6), channel_id=1, source_target_pairs={{0,32},{32,0},{1,33},{33,1},{2,34},{34,2},{3,35},{35,3},{4,36},{36... | collective-permute-start | bytes 1572872 | tf_op jit(solution)/shard_map/ppermute | solution.py:160
  3.4 1.1 constant_dynamic-update-slice_fusion.1
  4.4 0.6 collective-permute-done.4
  5.1 3.9 %collective-permute-start.5 = (bf16[1024,512]{1,0:T(8,128)(2,1)S(1)}, bf16[1024,512]{1,0:T(8,128)(2,1)S(1)}, u32[]{:S(2)}, u32[]{:S(2)}) collective-permute-start(bf16[1024,512]{1,0:T(8,128)(2,1)S(1)} %constant_dynamic-update-slice_fusion.refs_1_.refs_3_), channel_id=1, source_target_pairs={{0,16},{16,0},{1,17},{17,1},{2,18},{18,2},{3,19},{19,3},{4,20},{20... | collective-permute-start | bytes 3145736 | tf_op jit(solution)/shard_map/ppermute | solution.py:160
  9.1 0.0 copy-done.2
  9.1 0.1 copy.9
  9.9 2.6 %collective-permute-start = (bf16[64,512]{1,0:T(8,128)(2,1)S(1)}, bf16[64,512]{1,0:T(8,128)(2,1)S(1)}, u32[]{:S(2)}, u32[]{:S(2)}) collective-permute-start(bf16[64,512]{1,0:T(8,128)(2,1)S(1)} %get-tuple-element.20), channel_id=1, source_target_pairs={{0,32},{32,0},{1,33},{33,1},{2,34},{34,2},{3,35},{35,3},{4,36},{36... | collective-permute-start | bytes 196616 | tf_op jit(solution)/shard_map/ppermute | solution.py:160
  12.5 0.9 collective-permute-done
  13.4 27.7 %all_gather.3.refs_0_ = bf16[256,1024]{1,0:T(8,128)(2,1)S(1)} all-gather(bf16[64,1024]{1,0:T(8,128)(2,1)S(1)} %pad_maximum_fusion.1), channel_id=1, replica_groups={{0,4,8,12},{1,5,9,13},{2,6,10,14},{3,7,11,15},{16,20,24,28},{17,21,25,2..., dimensions={0}, use_global_device_ids=true | all-gather | bytes 655360 | tf_op jit(solution)/shard_map/all_gather | solution.py:197
  41.1 2.6 %collective-permute-start.1 = (bf16[256,1024]{1,0:T(8,128)(2,1)S(1)}, bf16[256,1024]{1,0:T(8,128)(2,1)S(1)}, u32[]{:S(2)}, u32[]{:S(2)}) collective-permute-start(bf16[256,1024]{1,0:T(8,128)(2,1)S(1)} %all_gather.3.refs_0_), channel_id=1, source_target_pairs={{0,15},{1,0},{2,1},{3,2},{4,3},{5,4},{6,5},{7,6},{8,7},{9,8},{10,9... | collective-permute-start | bytes 1572872 | tf_op jit(solution)/shard_map/ppermute | solution.py:165
  43.7 4.4 %collective-permute-start.2 = (bf16[256,1024]{1,0:T(8,128)(2,1)S(1)}, bf16[256,1024]{1,0:T(8,128)(2,1)}, u32[]{:S(2)}, u32[]{:S(2)}) collective-permute-start(bf16[256,1024]{1,0:T(8,128)(2,1)S(1)} %all_gather.3.refs_0_), channel_id=1, source_target_pairs={{0,1},{1,2},{2,3},{3,4},{4,5},{5,6},{6,7},{7,8},{8,9},{9,10},{10,1... | collective-permute-start | bytes 1572872 | tf_op jit(solution)/shard_map/ppermute | solution.py:165
  48.2 3.1 %collective-permute-start.3 = (bf16[256,1024]{1,0:T(8,128)(2,1)S(1)}, bf16[256,1024]{1,0:T(8,128)(2,1)}, u32[]{:S(2)}, u32[]{:S(2)}) collective-permute-start(bf16[256,1024]{1,0:T(8,128)(2,1)S(1)} %all_gather.3.refs_0_), channel_id=1, source_target_pairs={{0,14},{1,15},{2,0},{3,1},{4,2},{5,3},{6,4},{7,5},{8,6},{9,7},{10,... | collective-permute-start | bytes 1572872 | tf_op jit(solution)/shard_map/ppermute | solution.py:172
  51.3 0.0 collective-permute-done.5.refs_2_.refs_4_
  51.3 0.7 shard_map.85
  52.0 11.8 %all_to_all.10 = bf16[8,64,512]{2,1,0:T(8,128)(2,1)} all-to-all(bf16[8,64,512]{2,1,0:T(8,128)(2,1)S(1)} %shard_map.85), channel_id=1, replica_groups=mesh['y_lo'=2,'x'=4,'core'=2,'y_hi'=2,'z'=16] {'y_lo','x'}, dimensions={0} | all-to-all | bytes 1048576 | tf_op jit(solution)/shard_map/all_to_all | solution.py:181
  63.8 1.1 reduce_sum.24
  64.9 0.0 collective-permute-done.1.refs_0_
  64.9 0.0 collective-permute-done.2.refs_1_
  64.9 6.4 %collective-permute-done.3.refs_2_ = bf16[256,1024]{1,0:T(8,128)(2,1)} collective-permute-done((bf16[256,1024]{1,0:T(8,128)(2,1)S(1)}, bf16[256,1024]{1,0:T(8,128)(2,1)}, u32[]{:S(2)}, u32[]{:S(2)}) %collective-permute-start.3) | collective-permute-done | bytes 524320 | tf_op jit(solution)/shard_map/ppermute | solution.py:172
  71.3 3.0 %shard_map.86 = bf16[8,192,512]{2,1,0:T(8,128)(2,1)S(1)} custom-call(bf16[256,1024]{1,0:T(8,128)(2,1)S(1)} %collective-permute-done.1.refs_0_, bf16[256,1024]{1,0:T(8,128)(2,1)} %collective-permute-done.2.refs_1_, bf16[256,1024]{1,0:T(8,128)(2,1)} %collective-permute-done.3.refs_2_, bf16[1024,512]{1,0:T(8,128)(2,1)S(1)} %constant_dynamic-update-slice_fusion.refs_1_.refs_3_, ...), custom_call_target="tpu_custom_call" | custom-call | tf_op jit(solution)/shard_map/pallas_call | solution.py:50
  74.3 25.3 %all_to_all.11 = bf16[8,192,512]{2,1,0:T(8,128)(2,1)S(1)} all-to-all(bf16[8,192,512]{2,1,0:T(8,128)(2,1)S(1)} %shard_map.86), channel_id=1, replica_groups=mesh['y_lo'=2,'x'=4,'core'=2,'y_hi'=2,'z'=16] {'y_lo','x'}, dimensions={0} | all-to-all | bytes 3145728 | tf_op jit(solution)/shard_map/all_to_all | solution.py:181
  99.6 0.0 copy-start
  99.6 0.0 copy-start.1
  99.6 0.3 reduce_sum.25
  99.9 3.0 %collective-permute-start.6 = (bf16[256,512]{1,0:T(8,128)(2,1)S(1)}, bf16[256,512]{1,0:T(8,128)(2,1)S(1)}, u32[]{:S(2)}, u32[]{:S(2)}) collective-permute-start(bf16[256,512]{1,0:T(8,128)(2,1)S(1)} %pad_maximum_fusion), channel_id=1, source_target_pairs={{0,0},{16,256},{256,16},{272,272},{1,1},{17,257},{257,17},{273,273... | collective-permute-start | bytes 786440 | tf_op jit(solution)/shard_map/ppermute | solution.py:177
  102.9 6.0 %collective-permute-done.6.own = bf16[256,512]{1,0:T(8,128)(2,1)S(1)} collective-permute-done((bf16[256,512]{1,0:T(8,128)(2,1)S(1)}, bf16[256,512]{1,0:T(8,128)(2,1)S(1)}, u32[]{:S(2)}, u32[]{:S(2)}) %collective-permute-start.6) | collective-permute-done | bytes 262176 | tf_op jit(solution)/shard_map/ppermute | solution.py:177
  109.0 3.6 %collective-permute-start.7 = (bf16[256,512]{1,0:T(8,128)(2,1)S(1)}, bf16[256,512]{1,0:T(8,128)(2,1)S(1)}, u32[]{:S(2)}, u32[]{:S(2)}) collective-permute-start(bf16[256,512]{1,0:T(8,128)(2,1)S(1)} %collective-permute-done.6.own), channel_id=1, source_target_pairs={{0,32},{32,0},{1,33},{33,1},{2,34},{34,2},{3,35},{35,3},{4,36},{36... | collective-permute-start | bytes 786440 | tf_op jit(solution)/shard_map/ppermute | solution.py:160
  113.2 0.5 collective-permute-done.7.other
  113.7 0.0 copy-done
  113.7 0.0 copy-done.1
  113.7 5.7 %shard_map.87 = (f32[512,512]{1,0:T(8,128)}, bf16[512,512]{1,0:T(8,128)(2,1)}, bf16[512,512]{1,0:T(8,128)(2,1)S(1)}, f32[8,128]{1,0:T(8,128)S(1)}) custom-call(s32[1,1]{1,0:T(1,128)S(6)} %copy.12.count, bf16[256,512]{1,0:T(8,128)(2,1)S(1)} %collective-permute-done.6.own, bf16[256,512]{1,0:T(8,128)(2,1)S(1)} %collective-permute-done.7.other, ...), custom_call_target="tpu_custom_call" | custom-call | tf_op jit(solution)/shard_map/pallas_call | solution.py:116
  119.4 1.9 %collective-permute-start.8 = (bf16[512,512]{1,0:T(8,128)(2,1)S(1)}, bf16[512,512]{1,0:T(8,128)(2,1)S(1)}, u32[]{:S(2)}, u32[]{:S(2)}) collective-permute-start(bf16[512,512]{1,0:T(8,128)(2,1)S(1)} %get-tuple-element.15.own), channel_id=1, source_target_pairs={{0,32},{32,0},{1,33},{33,1},{2,34},{34,2},{3,35},{35,3},{4,36},{36... | collective-permute-start | bytes 1572872 | tf_op jit(solution)/shard_map/ppermute | solution.py:160
  121.4 1.9 %collective-permute-done.8.other = bf16[512,512]{1,0:T(8,128)(2,1)S(1)} collective-permute-done((bf16[512,512]{1,0:T(8,128)(2,1)S(1)}, bf16[512,512]{1,0:T(8,128)(2,1)S(1)}, u32[]{:S(2)}, u32[]{:S(2)}) %collective-permute-start.8) | collective-permute-done | bytes 524320 | tf_op jit(solution)/shard_map/ppermute | solution.py:160
  123.2 1.3 %shard_map.88 = bf16[256,512]{1,0:T(8,128)(2,1)} custom-call(bf16[512,512]{1,0:T(8,128)(2,1)S(1)} %get-tuple-element.15.own, bf16[512,512]{1,0:T(8,128)(2,1)S(1)} %collective-permute-done.8.other, f32[8,128]{1,0:T(8,128)S(1)} %get-tuple-element.16.grad_square), custom_call_target="tpu_custom_call" | custom-call | tf_op jit(solution)/shard_map/pallas_call | solution.py:150
  (6 shorter events, 0.1 us)
Async XLA Ops:
  0.6 8.4 %copy-start.2 = (bf16[512,128]{1,0:T(8,128)(2,1)S(1)}, bf16[512,128]{1,0:T(8,128)(2,1)}, u32[]{:S(2)}) copy-start(bf16[512,128]{1,0:T(8,128)(2,1)} %param.7) | copy-start | bytes 393220
  0.6 4.4 %collective-permute-start.4 = (bf16[512,512]{1,0:T(8,128)(2,1)}, bf16[512,512]{1,0:T(8,128)(2,1)S(1)}, u32[]{:S(2)}, u32[]{:S(2)}) collective-permute-start(bf16[512,512]{1,0:T(8,128)(2,1)} %param.6), channel_id=1, source_target_pairs={{0,32},{32,0},{1,33},{33,1},{2,34},{34,2},{3,35},{35,3},{4,36},{36... | collective-permute-start | bytes 1572872 | tf_op jit(solution)/shard_map/ppermute | solution.py:160
  5.1 46.1 %collective-permute-start.5 = (bf16[1024,512]{1,0:T(8,128)(2,1)S(1)}, bf16[1024,512]{1,0:T(8,128)(2,1)S(1)}, u32[]{:S(2)}, u32[]{:S(2)}) collective-permute-start(bf16[1024,512]{1,0:T(8,128)(2,1)S(1)} %constant_dynamic-update-slice_fusion.refs_1_.refs_3_), channel_id=1, source_target_pairs={{0,16},{16,0},{1,17},{17,1},{2,18},{18,2},{3,19},{19,3},{4,20},{20... | collective-permute-start | bytes 3145736 | tf_op jit(solution)/shard_map/ppermute | solution.py:160
  9.9 3.5 %collective-permute-start = (bf16[64,512]{1,0:T(8,128)(2,1)S(1)}, bf16[64,512]{1,0:T(8,128)(2,1)S(1)}, u32[]{:S(2)}, u32[]{:S(2)}) collective-permute-start(bf16[64,512]{1,0:T(8,128)(2,1)S(1)} %get-tuple-element.20), channel_id=1, source_target_pairs={{0,32},{32,0},{1,33},{33,1},{2,34},{34,2},{3,35},{35,3},{4,36},{36... | collective-permute-start | bytes 196616 | tf_op jit(solution)/shard_map/ppermute | solution.py:160
  41.1 23.8 %collective-permute-start.1 = (bf16[256,1024]{1,0:T(8,128)(2,1)S(1)}, bf16[256,1024]{1,0:T(8,128)(2,1)S(1)}, u32[]{:S(2)}, u32[]{:S(2)}) collective-permute-start(bf16[256,1024]{1,0:T(8,128)(2,1)S(1)} %all_gather.3.refs_0_), channel_id=1, source_target_pairs={{0,15},{1,0},{2,1},{3,2},{4,3},{5,4},{6,5},{7,6},{8,7},{9,8},{10,9... | collective-permute-start | bytes 1572872 | tf_op jit(solution)/shard_map/ppermute | solution.py:165
  43.7 21.2 %collective-permute-start.2 = (bf16[256,1024]{1,0:T(8,128)(2,1)S(1)}, bf16[256,1024]{1,0:T(8,128)(2,1)}, u32[]{:S(2)}, u32[]{:S(2)}) collective-permute-start(bf16[256,1024]{1,0:T(8,128)(2,1)S(1)} %all_gather.3.refs_0_), channel_id=1, source_target_pairs={{0,1},{1,2},{2,3},{3,4},{4,5},{5,6},{6,7},{7,8},{8,9},{9,10},{10,1... | collective-permute-start | bytes 1572872 | tf_op jit(solution)/shard_map/ppermute | solution.py:165
  48.2 23.2 %collective-permute-start.3 = (bf16[256,1024]{1,0:T(8,128)(2,1)S(1)}, bf16[256,1024]{1,0:T(8,128)(2,1)}, u32[]{:S(2)}, u32[]{:S(2)}) collective-permute-start(bf16[256,1024]{1,0:T(8,128)(2,1)S(1)} %all_gather.3.refs_0_), channel_id=1, source_target_pairs={{0,14},{1,15},{2,0},{3,1},{4,2},{5,3},{6,4},{7,5},{8,6},{9,7},{10,... | collective-permute-start | bytes 1572872 | tf_op jit(solution)/shard_map/ppermute | solution.py:172
  99.6 14.1 %copy-start = (f32[512,512]{1,0:T(8,128)S(1)}, f32[512,512]{1,0:T(8,128)}, u32[]{:S(2)}) copy-start(f32[512,512]{1,0:T(8,128)} %state.1) | copy-start | bytes 3145732
  99.6 14.1 %copy-start.1 = (bf16[512,512]{1,0:T(8,128)(2,1)S(1)}, bf16[512,512]{1,0:T(8,128)(2,1)}, u32[]{:S(2)}) copy-start(bf16[512,512]{1,0:T(8,128)(2,1)} %stale.1) | copy-start | bytes 1572868
  99.9 9.1 %collective-permute-start.6 = (bf16[256,512]{1,0:T(8,128)(2,1)S(1)}, bf16[256,512]{1,0:T(8,128)(2,1)S(1)}, u32[]{:S(2)}, u32[]{:S(2)}) collective-permute-start(bf16[256,512]{1,0:T(8,128)(2,1)S(1)} %pad_maximum_fusion), channel_id=1, source_target_pairs={{0,0},{16,256},{256,16},{272,272},{1,1},{17,257},{257,17},{273,273... | collective-permute-start | bytes 786440 | tf_op jit(solution)/shard_map/ppermute | solution.py:177
  109.0 4.7 %collective-permute-start.7 = (bf16[256,512]{1,0:T(8,128)(2,1)S(1)}, bf16[256,512]{1,0:T(8,128)(2,1)S(1)}, u32[]{:S(2)}, u32[]{:S(2)}) collective-permute-start(bf16[256,512]{1,0:T(8,128)(2,1)S(1)} %collective-permute-done.6.own), channel_id=1, source_target_pairs={{0,32},{32,0},{1,33},{33,1},{2,34},{34,2},{3,35},{35,3},{4,36},{36... | collective-permute-start | bytes 786440 | tf_op jit(solution)/shard_map/ppermute | solution.py:160
  119.4 3.8 %collective-permute-start.8 = (bf16[512,512]{1,0:T(8,128)(2,1)S(1)}, bf16[512,512]{1,0:T(8,128)(2,1)S(1)}, u32[]{:S(2)}, u32[]{:S(2)}) collective-permute-start(bf16[512,512]{1,0:T(8,128)(2,1)S(1)} %get-tuple-element.15.own), channel_id=1, source_target_pairs={{0,32},{32,0},{1,33},{33,1},{2,34},{34,2},{3,35},{35,3},{4,36},{36... | collective-permute-start | bytes 1572872 | tf_op jit(solution)/shard_map/ppermute | solution.py:160

commit v5 on v4

--- a/solution.py
+++ b/solution.py
@@ -30,13 +30,17 @@
 
 
 def partial_kernel(classes, *refs):
-    features, hidden, out = refs[:classes], refs[classes:-1], refs[-1]
+    features, hidden, out, held, sems = refs[:classes], refs[classes:-3], refs[-3], refs[-2], refs[-1]
     rows = features[0].shape[0] // CLASSES
     own = lax.axis_index("y_hi")
-    for column in range(2):
-        first = (own + column - 2 * own * column) * CLASSES
-        for at in range(classes):
-            total = dot(features[at][...], hidden[column][...]).astype(BF16)
+    copies = [pltpu.make_async_copy(features[at], held.at[at], sems.at[at]) for at in range(classes)]
+    for copy in copies:
+        copy.start()
+    for at in range(classes):
+        copies[at].wait()
+        for column in range(2):
+            first = (own + column - 2 * own * column) * CLASSES
+            total = dot(held[at], hidden[column][...]).astype(BF16)
             for block in range(CLASSES):
                 out[first + block, at * rows : (at + 1) * rows, :] = total[
                     block * rows : (block + 1) * rows
@@ -45,13 +49,15 @@
 
 def partials(features, hidden):
     classes = len(features)
-    rows = features[0].shape[0] // CLASSES
+    height, tokens = features[0].shape
+    rows = height // CLASSES
     width = hidden[0].shape[1]
     return pl.pallas_call(
         functools.partial(partial_kernel, classes),
         out_shape=jax.ShapeDtypeStruct((2 * CLASSES, classes * rows, width), BF16),
-        in_specs=[VMEM] * (classes + 2),
+        in_specs=[pl.BlockSpec(memory_space=pl.ANY)] * classes + [VMEM] * 2,
         out_specs=VMEM,
+        scratch_shapes=[pltpu.VMEM((classes, height, tokens), BF16), pltpu.SemaphoreType.DMA((classes,))],
         compiler_params=LIMIT,
     )(*features, *hidden)
 

time: 125 us -> 125 us (level)
  the two profiles are of different devices: /device:TPU:105 before, /device:TPU:9 now
where the time goes in v5:
time: 125 us; the launch traced here: 124 us
  blocking collectives  65.6 us (52%)
  starting transfers between devices  27.9 us (22%)
  waiting for transfers between devices  15.9 us (13%)
  Pallas kernels  10.4 us (8%)
  between operations  2.12 us (2%)
  other arithmetic  1.42 us (1%)
  local copies, waits for them, and re-layouts  1.26 us (1%)
    all_to_all x2, blocking collectives, reduced(): got = lax.all_to_all(parts, ('y_lo', 'x'), 0, 0, tiled=True)  34.2 us
    all_gather x1, blocking collectives, per_device(): lax.all_gather(block, 'z', axis=0, tiled=True, axis_index_groups=strided)  31.4 us
    ppermute x5, starting transfers between devices, other_of(): return lax.ppermute(value, axis, [(0, 1), (1, 0)])  17.5 us
    ppermute x1, waiting for transfers between devices, two_away(): return lax.ppermute(value, ('core', 'z'), pairs)  7.71 us
    pallas_call x1, Pallas kernels, roots(): pl.pallas_call(newton_kernel, out_shape=(jax.ShapeDtypeStruct((BLOCK, BLO...  5.74 us
    ppermute x2, starting transfers between devices, along_z(): return lax.ppermute(value, 'z', [(i, (i - by) % size) for i in range(size)])  5.27 us
    ppermute x1, waiting for transfers between devices, to_home(): return lax.ppermute(value, ('y_lo', 'y_hi'), pairs)  4.24 us
    ppermute x5, waiting for transfers between devices, other_of(): return lax.ppermute(value, axis, [(0, 1), (1, 0)])  3.9 us
  transfers between devices with their start and end apart: 9, of which 6 were waited for; matrix products, arithmetic and copies ran while one was open for 2% of the time, Pallas kernels for 1%

profile of v5, /device:TPU:9, one launch (start us, length us, event | category | flops | bytes accessed | tf_op | source)
XLA Modules:
  0.0 124.5 jit_solution(612033591886607009)
XLA Ops:
  0.6 0.0 copy-start.2
  0.6 2.7 %collective-permute-start.4 = (bf16[512,512]{1,0:T(8,128)(2,1)}, bf16[512,512]{1,0:T(8,128)(2,1)S(1)}, u32[]{:S(2)}, u32[]{:S(2)}) collective-permute-start(bf16[512,512]{1,0:T(8,128)(2,1)} %param.6), channel_id=1, source_target_pairs={{0,32},{32,0},{1,33},{33,1},{2,34},{34,2},{3,35},{35,3},{4,36},{36... | collective-permute-start | bytes 1572872 | tf_op jit(solution)/shard_map/ppermute | solution.py:166
  3.4 1.1 constant_dynamic-update-slice_fusion.1
  4.4 0.6 collective-permute-done.4
  5.1 3.9 %collective-permute-start.5 = (bf16[1024,512]{1,0:T(8,128)(2,1)S(1)}, bf16[1024,512]{1,0:T(8,128)(2,1)S(1)}, u32[]{:S(2)}, u32[]{:S(2)}) collective-permute-start(bf16[1024,512]{1,0:T(8,128)(2,1)S(1)} %constant_dynamic-update-slice_fusion.refs_1_.refs_3_), channel_id=1, source_target_pairs={{0,16},{16,0},{1,17},{17,1},{2,18},{18,2},{3,19},{19,3},{4,20},{20... | collective-permute-start | bytes 3145736 | tf_op jit(solution)/shard_map/ppermute | solution.py:166
  9.1 0.0 copy-done.2
  9.1 0.1 copy.9
  9.9 2.6 %collective-permute-start = (bf16[64,512]{1,0:T(8,128)(2,1)S(1)}, bf16[64,512]{1,0:T(8,128)(2,1)S(1)}, u32[]{:S(2)}, u32[]{:S(2)}) collective-permute-start(bf16[64,512]{1,0:T(8,128)(2,1)S(1)} %get-tuple-element.20), channel_id=1, source_target_pairs={{0,32},{32,0},{1,33},{33,1},{2,34},{34,2},{3,35},{35,3},{4,36},{36... | collective-permute-start | bytes 196616 | tf_op jit(solution)/shard_map/ppermute | solution.py:166
  12.5 0.9 collective-permute-done
  13.4 31.4 %all_gather.3.refs_0_ = bf16[256,1024]{1,0:T(8,128)(2,1)S(1)} all-gather(bf16[64,1024]{1,0:T(8,128)(2,1)S(1)} %pad_maximum_fusion.1), channel_id=1, replica_groups={{0,4,8,12},{1,5,9,13},{2,6,10,14},{3,7,11,15},{16,20,24,28},{17,21,25,2..., dimensions={0}, use_global_device_ids=true | all-gather | bytes 655360 | tf_op jit(solution)/shard_map/all_gather | solution.py:203
  44.8 3.2 %collective-permute-start.1 = (bf16[256,1024]{1,0:T(8,128)(2,1)S(1)}, bf16[256,1024]{1,0:T(8,128)(2,1)S(1)}, u32[]{:S(2)}, u32[]{:S(2)}) collective-permute-start(bf16[256,1024]{1,0:T(8,128)(2,1)S(1)} %all_gather.3.refs_0_), channel_id=1, source_target_pairs={{0,15},{1,0},{2,1},{3,2},{4,3},{5,4},{6,5},{7,6},{8,7},{9,8},{10,9... | collective-permute-start | bytes 1572872 | tf_op jit(solution)/shard_map/ppermute | solution.py:171
  48.1 2.0 %collective-permute-start.2 = (bf16[256,1024]{1,0:T(8,128)(2,1)S(1)}, bf16[256,1024]{1,0:T(8,128)(2,1)}, u32[]{:S(2)}, u32[]{:S(2)}) collective-permute-start(bf16[256,1024]{1,0:T(8,128)(2,1)S(1)} %all_gather.3.refs_0_), channel_id=1, source_target_pairs={{0,1},{1,2},{2,3},{3,4},{4,5},{5,6},{6,7},{7,8},{8,9},{9,10},{10,1... | collective-permute-start | bytes 1572872 | tf_op jit(solution)/shard_map/ppermute | solution.py:171
  50.1 2.1 %collective-permute-start.3 = (bf16[256,1024]{1,0:T(8,128)(2,1)S(1)}, bf16[256,1024]{1,0:T(8,128)(2,1)}, u32[]{:S(2)}, u32[]{:S(2)}) collective-permute-start(bf16[256,1024]{1,0:T(8,128)(2,1)S(1)} %all_gather.3.refs_0_), channel_id=1, source_target_pairs={{0,14},{1,15},{2,0},{3,1},{4,2},{5,3},{6,4},{7,5},{8,6},{9,7},{10,... | collective-permute-start | bytes 1572872 | tf_op jit(solution)/shard_map/ppermute | solution.py:178
  52.2 0.0 collective-permute-done.5.refs_2_.refs_4_
  52.2 0.8 shard_map.85
  53.0 11.5 %all_to_all.10 = bf16[8,64,512]{2,1,0:T(8,128)(2,1)} all-to-all(bf16[8,64,512]{2,1,0:T(8,128)(2,1)S(1)} %shard_map.85), channel_id=1, replica_groups=mesh['y_lo'=2,'x'=4,'core'=2,'y_hi'=2,'z'=16] {'y_lo','x'}, dimensions={0} | all-to-all | bytes 1048576 | tf_op jit(solution)/shard_map/all_to_all | solution.py:187
  64.4 1.1 reduce_sum.24
  65.5 0.0 collective-permute-done.1.refs_0_
  65.5 0.0 collective-permute-done.2.refs_1_
  65.6 7.7 %collective-permute-done.3.refs_2_ = bf16[256,1024]{1,0:T(8,128)(2,1)} collective-permute-done((bf16[256,1024]{1,0:T(8,128)(2,1)S(1)}, bf16[256,1024]{1,0:T(8,128)(2,1)}, u32[]{:S(2)}, u32[]{:S(2)}) %collective-permute-start.3) | collective-permute-done | bytes 524320 | tf_op jit(solution)/shard_map/ppermute | solution.py:178
  73.3 2.5 %shard_map.86 = bf16[8,192,512]{2,1,0:T(8,128)(2,1)S(1)} custom-call(bf16[256,1024]{1,0:T(8,128)(2,1)S(1)} %collective-permute-done.1.refs_0_, bf16[256,1024]{1,0:T(8,128)(2,1)} %collective-permute-done.2.refs_1_, bf16[256,1024]{1,0:T(8,128)(2,1)} %collective-permute-done.3.refs_2_, bf16[1024,512]{1,0:T(8,128)(2,1)S(1)} %constant_dynamic-update-slice_fusion.refs_1_.refs_3_, ...), custom_call_target="tpu_custom_call" | custom-call | tf_op jit(solution)/shard_map/pallas_call | solution.py:55
  75.8 22.7 %all_to_all.11 = bf16[8,192,512]{2,1,0:T(8,128)(2,1)S(1)} all-to-all(bf16[8,192,512]{2,1,0:T(8,128)(2,1)S(1)} %shard_map.86), channel_id=1, replica_groups=mesh['y_lo'=2,'x'=4,'core'=2,'y_hi'=2,'z'=16] {'y_lo','x'}, dimensions={0} | all-to-all | bytes 3145728 | tf_op jit(solution)/shard_map/all_to_all | solution.py:187
  98.5 0.0 copy-start
  98.5 0.0 copy-start.1
  98.5 0.3 reduce_sum.25
  98.8 3.0 %collective-permute-start.6 = (bf16[256,512]{1,0:T(8,128)(2,1)S(1)}, bf16[256,512]{1,0:T(8,128)(2,1)S(1)}, u32[]{:S(2)}, u32[]{:S(2)}) collective-permute-start(bf16[256,512]{1,0:T(8,128)(2,1)S(1)} %pad_maximum_fusion), channel_id=1, source_target_pairs={{0,0},{16,256},{256,16},{272,272},{1,1},{17,257},{257,17},{273,273... | collective-permute-start | bytes 786440 | tf_op jit(solution)/shard_map/ppermute | solution.py:183
  101.8 4.2 %collective-permute-done.6.own = bf16[256,512]{1,0:T(8,128)(2,1)S(1)} collective-permute-done((bf16[256,512]{1,0:T(8,128)(2,1)S(1)}, bf16[256,512]{1,0:T(8,128)(2,1)S(1)}, u32[]{:S(2)}, u32[]{:S(2)}) %collective-permute-start.6) | collective-permute-done | bytes 262176 | tf_op jit(solution)/shard_map/ppermute | solution.py:183
  106.0 6.4 %collective-permute-start.7 = (bf16[256,512]{1,0:T(8,128)(2,1)S(1)}, bf16[256,512]{1,0:T(8,128)(2,1)S(1)}, u32[]{:S(2)}, u32[]{:S(2)}) collective-permute-start(bf16[256,512]{1,0:T(8,128)(2,1)S(1)} %collective-permute-done.6.own), channel_id=1, source_target_pairs={{0,32},{32,0},{1,33},{33,1},{2,34},{34,2},{3,35},{35,3},{4,36},{36... | collective-permute-start | bytes 786440 | tf_op jit(solution)/shard_map/ppermute | solution.py:166
  113.1 0.5 collective-permute-done.7.other
  113.6 0.0 copy-done
  113.6 0.0 copy-done.1
  113.6 5.7 %shard_map.87 = (f32[512,512]{1,0:T(8,128)}, bf16[512,512]{1,0:T(8,128)(2,1)}, bf16[512,512]{1,0:T(8,128)(2,1)S(1)}, f32[8,128]{1,0:T(8,128)S(1)}) custom-call(s32[1,1]{1,0:T(1,128)S(6)} %copy.12.count, bf16[256,512]{1,0:T(8,128)(2,1)S(1)} %collective-permute-done.6.own, bf16[256,512]{1,0:T(8,128)(2,1)S(1)} %collective-permute-done.7.other, ...), custom_call_target="tpu_custom_call" | custom-call | tf_op jit(solution)/shard_map/pallas_call | solution.py:122
  119.4 1.9 %collective-permute-start.8 = (bf16[512,512]{1,0:T(8,128)(2,1)S(1)}, bf16[512,512]{1,0:T(8,128)(2,1)S(1)}, u32[]{:S(2)}, u32[]{:S(2)}) collective-permute-start(bf16[512,512]{1,0:T(8,128)(2,1)S(1)} %get-tuple-element.15.own), channel_id=1, source_target_pairs={{0,32},{32,0},{1,33},{33,1},{2,34},{34,2},{3,35},{35,3},{4,36},{36... | collective-permute-start | bytes 1572872 | tf_op jit(solution)/shard_map/ppermute | solution.py:166
  121.3 1.9 %collective-permute-done.8.other = bf16[512,512]{1,0:T(8,128)(2,1)S(1)} collective-permute-done((bf16[512,512]{1,0:T(8,128)(2,1)S(1)}, bf16[512,512]{1,0:T(8,128)(2,1)S(1)}, u32[]{:S(2)}, u32[]{:S(2)}) %collective-permute-start.8) | collective-permute-done | bytes 524320 | tf_op jit(solution)/shard_map/ppermute | solution.py:166
  123.2 1.3 %shard_map.88 = bf16[256,512]{1,0:T(8,128)(2,1)} custom-call(bf16[512,512]{1,0:T(8,128)(2,1)S(1)} %get-tuple-element.15.own, bf16[512,512]{1,0:T(8,128)(2,1)S(1)} %collective-permute-done.8.other, f32[8,128]{1,0:T(8,128)S(1)} %get-tuple-element.16.grad_square), custom_call_target="tpu_custom_call" | custom-call | tf_op jit(solution)/shard_map/pallas_call | solution.py:156
  (6 shorter events, 0.1 us)
Async XLA Ops:
  0.6 8.4 %copy-start.2 = (bf16[512,128]{1,0:T(8,128)(2,1)S(1)}, bf16[512,128]{1,0:T(8,128)(2,1)}, u32[]{:S(2)}) copy-start(bf16[512,128]{1,0:T(8,128)(2,1)} %param.7) | copy-start | bytes 393220
  0.6 4.4 %collective-permute-start.4 = (bf16[512,512]{1,0:T(8,128)(2,1)}, bf16[512,512]{1,0:T(8,128)(2,1)S(1)}, u32[]{:S(2)}, u32[]{:S(2)}) collective-permute-start(bf16[512,512]{1,0:T(8,128)(2,1)} %param.6), channel_id=1, source_target_pairs={{0,32},{32,0},{1,33},{33,1},{2,34},{34,2},{3,35},{35,3},{4,36},{36... | collective-permute-start | bytes 1572872 | tf_op jit(solution)/shard_map/ppermute | solution.py:166
  5.1 47.0 %collective-permute-start.5 = (bf16[1024,512]{1,0:T(8,128)(2,1)S(1)}, bf16[1024,512]{1,0:T(8,128)(2,1)S(1)}, u32[]{:S(2)}, u32[]{:S(2)}) collective-permute-start(bf16[1024,512]{1,0:T(8,128)(2,1)S(1)} %constant_dynamic-update-slice_fusion.refs_1_.refs_3_), channel_id=1, source_target_pairs={{0,16},{16,0},{1,17},{17,1},{2,18},{18,2},{3,19},{19,3},{4,20},{20... | collective-permute-start | bytes 3145736 | tf_op jit(solution)/shard_map/ppermute | solution.py:166
  9.9 3.5 %collective-permute-start = (bf16[64,512]{1,0:T(8,128)(2,1)S(1)}, bf16[64,512]{1,0:T(8,128)(2,1)S(1)}, u32[]{:S(2)}, u32[]{:S(2)}) collective-permute-start(bf16[64,512]{1,0:T(8,128)(2,1)S(1)} %get-tuple-element.20), channel_id=1, source_target_pairs={{0,32},{32,0},{1,33},{33,1},{2,34},{34,2},{3,35},{35,3},{4,36},{36... | collective-permute-start | bytes 196616 | tf_op jit(solution)/shard_map/ppermute | solution.py:166
  44.8 20.7 %collective-permute-start.1 = (bf16[256,1024]{1,0:T(8,128)(2,1)S(1)}, bf16[256,1024]{1,0:T(8,128)(2,1)S(1)}, u32[]{:S(2)}, u32[]{:S(2)}) collective-permute-start(bf16[256,1024]{1,0:T(8,128)(2,1)S(1)} %all_gather.3.refs_0_), channel_id=1, source_target_pairs={{0,15},{1,0},{2,1},{3,2},{4,3},{5,4},{6,5},{7,6},{8,7},{9,8},{10,9... | collective-permute-start | bytes 1572872 | tf_op jit(solution)/shard_map/ppermute | solution.py:171
  48.1 17.5 %collective-permute-start.2 = (bf16[256,1024]{1,0:T(8,128)(2,1)S(1)}, bf16[256,1024]{1,0:T(8,128)(2,1)}, u32[]{:S(2)}, u32[]{:S(2)}) collective-permute-start(bf16[256,1024]{1,0:T(8,128)(2,1)S(1)} %all_gather.3.refs_0_), channel_id=1, source_target_pairs={{0,1},{1,2},{2,3},{3,4},{4,5},{5,6},{6,7},{7,8},{8,9},{9,10},{10,1... | collective-permute-start | bytes 1572872 | tf_op jit(solution)/shard_map/ppermute | solution.py:171
  50.1 23.2 %collective-permute-start.3 = (bf16[256,1024]{1,0:T(8,128)(2,1)S(1)}, bf16[256,1024]{1,0:T(8,128)(2,1)}, u32[]{:S(2)}, u32[]{:S(2)}) collective-permute-start(bf16[256,1024]{1,0:T(8,128)(2,1)S(1)} %all_gather.3.refs_0_), channel_id=1, source_target_pairs={{0,14},{1,15},{2,0},{3,1},{4,2},{5,3},{6,4},{7,5},{8,6},{9,7},{10,... | collective-permute-start | bytes 1572872 | tf_op jit(solution)/shard_map/ppermute | solution.py:178
  98.5 15.1 %copy-start = (f32[512,512]{1,0:T(8,128)S(1)}, f32[512,512]{1,0:T(8,128)}, u32[]{:S(2)}) copy-start(f32[512,512]{1,0:T(8,128)} %state.1) | copy-start | bytes 3145732
  98.5 15.1 %copy-start.1 = (bf16[512,512]{1,0:T(8,128)(2,1)S(1)}, bf16[512,512]{1,0:T(8,128)(2,1)}, u32[]{:S(2)}) copy-start(bf16[512,512]{1,0:T(8,128)(2,1)} %stale.1) | copy-start | bytes 1572868
  98.8 7.2 %collective-permute-start.6 = (bf16[256,512]{1,0:T(8,128)(2,1)S(1)}, bf16[256,512]{1,0:T(8,128)(2,1)S(1)}, u32[]{:S(2)}, u32[]{:S(2)}) collective-permute-start(bf16[256,512]{1,0:T(8,128)(2,1)S(1)} %pad_maximum_fusion), channel_id=1, source_target_pairs={{0,0},{16,256},{256,16},{272,272},{1,1},{17,257},{257,17},{273,273... | collective-permute-start | bytes 786440 | tf_op jit(solution)/shard_map/ppermute | solution.py:183
  106.0 7.6 %collective-permute-start.7 = (bf16[256,512]{1,0:T(8,128)(2,1)S(1)}, bf16[256,512]{1,0:T(8,128)(2,1)S(1)}, u32[]{:S(2)}, u32[]{:S(2)}) collective-permute-start(bf16[256,512]{1,0:T(8,128)(2,1)S(1)} %collective-permute-done.6.own), channel_id=1, source_target_pairs={{0,32},{32,0},{1,33},{33,1},{2,34},{34,2},{3,35},{35,3},{4,36},{36... | collective-permute-start | bytes 786440 | tf_op jit(solution)/shard_map/ppermute | solution.py:166
  119.4 3.8 %collective-permute-start.8 = (bf16[512,512]{1,0:T(8,128)(2,1)S(1)}, bf16[512,512]{1,0:T(8,128)(2,1)S(1)}, u32[]{:S(2)}, u32[]{:S(2)}) collective-permute-start(bf16[512,512]{1,0:T(8,128)(2,1)S(1)} %get-tuple-element.15.own), channel_id=1, source_target_pairs={{0,32},{32,0},{1,33},{33,1},{2,34},{34,2},{3,35},{35,3},{4,36},{36... | collective-permute-start | bytes 1572872 | tf_op jit(solution)/shard_map/ppermute | solution.py:166

commit v6 on v5

--- a/solution.py
+++ b/solution.py
@@ -65,7 +65,7 @@
 def newton_kernel(count, own, other, state, stale, new_factor, new_root, payload, grad_square, grad, matrix, turned, square):
     side, first, steps = lax.axis_index("core"), lax.rem(lax.axis_index("z"), CLASSES), count[0, 0]
     rows = HALF // CLASSES
-    for at, shift in enumerate((0, 1, 3, 2)):
+    for at, shift in enumerate((0, 2, 1, 3)):
         start = lax.rem(first + shift, CLASSES) * (2 * rows)
         mine = pl.multiple_of(start + side * rows, rows)
         theirs = pl.multiple_of(start + (1 - side) * rows, rows)
@@ -201,12 +201,12 @@
     size = lax.axis_size("z")
     strided = [[at + CLASSES * i for i in range(size // CLASSES)] for at in range(CLASSES)]
     own_class = lax.all_gather(block, "z", axis=0, tiled=True, axis_index_groups=strided)
+    across = two_away(own_class)
     above = along_z(own_class, 1)
     below = along_z(own_class, -1)
-    across = two_away(own_class)
     own = reduced(partials([own_class], columns))
-    above, below, across, own = lax.optimization_barrier((above, below, across, own))
-    rest = reduced(partials([above, below, across], columns))
+    across, above, below, own = lax.optimization_barrier((across, above, below, own))
+    rest = reduced(partials([across, above, below], columns))
     own = to_home(jnp.concatenate([own, rest], axis=0))
     other = other_of(own, "core")
     new_factor, new_root, payload, grad_square = roots(newton_steps, own, other, factor_state, stale_root)

time: 125 us -> 122 us (0.976)
  the two profiles are of different devices: /device:TPU:9 before, /device:TPU:41 now
where the time goes in v6:
time: 122 us; the launch traced here: 121 us
  blocking collectives  61.4 us (50%)
  starting transfers between devices  36.7 us (30%)
  waiting for transfers between devices  11.7 us (10%)
  Pallas kernels  6.84 us (6%)
  between operations  2.11 us (2%)
  other arithmetic  1.42 us (1%)
  local copies, waits for them, and re-layouts  1.26 us (1%)
    all_to_all x2, blocking collectives, reduced(): got = lax.all_to_all(parts, ('y_lo', 'x'), 0, 0, tiled=True)  32.5 us
    all_gather x1, blocking collectives, per_device(): lax.all_gather(block, 'z', axis=0, tiled=True, axis_index_groups=strided)  28.8 us
    ppermute x5, starting transfers between devices, other_of(): return lax.ppermute(value, axis, [(0, 1), (1, 0)])  22.7 us
    ppermute x2, starting transfers between devices, along_z(): return lax.ppermute(value, 'z', [(i, (i - by) % size) for i in range(size)])  7.09 us
    ppermute x1, waiting for transfers between devices, to_home(): return lax.ppermute(value, ('y_lo', 'y_hi'), pairs)  4.15 us
    ppermute x2, waiting for transfers between devices, along_z(): return lax.ppermute(value, 'z', [(i, (i - by) % size) for i in range(size)])  4.06 us
    ppermute x1, starting transfers between devices, two_away(): return lax.ppermute(value, ('core', 'z'), pairs)  3.75 us
    ppermute x5, waiting for transfers between devices, other_of(): return lax.ppermute(value, axis, [(0, 1), (1, 0)])  3.54 us
  transfers between devices with their start and end apart: 9, of which 7 were waited for; matrix products, arithmetic and copies ran while one was open for 2% of the time, Pallas kernels for 1%

profile of v6, /device:TPU:41, one launch (start us, length us, event | category | flops | bytes accessed | tf_op | source)
XLA Modules:
  0.0 121.4 jit_solution(1364906659494513948)
XLA Ops:
  0.6 0.0 copy-start.2
  0.6 2.7 %collective-permute-start.4 = (bf16[512,512]{1,0:T(8,128)(2,1)}, bf16[512,512]{1,0:T(8,128)(2,1)S(1)}, u32[]{:S(2)}, u32[]{:S(2)}) collective-permute-start(bf16[512,512]{1,0:T(8,128)(2,1)} %param.6), channel_id=1, source_target_pairs={{0,32},{32,0},{1,33},{33,1},{2,34},{34,2},{3,35},{35,3},{4,36},{36... | collective-permute-start | bytes 1572872 | tf_op jit(solution)/shard_map/ppermute | solution.py:166
  3.4 1.1 constant_dynamic-update-slice_fusion.1
  4.4 0.6 collective-permute-done.4
  5.1 3.9 %collective-permute-start.5 = (bf16[1024,512]{1,0:T(8,128)(2,1)S(1)}, bf16[1024,512]{1,0:T(8,128)(2,1)S(1)}, u32[]{:S(2)}, u32[]{:S(2)}) collective-permute-start(bf16[1024,512]{1,0:T(8,128)(2,1)S(1)} %constant_dynamic-update-slice_fusion.refs_1_.refs_3_), channel_id=1, source_target_pairs={{0,16},{16,0},{1,17},{17,1},{2,18},{18,2},{3,19},{19,3},{4,20},{20... | collective-permute-start | bytes 3145736 | tf_op jit(solution)/shard_map/ppermute | solution.py:166
  9.1 0.0 copy-done.2
  9.1 0.1 copy.9
  9.9 2.6 %collective-permute-start = (bf16[64,512]{1,0:T(8,128)(2,1)S(1)}, bf16[64,512]{1,0:T(8,128)(2,1)S(1)}, u32[]{:S(2)}, u32[]{:S(2)}) collective-permute-start(bf16[64,512]{1,0:T(8,128)(2,1)S(1)} %get-tuple-element.20), channel_id=1, source_target_pairs={{0,32},{32,0},{1,33},{33,1},{2,34},{34,2},{3,35},{35,3},{4,36},{36... | collective-permute-start | bytes 196616 | tf_op jit(solution)/shard_map/ppermute | solution.py:166
  12.5 0.9 collective-permute-done
  13.4 28.8 %all_gather.3.refs_0_ = bf16[256,1024]{1,0:T(8,128)(2,1)S(1)} all-gather(bf16[64,1024]{1,0:T(8,128)(2,1)S(1)} %pad_maximum_fusion.1), channel_id=1, replica_groups={{0,4,8,12},{1,5,9,13},{2,6,10,14},{3,7,11,15},{16,20,24,28},{17,21,25,2..., dimensions={0}, use_global_device_ids=true | all-gather | bytes 655360 | tf_op jit(solution)/shard_map/all_gather | solution.py:203
  42.2 3.8 %collective-permute-start.1 = (bf16[256,1024]{1,0:T(8,128)(2,1)S(1)}, bf16[256,1024]{1,0:T(8,128)(2,1)S(1)}, u32[]{:S(2)}, u32[]{:S(2)}) collective-permute-start(bf16[256,1024]{1,0:T(8,128)(2,1)S(1)} %all_gather.3.refs_0_), channel_id=1, source_target_pairs={{0,14},{1,15},{2,0},{3,1},{4,2},{5,3},{6,4},{7,5},{8,6},{9,7},{10,... | collective-permute-start | bytes 1572872 | tf_op jit(solution)/shard_map/ppermute | solution.py:178
  46.0 2.6 %collective-permute-start.2 = (bf16[256,1024]{1,0:T(8,128)(2,1)S(1)}, bf16[256,1024]{1,0:T(8,128)(2,1)}, u32[]{:S(2)}, u32[]{:S(2)}) collective-permute-start(bf16[256,1024]{1,0:T(8,128)(2,1)S(1)} %all_gather.3.refs_0_), channel_id=1, source_target_pairs={{0,15},{1,0},{2,1},{3,2},{4,3},{5,4},{6,5},{7,6},{8,7},{9,8},{10,9... | collective-permute-start | bytes 1572872 | tf_op jit(solution)/shard_map/ppermute | solution.py:171
  48.6 4.4 %collective-permute-start.3 = (bf16[256,1024]{1,0:T(8,128)(2,1)S(1)}, bf16[256,1024]{1,0:T(8,128)(2,1)}, u32[]{:S(2)}, u32[]{:S(2)}) collective-permute-start(bf16[256,1024]{1,0:T(8,128)(2,1)S(1)} %all_gather.3.refs_0_), channel_id=1, source_target_pairs={{0,1},{1,2},{2,3},{3,4},{4,5},{5,6},{6,7},{7,8},{8,9},{9,10},{10,1... | collective-permute-start | bytes 1572872 | tf_op jit(solution)/shard_map/ppermute | solution.py:171
  53.1 0.0 collective-permute-done.5.refs_2_.refs_4_
  53.1 0.8 shard_map.85
  53.9 11.5 %all_to_all.10 = bf16[8,64,512]{2,1,0:T(8,128)(2,1)} all-to-all(bf16[8,64,512]{2,1,0:T(8,128)(2,1)S(1)} %shard_map.85), channel_id=1, replica_groups=mesh['y_lo'=2,'x'=4,'core'=2,'y_hi'=2,'z'=16] {'y_lo','x'}, dimensions={0} | all-to-all | bytes 1048576 | tf_op jit(solution)/shard_map/all_to_all | solution.py:187
  65.4 1.1 reduce_sum.24
  66.5 0.0 collective-permute-done.1.refs_0_
  66.5 2.6 %collective-permute-done.2.refs_1_ = bf16[256,1024]{1,0:T(8,128)(2,1)} collective-permute-done((bf16[256,1024]{1,0:T(8,128)(2,1)S(1)}, bf16[256,1024]{1,0:T(8,128)(2,1)}, u32[]{:S(2)}, u32[]{:S(2)}) %collective-permute-start.2) | collective-permute-done | bytes 524320 | tf_op jit(solution)/shard_map/ppermute | solution.py:171
  69.1 1.5 %collective-permute-done.3.refs_2_ = bf16[256,1024]{1,0:T(8,128)(2,1)} collective-permute-done((bf16[256,1024]{1,0:T(8,128)(2,1)S(1)}, bf16[256,1024]{1,0:T(8,128)(2,1)}, u32[]{:S(2)}, u32[]{:S(2)}) %collective-permute-start.3) | collective-permute-done | bytes 524320 | tf_op jit(solution)/shard_map/ppermute | solution.py:171
  70.6 2.5 %shard_map.86 = bf16[8,192,512]{2,1,0:T(8,128)(2,1)S(1)} custom-call(bf16[256,1024]{1,0:T(8,128)(2,1)S(1)} %collective-permute-done.1.refs_0_, bf16[256,1024]{1,0:T(8,128)(2,1)} %collective-permute-done.2.refs_1_, bf16[256,1024]{1,0:T(8,128)(2,1)} %collective-permute-done.3.refs_2_, bf16[1024,512]{1,0:T(8,128)(2,1)S(1)} %constant_dynamic-update-slice_fusion.refs_1_.refs_3_, ...), custom_call_target="tpu_custom_call" | custom-call | tf_op jit(solution)/shard_map/pallas_call | solution.py:55
  73.1 21.0 %all_to_all.11 = bf16[8,192,512]{2,1,0:T(8,128)(2,1)S(1)} all-to-all(bf16[8,192,512]{2,1,0:T(8,128)(2,1)S(1)} %shard_map.86), channel_id=1, replica_groups=mesh['y_lo'=2,'x'=4,'core'=2,'y_hi'=2,'z'=16] {'y_lo','x'}, dimensions={0} | all-to-all | bytes 3145728 | tf_op jit(solution)/shard_map/all_to_all | solution.py:187
  94.1 0.0 copy-start
  94.1 0.0 copy-start.1
  94.1 0.3 reduce_sum.25
  94.4 3.1 %collective-permute-start.6 = (bf16[256,512]{1,0:T(8,128)(2,1)S(1)}, bf16[256,512]{1,0:T(8,128)(2,1)S(1)}, u32[]{:S(2)}, u32[]{:S(2)}) collective-permute-start(bf16[256,512]{1,0:T(8,128)(2,1)S(1)} %pad_maximum_fusion), channel_id=1, source_target_pairs={{0,0},{16,256},{256,16},{272,272},{1,1},{17,257},{257,17},{273,273... | collective-permute-start | bytes 786440 | tf_op jit(solution)/shard_map/ppermute | solution.py:183
  97.5 4.1 %collective-permute-done.6.own = bf16[256,512]{1,0:T(8,128)(2,1)S(1)} collective-permute-done((bf16[256,512]{1,0:T(8,128)(2,1)S(1)}, bf16[256,512]{1,0:T(8,128)(2,1)S(1)}, u32[]{:S(2)}, u32[]{:S(2)}) %collective-permute-start.6) | collective-permute-done | bytes 262176 | tf_op jit(solution)/shard_map/ppermute | solution.py:183
  101.6 8.1 %collective-permute-start.7 = (bf16[256,512]{1,0:T(8,128)(2,1)S(1)}, bf16[256,512]{1,0:T(8,128)(2,1)S(1)}, u32[]{:S(2)}, u32[]{:S(2)}) collective-permute-start(bf16[256,512]{1,0:T(8,128)(2,1)S(1)} %collective-permute-done.6.own), channel_id=1, source_target_pairs={{0,32},{32,0},{1,33},{33,1},{2,34},{34,2},{3,35},{35,3},{4,36},{36... | collective-permute-start | bytes 786440 | tf_op jit(solution)/shard_map/ppermute | solution.py:166
  110.4 0.5 collective-permute-done.7.other
  110.9 0.0 copy-done
  110.9 0.0 copy-done.1
  110.9 2.2 %shard_map.87 = (f32[512,512]{1,0:T(8,128)}, bf16[512,512]{1,0:T(8,128)(2,1)}, bf16[512,512]{1,0:T(8,128)(2,1)S(1)}, f32[8,128]{1,0:T(8,128)S(1)}) custom-call(s32[1,1]{1,0:T(1,128)S(6)} %copy.12.count, bf16[256,512]{1,0:T(8,128)(2,1)S(1)} %collective-permute-done.6.own, bf16[256,512]{1,0:T(8,128)(2,1)S(1)} %collective-permute-done.7.other, ...), custom_call_target="tpu_custom_call" | custom-call | tf_op jit(solution)/shard_map/pallas_call | solution.py:122
  113.1 5.4 %collective-permute-start.8 = (bf16[512,512]{1,0:T(8,128)(2,1)S(1)}, bf16[512,512]{1,0:T(8,128)(2,1)S(1)}, u32[]{:S(2)}, u32[]{:S(2)}) collective-permute-start(bf16[512,512]{1,0:T(8,128)(2,1)S(1)} %get-tuple-element.15.own), channel_id=1, source_target_pairs={{0,32},{32,0},{1,33},{33,1},{2,34},{34,2},{3,35},{35,3},{4,36},{36... | collective-permute-start | bytes 1572872 | tf_op jit(solution)/shard_map/ppermute | solution.py:166
  118.6 1.5 %collective-permute-done.8.other = bf16[512,512]{1,0:T(8,128)(2,1)S(1)} collective-permute-done((bf16[512,512]{1,0:T(8,128)(2,1)S(1)}, bf16[512,512]{1,0:T(8,128)(2,1)S(1)}, u32[]{:S(2)}, u32[]{:S(2)}) %collective-permute-start.8) | collective-permute-done | bytes 524320 | tf_op jit(solution)/shard_map/ppermute | solution.py:166
  120.1 1.3 %shard_map.88 = bf16[256,512]{1,0:T(8,128)(2,1)} custom-call(bf16[512,512]{1,0:T(8,128)(2,1)S(1)} %get-tuple-element.15.own, bf16[512,512]{1,0:T(8,128)(2,1)S(1)} %collective-permute-done.8.other, f32[8,128]{1,0:T(8,128)S(1)} %get-tuple-element.16.grad_square), custom_call_target="tpu_custom_call" | custom-call | tf_op jit(solution)/shard_map/pallas_call | solution.py:156
  (6 shorter events, 0.1 us)
Async XLA Ops:
  0.6 8.4 %copy-start.2 = (bf16[512,128]{1,0:T(8,128)(2,1)S(1)}, bf16[512,128]{1,0:T(8,128)(2,1)}, u32[]{:S(2)}) copy-start(bf16[512,128]{1,0:T(8,128)(2,1)} %param.7) | copy-start | bytes 393220
  0.6 4.4 %collective-permute-start.4 = (bf16[512,512]{1,0:T(8,128)(2,1)}, bf16[512,512]{1,0:T(8,128)(2,1)S(1)}, u32[]{:S(2)}, u32[]{:S(2)}) collective-permute-start(bf16[512,512]{1,0:T(8,128)(2,1)} %param.6), channel_id=1, source_target_pairs={{0,32},{32,0},{1,33},{33,1},{2,34},{34,2},{3,35},{35,3},{4,36},{36... | collective-permute-start | bytes 1572872 | tf_op jit(solution)/shard_map/ppermute | solution.py:166
  5.1 47.9 %collective-permute-start.5 = (bf16[1024,512]{1,0:T(8,128)(2,1)S(1)}, bf16[1024,512]{1,0:T(8,128)(2,1)S(1)}, u32[]{:S(2)}, u32[]{:S(2)}) collective-permute-start(bf16[1024,512]{1,0:T(8,128)(2,1)S(1)} %constant_dynamic-update-slice_fusion.refs_1_.refs_3_), channel_id=1, source_target_pairs={{0,16},{16,0},{1,17},{17,1},{2,18},{18,2},{3,19},{19,3},{4,20},{20... | collective-permute-start | bytes 3145736 | tf_op jit(solution)/shard_map/ppermute | solution.py:166
  9.9 3.5 %collective-permute-start = (bf16[64,512]{1,0:T(8,128)(2,1)S(1)}, bf16[64,512]{1,0:T(8,128)(2,1)S(1)}, u32[]{:S(2)}, u32[]{:S(2)}) collective-permute-start(bf16[64,512]{1,0:T(8,128)(2,1)S(1)} %get-tuple-element.20), channel_id=1, source_target_pairs={{0,32},{32,0},{1,33},{33,1},{2,34},{34,2},{3,35},{35,3},{4,36},{36... | collective-permute-start | bytes 196616 | tf_op jit(solution)/shard_map/ppermute | solution.py:166
  42.2 24.3 %collective-permute-start.1 = (bf16[256,1024]{1,0:T(8,128)(2,1)S(1)}, bf16[256,1024]{1,0:T(8,128)(2,1)S(1)}, u32[]{:S(2)}, u32[]{:S(2)}) collective-permute-start(bf16[256,1024]{1,0:T(8,128)(2,1)S(1)} %all_gather.3.refs_0_), channel_id=1, source_target_pairs={{0,14},{1,15},{2,0},{3,1},{4,2},{5,3},{6,4},{7,5},{8,6},{9,7},{10,... | collective-permute-start | bytes 1572872 | tf_op jit(solution)/shard_map/ppermute | solution.py:178
  46.0 23.1 %collective-permute-start.2 = (bf16[256,1024]{1,0:T(8,128)(2,1)S(1)}, bf16[256,1024]{1,0:T(8,128)(2,1)}, u32[]{:S(2)}, u32[]{:S(2)}) collective-permute-start(bf16[256,1024]{1,0:T(8,128)(2,1)S(1)} %all_gather.3.refs_0_), channel_id=1, source_target_pairs={{0,15},{1,0},{2,1},{3,2},{4,3},{5,4},{6,5},{7,6},{8,7},{9,8},{10,9... | collective-permute-start | bytes 1572872 | tf_op jit(solution)/shard_map/ppermute | solution.py:171
  48.6 21.9 %collective-permute-start.3 = (bf16[256,1024]{1,0:T(8,128)(2,1)S(1)}, bf16[256,1024]{1,0:T(8,128)(2,1)}, u32[]{:S(2)}, u32[]{:S(2)}) collective-permute-start(bf16[256,1024]{1,0:T(8,128)(2,1)S(1)} %all_gather.3.refs_0_), channel_id=1, source_target_pairs={{0,1},{1,2},{2,3},{3,4},{4,5},{5,6},{6,7},{7,8},{8,9},{9,10},{10,1... | collective-permute-start | bytes 1572872 | tf_op jit(solution)/shard_map/ppermute | solution.py:171
  94.1 16.8 %copy-start = (f32[512,512]{1,0:T(8,128)S(1)}, f32[512,512]{1,0:T(8,128)}, u32[]{:S(2)}) copy-start(f32[512,512]{1,0:T(8,128)} %state.1) | copy-start | bytes 3145732
  94.1 16.8 %copy-start.1 = (bf16[512,512]{1,0:T(8,128)(2,1)S(1)}, bf16[512,512]{1,0:T(8,128)(2,1)}, u32[]{:S(2)}) copy-start(bf16[512,512]{1,0:T(8,128)(2,1)} %stale.1) | copy-start | bytes 1572868
  94.4 7.2 %collective-permute-start.6 = (bf16[256,512]{1,0:T(8,128)(2,1)S(1)}, bf16[256,512]{1,0:T(8,128)(2,1)S(1)}, u32[]{:S(2)}, u32[]{:S(2)}) collective-permute-start(bf16[256,512]{1,0:T(8,128)(2,1)S(1)} %pad_maximum_fusion), channel_id=1, source_target_pairs={{0,0},{16,256},{256,16},{272,272},{1,1},{17,257},{257,17},{273,273... | collective-permute-start | bytes 786440 | tf_op jit(solution)/shard_map/ppermute | solution.py:183
  101.6 9.3 %collective-permute-start.7 = (bf16[256,512]{1,0:T(8,128)(2,1)S(1)}, bf16[256,512]{1,0:T(8,128)(2,1)S(1)}, u32[]{:S(2)}, u32[]{:S(2)}) collective-permute-start(bf16[256,512]{1,0:T(8,128)(2,1)S(1)} %collective-permute-done.6.own), channel_id=1, source_target_pairs={{0,32},{32,0},{1,33},{33,1},{2,34},{34,2},{3,35},{35,3},{4,36},{36... | collective-permute-start | bytes 786440 | tf_op jit(solution)/shard_map/ppermute | solution.py:166
  113.1 6.9 %collective-permute-start.8 = (bf16[512,512]{1,0:T(8,128)(2,1)S(1)}, bf16[512,512]{1,0:T(8,128)(2,1)S(1)}, u32[]{:S(2)}, u32[]{:S(2)}) collective-permute-start(bf16[512,512]{1,0:T(8,128)(2,1)S(1)} %get-tuple-element.15.own), channel_id=1, source_target_pairs={{0,32},{32,0},{1,33},{33,1},{2,34},{34,2},{3,35},{35,3},{4,36},{36... | collective-permute-start | bytes 1572872 | tf_op jit(solution)/shard_map/ppermute | solution.py:166

commit v7 on v6

--- a/solution.py
+++ b/solution.py
@@ -191,13 +191,14 @@
 def per_device(hidden, out_grad, token_counts, factor_state, stale_root, newton_steps):
     core = lax.axis_index("core")
     column = jnp.concatenate([hidden, other_of(hidden, "core")], axis=0)
-    columns = (column, other_of(column, "y_hi"))
     positions = lax.broadcasted_iota(jnp.int32, (out_grad.shape[0], 1), 0)
     kept = jnp.where(positions < token_counts[0], out_grad, jnp.zeros_like(out_grad)).T
     rows = kept.shape[0] // 2
     mine = lax.dynamic_slice_in_dim(kept, core * rows, rows, 0)
     sent = lax.dynamic_slice_in_dim(kept, (1 - core) * rows, rows, 0)
-    block = jnp.concatenate([mine, other_of(sent, "core")], axis=1)
+    got, column = lax.optimization_barrier((other_of(sent, "core"), column))
+    columns = (column, other_of(column, "y_hi"))
+    block = jnp.concatenate([mine, got], axis=1)
     size = lax.axis_size("z")
     strided = [[at + CLASSES * i for i in range(size // CLASSES)] for at in range(CLASSES)]
     own_class = lax.all_gather(block, "z", axis=0, tiled=True, axis_index_groups=strided)

time: 122 us -> 123 us (level)
  the two profiles are of different devices: /device:TPU:41 before, /device:TPU:9 now
where the time goes in v7:
time: 123 us; the launch traced here: 121 us
  blocking collectives  64.6 us (53%)
  starting transfers between devices  28.4 us (23%)
  waiting for transfers between devices  13.1 us (11%)
  Pallas kernels  8.92 us (7%)
  other arithmetic  2.53 us (2%)
  between operations  2.11 us (2%)
    all_to_all x2, blocking collectives, reduced(): got = lax.all_to_all(parts, ('y_lo', 'x'), 0, 0, tiled=True)  34.3 us
    all_gather x1, blocking collectives, per_device(): lax.all_gather(block, 'z', axis=0, tiled=True, axis_index_groups=strided)  30.4 us
    ppermute x5, starting transfers between devices, other_of(): return lax.ppermute(value, axis, [(0, 1), (1, 0)])  16.7 us
    ppermute x2, waiting for transfers between devices, along_z(): return lax.ppermute(value, 'z', [(i, (i - by) % size) for i in range(size)])  6.38 us
    ppermute x2, starting transfers between devices, along_z(): return lax.ppermute(value, 'z', [(i, (i - by) % size) for i in range(size)])  5.71 us
    pallas_call x1, Pallas kernels, roots(): pl.pallas_call(newton_kernel, out_shape=(jax.ShapeDtypeStruct((BLOCK, BLO...  4.32 us
    ppermute x1, waiting for transfers between devices, to_home(): return lax.ppermute(value, ('y_lo', 'y_hi'), pairs)  4.24 us
    pallas_call x2, Pallas kernels, partials(): pl.pallas_call(functools.partial(partial_kernel, classes), out_shape=jax....  3.28 us
  transfers between devices with their start and end apart: 9, of which 5 were waited for; matrix products, arithmetic and copies ran while one was open for 3% of the time, Pallas kernels for 1%

profile of v7, /device:TPU:9, one launch (start us, length us, event | category | flops | bytes accessed | tf_op | source)
XLA Modules:
  0.0 120.7 jit_solution(10223101204423588213)
XLA Ops:
  0.6 2.6 %collective-permute-start.1 = (bf16[512,512]{1,0:T(8,128)(2,1)}, bf16[512,512]{1,0:T(8,128)(2,1)S(1)}, u32[]{:S(2)}, u32[]{:S(2)}) collective-permute-start(bf16[512,512]{1,0:T(8,128)(2,1)} %param.6), channel_id=1, source_target_pairs={{0,32},{32,0},{1,33},{33,1},{2,34},{34,2},{3,35},{35,3},{4,36},{36... | collective-permute-start | bytes 1572872 | tf_op jit(solution)/shard_map/ppermute | solution.py:166
  3.2 1.0 copy.9
  5.0 1.9 %collective-permute-start = (bf16[64,512]{1,0:T(8,128)(2,1)S(1)}, bf16[64,512]{1,0:T(8,128)(2,1)S(1)}, u32[]{:S(2)}, u32[]{:S(2)}) collective-permute-start(bf16[64,512]{1,0:T(8,128)(2,1)S(1)} %get-tuple-element.24), channel_id=1, source_target_pairs={{0,32},{32,0},{1,33},{33,1},{2,34},{34,2},{3,35},{35,3},{4,36},{36... | collective-permute-start | bytes 196616 | tf_op jit(solution)/shard_map/ppermute | solution.py:166
  6.9 0.0 collective-permute-done.1
  6.9 1.1 pad_maximum_fusion.refs_1_.refs_3_
  8.0 0.1 collective-permute-done
  8.1 3.9 %collective-permute-start.5 = (bf16[1024,512]{1,0:T(8,128)(2,1)S(1)}, bf16[1024,512]{1,0:T(8,128)(2,1)S(1)}, u32[]{:S(2)}, u32[]{:S(2)}) collective-permute-start(bf16[1024,512]{1,0:T(8,128)(2,1)S(1)} %pad_maximum_fusion.refs_1_.refs_3_), channel_id=1, source_target_pairs={{0,16},{16,0},{1,17},{17,1},{2,18},{18,2},{3,19},{19,3},{4,20},{20... | collective-permute-start | bytes 3145736 | tf_op jit(solution)/shard_map/ppermute | solution.py:166
  12.0 30.4 %all_gather.3.refs_0_ = bf16[256,1024]{1,0:T(8,128)(2,1)S(1)} all-gather(bf16[64,1024]{1,0:T(8,128)(2,1)S(1)} %pad_maximum_fusion.2), channel_id=1, replica_groups={{0,4,8,12},{1,5,9,13},{2,6,10,14},{3,7,11,15},{16,20,24,28},{17,21,25,2..., dimensions={0}, use_global_device_ids=true | all-gather | bytes 655360 | tf_op jit(solution)/shard_map/all_gather | solution.py:204
  42.4 3.1 %collective-permute-start.2 = (bf16[256,1024]{1,0:T(8,128)(2,1)S(1)}, bf16[256,1024]{1,0:T(8,128)(2,1)S(1)}, u32[]{:S(2)}, u32[]{:S(2)}) collective-permute-start(bf16[256,1024]{1,0:T(8,128)(2,1)S(1)} %all_gather.3.refs_0_), channel_id=1, source_target_pairs={{0,14},{1,15},{2,0},{3,1},{4,2},{5,3},{6,4},{7,5},{8,6},{9,7},{10,... | collective-permute-start | bytes 1572872 | tf_op jit(solution)/shard_map/ppermute | solution.py:178
  45.5 3.8 %collective-permute-start.3 = (bf16[256,1024]{1,0:T(8,128)(2,1)S(1)}, bf16[256,1024]{1,0:T(8,128)(2,1)}, u32[]{:S(2)}, u32[]{:S(2)}) collective-permute-start(bf16[256,1024]{1,0:T(8,128)(2,1)S(1)} %all_gather.3.refs_0_), channel_id=1, source_target_pairs={{0,15},{1,0},{2,1},{3,2},{4,3},{5,4},{6,5},{7,6},{8,7},{9,8},{10,9... | collective-permute-start | bytes 1572872 | tf_op jit(solution)/shard_map/ppermute | solution.py:171
  49.3 1.9 %collective-permute-start.4 = (bf16[256,1024]{1,0:T(8,128)(2,1)S(1)}, bf16[256,1024]{1,0:T(8,128)(2,1)}, u32[]{:S(2)}, u32[]{:S(2)}) collective-permute-start(bf16[256,1024]{1,0:T(8,128)(2,1)S(1)} %all_gather.3.refs_0_), channel_id=1, source_target_pairs={{0,1},{1,2},{2,3},{3,4},{4,5},{5,6},{6,7},{7,8},{8,9},{9,10},{10,1... | collective-permute-start | bytes 1572872 | tf_op jit(solution)/shard_map/ppermute | solution.py:171
  51.2 0.0 collective-permute-done.5.refs_2_.refs_4_
  51.2 0.8 shard_map.85
  52.0 11.5 %all_to_all.10 = bf16[8,64,512]{2,1,0:T(8,128)(2,1)} all-to-all(bf16[8,64,512]{2,1,0:T(8,128)(2,1)S(1)} %shard_map.85), channel_id=1, replica_groups=mesh['y_lo'=2,'x'=4,'core'=2,'y_hi'=2,'z'=16] {'y_lo','x'}, dimensions={0} | all-to-all | bytes 1048576 | tf_op jit(solution)/shard_map/all_to_all | solution.py:187
  63.4 1.1 reduce_sum.24
  64.6 0.0 collective-permute-done.2.refs_0_
  64.6 0.0 collective-permute-done.3.refs_1_
  64.6 6.4 %collective-permute-done.4.refs_2_ = bf16[256,1024]{1,0:T(8,128)(2,1)} collective-permute-done((bf16[256,1024]{1,0:T(8,128)(2,1)S(1)}, bf16[256,1024]{1,0:T(8,128)(2,1)}, u32[]{:S(2)}, u32[]{:S(2)}) %collective-permute-start.4) | collective-permute-done | bytes 524320 | tf_op jit(solution)/shard_map/ppermute | solution.py:171
  71.0 2.5 %shard_map.86 = bf16[8,192,512]{2,1,0:T(8,128)(2,1)S(1)} custom-call(bf16[256,1024]{1,0:T(8,128)(2,1)S(1)} %collective-permute-done.2.refs_0_, bf16[256,1024]{1,0:T(8,128)(2,1)} %collective-permute-done.3.refs_1_, bf16[256,1024]{1,0:T(8,128)(2,1)} %collective-permute-done.4.refs_2_, bf16[1024,512]{1,0:T(8,128)(2,1)S(1)} %pad_maximum_fusion.refs_1_.refs_3_, ...), custom_call_target="tpu_custom_call" | custom-call | tf_op jit(solution)/shard_map/pallas_call | solution.py:55
  73.5 22.8 %all_to_all.11 = bf16[8,192,512]{2,1,0:T(8,128)(2,1)S(1)} all-to-all(bf16[8,192,512]{2,1,0:T(8,128)(2,1)S(1)} %shard_map.86), channel_id=1, replica_groups=mesh['y_lo'=2,'x'=4,'core'=2,'y_hi'=2,'z'=16] {'y_lo','x'}, dimensions={0} | all-to-all | bytes 3145728 | tf_op jit(solution)/shard_map/all_to_all | solution.py:187
  96.3 0.0 copy-start
  96.3 0.0 copy-start.1
  96.3 0.3 reduce_sum.25
  96.6 3.0 %collective-permute-start.6 = (bf16[256,512]{1,0:T(8,128)(2,1)S(1)}, bf16[256,512]{1,0:T(8,128)(2,1)S(1)}, u32[]{:S(2)}, u32[]{:S(2)}) collective-permute-start(bf16[256,512]{1,0:T(8,128)(2,1)S(1)} %pad_maximum_fusion.1), channel_id=1, source_target_pairs={{0,0},{16,256},{256,16},{272,272},{1,1},{17,257},{257,17},{273,273... | collective-permute-start | bytes 786440 | tf_op jit(solution)/shard_map/ppermute | solution.py:183
  99.6 4.2 %collective-permute-done.6.own = bf16[256,512]{1,0:T(8,128)(2,1)S(1)} collective-permute-done((bf16[256,512]{1,0:T(8,128)(2,1)S(1)}, bf16[256,512]{1,0:T(8,128)(2,1)S(1)}, u32[]{:S(2)}, u32[]{:S(2)}) %collective-permute-start.6) | collective-permute-done | bytes 262176 | tf_op jit(solution)/shard_map/ppermute | solution.py:183
  103.8 6.3 %collective-permute-start.7 = (bf16[256,512]{1,0:T(8,128)(2,1)S(1)}, bf16[256,512]{1,0:T(8,128)(2,1)S(1)}, u32[]{:S(2)}, u32[]{:S(2)}) collective-permute-start(bf16[256,512]{1,0:T(8,128)(2,1)S(1)} %collective-permute-done.6.own), channel_id=1, source_target_pairs={{0,32},{32,0},{1,33},{33,1},{2,34},{34,2},{3,35},{35,3},{4,36},{36... | collective-permute-start | bytes 786440 | tf_op jit(solution)/shard_map/ppermute | solution.py:166
  110.8 0.5 collective-permute-done.7.other
  111.3 0.0 copy-done
  111.3 0.0 copy-done.1
  111.3 4.3 %shard_map.87 = (f32[512,512]{1,0:T(8,128)}, bf16[512,512]{1,0:T(8,128)(2,1)}, bf16[512,512]{1,0:T(8,128)(2,1)S(1)}, f32[8,128]{1,0:T(8,128)S(1)}) custom-call(s32[1,1]{1,0:T(1,128)S(6)} %copy.11.count, bf16[256,512]{1,0:T(8,128)(2,1)S(1)} %collective-permute-done.6.own, bf16[256,512]{1,0:T(8,128)(2,1)S(1)} %collective-permute-done.7.other, ...), custom_call_target="tpu_custom_call" | custom-call | tf_op jit(solution)/shard_map/pallas_call | solution.py:122
  115.6 1.9 %collective-permute-start.8 = (bf16[512,512]{1,0:T(8,128)(2,1)S(1)}, bf16[512,512]{1,0:T(8,128)(2,1)S(1)}, u32[]{:S(2)}, u32[]{:S(2)}) collective-permute-start(bf16[512,512]{1,0:T(8,128)(2,1)S(1)} %get-tuple-element.19.own), channel_id=1, source_target_pairs={{0,32},{32,0},{1,33},{33,1},{2,34},{34,2},{3,35},{35,3},{4,36},{36... | collective-permute-start | bytes 1572872 | tf_op jit(solution)/shard_map/ppermute | solution.py:166
  117.5 1.9 %collective-permute-done.8.other = bf16[512,512]{1,0:T(8,128)(2,1)S(1)} collective-permute-done((bf16[512,512]{1,0:T(8,128)(2,1)S(1)}, bf16[512,512]{1,0:T(8,128)(2,1)S(1)}, u32[]{:S(2)}, u32[]{:S(2)}) %collective-permute-start.8) | collective-permute-done | bytes 524320 | tf_op jit(solution)/shard_map/ppermute | solution.py:166
  119.4 1.3 %shard_map.88 = bf16[256,512]{1,0:T(8,128)(2,1)} custom-call(bf16[512,512]{1,0:T(8,128)(2,1)S(1)} %get-tuple-element.19.own, bf16[512,512]{1,0:T(8,128)(2,1)S(1)} %collective-permute-done.8.other, f32[8,128]{1,0:T(8,128)S(1)} %get-tuple-element.20.grad_square), custom_call_target="tpu_custom_call" | custom-call | tf_op jit(solution)/shard_map/pallas_call | solution.py:156
  (5 shorter events, 0.1 us)
Async XLA Ops:
  0.6 6.3 %collective-permute-start.1 = (bf16[512,512]{1,0:T(8,128)(2,1)}, bf16[512,512]{1,0:T(8,128)(2,1)S(1)}, u32[]{:S(2)}, u32[]{:S(2)}) collective-permute-start(bf16[512,512]{1,0:T(8,128)(2,1)} %param.6), channel_id=1, source_target_pairs={{0,32},{32,0},{1,33},{33,1},{2,34},{34,2},{3,35},{35,3},{4,36},{36... | collective-permute-start | bytes 1572872 | tf_op jit(solution)/shard_map/ppermute | solution.py:166
  5.0 3.1 %collective-permute-start = (bf16[64,512]{1,0:T(8,128)(2,1)S(1)}, bf16[64,512]{1,0:T(8,128)(2,1)S(1)}, u32[]{:S(2)}, u32[]{:S(2)}) collective-permute-start(bf16[64,512]{1,0:T(8,128)(2,1)S(1)} %get-tuple-element.24), channel_id=1, source_target_pairs={{0,32},{32,0},{1,33},{33,1},{2,34},{34,2},{3,35},{35,3},{4,36},{36... | collective-permute-start | bytes 196616 | tf_op jit(solution)/shard_map/ppermute | solution.py:166
  8.1 43.1 %collective-permute-start.5 = (bf16[1024,512]{1,0:T(8,128)(2,1)S(1)}, bf16[1024,512]{1,0:T(8,128)(2,1)S(1)}, u32[]{:S(2)}, u32[]{:S(2)}) collective-permute-start(bf16[1024,512]{1,0:T(8,128)(2,1)S(1)} %pad_maximum_fusion.refs_1_.refs_3_), channel_id=1, source_target_pairs={{0,16},{16,0},{1,17},{17,1},{2,18},{18,2},{3,19},{19,3},{4,20},{20... | collective-permute-start | bytes 3145736 | tf_op jit(solution)/shard_map/ppermute | solution.py:166
  42.4 22.2 %collective-permute-start.2 = (bf16[256,1024]{1,0:T(8,128)(2,1)S(1)}, bf16[256,1024]{1,0:T(8,128)(2,1)S(1)}, u32[]{:S(2)}, u32[]{:S(2)}) collective-permute-start(bf16[256,1024]{1,0:T(8,128)(2,1)S(1)} %all_gather.3.refs_0_), channel_id=1, source_target_pairs={{0,14},{1,15},{2,0},{3,1},{4,2},{5,3},{6,4},{7,5},{8,6},{9,7},{10,... | collective-permute-start | bytes 1572872 | tf_op jit(solution)/shard_map/ppermute | solution.py:178
  45.5 19.1 %collective-permute-start.3 = (bf16[256,1024]{1,0:T(8,128)(2,1)S(1)}, bf16[256,1024]{1,0:T(8,128)(2,1)}, u32[]{:S(2)}, u32[]{:S(2)}) collective-permute-start(bf16[256,1024]{1,0:T(8,128)(2,1)S(1)} %all_gather.3.refs_0_), channel_id=1, source_target_pairs={{0,15},{1,0},{2,1},{3,2},{4,3},{5,4},{6,5},{7,6},{8,7},{9,8},{10,9... | collective-permute-start | bytes 1572872 | tf_op jit(solution)/shard_map/ppermute | solution.py:171
  49.3 21.7 %collective-permute-start.4 = (bf16[256,1024]{1,0:T(8,128)(2,1)S(1)}, bf16[256,1024]{1,0:T(8,128)(2,1)}, u32[]{:S(2)}, u32[]{:S(2)}) collective-permute-start(bf16[256,1024]{1,0:T(8,128)(2,1)S(1)} %all_gather.3.refs_0_), channel_id=1, source_target_pairs={{0,1},{1,2},{2,3},{3,4},{4,5},{5,6},{6,7},{7,8},{8,9},{9,10},{10,1... | collective-permute-start | bytes 1572872 | tf_op jit(solution)/shard_map/ppermute | solution.py:171
  96.3 15.0 %copy-start = (f32[512,512]{1,0:T(8,128)S(1)}, f32[512,512]{1,0:T(8,128)}, u32[]{:S(2)}) copy-start(f32[512,512]{1,0:T(8,128)} %state.1) | copy-start | bytes 3145732
  96.3 15.0 %copy-start.1 = (bf16[512,512]{1,0:T(8,128)(2,1)S(1)}, bf16[512,512]{1,0:T(8,128)(2,1)}, u32[]{:S(2)}) copy-start(bf16[512,512]{1,0:T(8,128)(2,1)} %stale.1) | copy-start | bytes 1572868
  96.6 7.2 %collective-permute-start.6 = (bf16[256,512]{1,0:T(8,128)(2,1)S(1)}, bf16[256,512]{1,0:T(8,128)(2,1)S(1)}, u32[]{:S(2)}, u32[]{:S(2)}) collective-permute-start(bf16[256,512]{1,0:T(8,128)(2,1)S(1)} %pad_maximum_fusion.1), channel_id=1, source_target_pairs={{0,0},{16,256},{256,16},{272,272},{1,1},{17,257},{257,17},{273,273... | collective-permute-start | bytes 786440 | tf_op jit(solution)/shard_map/ppermute | solution.py:183
  103.8 7.5 %collective-permute-start.7 = (bf16[256,512]{1,0:T(8,128)(2,1)S(1)}, bf16[256,512]{1,0:T(8,128)(2,1)S(1)}, u32[]{:S(2)}, u32[]{:S(2)}) collective-permute-start(bf16[256,512]{1,0:T(8,128)(2,1)S(1)} %collective-permute-done.6.own), channel_id=1, source_target_pairs={{0,32},{32,0},{1,33},{33,1},{2,34},{34,2},{3,35},{35,3},{4,36},{36... | collective-permute-start | bytes 786440 | tf_op jit(solution)/shard_map/ppermute | solution.py:166
  115.6 3.8 %collective-permute-start.8 = (bf16[512,512]{1,0:T(8,128)(2,1)S(1)}, bf16[512,512]{1,0:T(8,128)(2,1)S(1)}, u32[]{:S(2)}, u32[]{:S(2)}) collective-permute-start(bf16[512,512]{1,0:T(8,128)(2,1)S(1)} %get-tuple-element.19.own), channel_id=1, source_target_pairs={{0,32},{32,0},{1,33},{33,1},{2,34},{34,2},{3,35},{35,3},{4,36},{36... | collective-permute-start | bytes 1572872 | tf_op jit(solution)/shard_map/ppermute | solution.py:166
